TPU v7x, 512 devices: a whole 4x8x8 slice. The times are simulated.
512 devices in a mesh: dp: 4 (over y_hi), expert: 32 (over z, y_lo, core), context: 4 (over x).
Axes of the slice: x: 4, y: 8 (y_hi: 4, y_lo: 2; y = y_hi * 2 + y_lo), z: 8, core: 2. Of those that a mesh axis runs over, the one named last changes fastest.
Arguments:
- grad_out: bfloat16 [65536, 4096], P(('dp', 'expert', 'context')), may hold values from -6 to 6
- routes: int32 [65536, 8], P(('dp', 'expert', 'context')), may hold values from 0 to 127, all different within a row; in each aligned block of 128 rows (0 to 127, 128 to 255, ...) at most 16 rows name the same one
- route_weight: bfloat16 [65536, 8], P(('dp', 'expert', 'context')), may hold values from 0.099609375 to 1
- saved_gate: bfloat16 [4, 32, 4, 32, 16, 768], P('dp', 'expert', 'context'), may hold values from -6 to 6
- saved_up: bfloat16 [4, 32, 4, 32, 16, 768], P('dp', 'expert', 'context'), may hold values from -6 to 6
- down_weight: bfloat16 [32, 768, 4096], P('expert', None, ('dp', 'context')), may hold values from -0.21875 to 0.21875
Outputs:
- grad_gate: bfloat16 [4, 32, 4, 32, 16, 768], P('dp', 'expert', 'context')
- grad_up: bfloat16 [4, 32, 4, 32, 16, 768], P('dp', 'expert', 'context')
- grad_weight: float32 [65536, 8], P(('dp', 'expert', 'context'))
Inputs may be any that keep to these rules, and one draw needn't show every extreme that they name: `routes`: each row names 8 different experts; among the rows of one device no expert is named by more than 16 rows.
All inputs are finite; a program needn't handle non-finite values.
Results may differ from a plain program's by a relative error of at most 0.003.
Values may be sent and summed in bfloat16 or wider, within the bound.
No kernel may reach another device: no remote copies, remote signals or barrier semaphores. Data moves between devices by JAX's collectives and lax.ppermute only.
A program may use at most 64 MiB of HBM per device.

v0:
```python
import jax
import jax.numpy as jnp
from jax import lax
from jax.sharding import PartitionSpec as P

EXPERTS = 128


def slot_positions(routes_dev, ranks, cap, per_rank):
    flat = routes_dev.reshape(-1)
    served = jnp.arange(ranks, dtype=jnp.int32) * per_rank
    hits = (flat[:, None] == served[None, :]).astype(jnp.int32)
    before = jnp.cumsum(hits, axis=0) - hits
    target = before + (jnp.arange(ranks, dtype=jnp.int32) * cap)[None, :]
    live = jnp.sum(hits, axis=1) > 0
    return jnp.where(live, jnp.sum(hits * target, axis=1), -1)


def expert_math(back, slot_weight, gate, up):
    gate_f = gate.astype(jnp.float32)
    up_f = up.astype(jnp.float32)
    sigma = jax.nn.sigmoid(gate_f)
    hidden = (gate_f * sigma * up_f).astype(jnp.bfloat16)
    hidden = lax.optimization_barrier(hidden)
    slot_grad = jnp.sum(hidden.astype(jnp.float32) * back, axis=-1)
    grad_hidden = slot_weight.astype(jnp.float32)[..., None] * back
    grad_gate = (grad_hidden * up_f * sigma * (1.0 + gate_f * (1.0 - sigma))).astype(jnp.bfloat16)
    grad_up = (grad_hidden * gate_f * sigma).astype(jnp.bfloat16)
    return (grad_gate, grad_up, slot_grad)


def body(grad_out, routes, route_weight, saved_gate, saved_up, down_weight):
    ranks = lax.axis_size("expert")
    cap = saved_gate.shape[4]
    hidden_units = saved_gate.shape[5]
    tok_rows = grad_out.shape[0]
    width = grad_out.shape[1]
    topk_count = routes.shape[1]
    slots = ranks * cap
    position = slot_positions(routes, ranks, cap, EXPERTS // ranks)
    onehot = position[:, None] == jnp.arange(slots, dtype=jnp.int32)[None, :]
    choose = onehot.reshape(tok_rows, topk_count, slots).any(axis=1).astype(jnp.bfloat16)
    outgoing = lax.dot_general(
        choose, grad_out, (((0,), (0,)), ((), ())), preferred_element_type=jnp.float32
    )
    outgoing = outgoing.astype(jnp.bfloat16).reshape(ranks, cap, width)
    slot_weight = jnp.sum(
        jnp.where(onehot, route_weight.reshape(-1)[:, None].astype(jnp.float32), 0.0), axis=0
    )
    slot_weight = slot_weight.astype(jnp.bfloat16).reshape(ranks, cap)
    local_weight = down_weight[0]
    received, received_weight = (
        lax.all_to_all(outgoing, "expert", split_axis=0, concat_axis=0, tiled=True),
        lax.all_to_all(slot_weight, "expert", split_axis=0, concat_axis=0, tiled=True),
    )
    received_rows = received.reshape(slots, width)
    back = lax.dot_general(
        received_rows,
        lax.all_gather(local_weight, ("dp", "context"), axis=1, tiled=True),
        (((1,), (1,)), ((), ())),
        preferred_element_type=jnp.float32,
    )
    back = back.reshape(ranks, cap, hidden_units)
    grad_gate, grad_up, slot_grad = expert_math(
        back, received_weight, saved_gate[0, 0, 0], saved_up[0, 0, 0]
    )
    returned = lax.all_to_all(slot_grad, "expert", split_axis=0, concat_axis=0, tiled=True)
    grad_weight = jnp.sum(jnp.where(onehot, returned.reshape(-1)[None, :], 0.0), axis=-1)
    grad_weight = grad_weight.reshape(tok_rows, topk_count)
    return (grad_gate[None, None, None], grad_up[None, None, None], grad_weight)


def solution(mesh):
    placed = (
        P(("dp", "expert", "context"), None),
        P(("dp", "expert", "context"), None),
        P(("dp", "expert", "context"), None),
        P("dp", "expert", "context", None, None, None),
        P("dp", "expert", "context", None, None, None),
        P("expert", None, ("dp", "context")),
    )
    return jax.shard_map(
        body,
        mesh=mesh,
        in_specs=placed,
        out_specs=(
            P("dp", "expert", "context", None, None, None),
            P("dp", "expert", "context", None, None, None),
            P(("dp", "expert", "context"), None),
        ),
        check_vma=False,
    )
```

profile of v0, /device:TPU:1, one launch (start us, length us, event | category | flops | bytes accessed | tf_op | source)
XLA Modules:
  0.0 209.8 jit_solution(7847362634378324971)
XLA Ops:
  7.2 0.0 copy-start
  7.2 0.0 all-gather.3.cloned.1.call-start
  7.2 0.7 all-gather.3.cloned.1.call-update
  7.9 0.8 copy.22
  8.7 0.1 eq.49
  8.8 0.1 eq.45
  8.9 0.1 compare_convert_fusion
  9.0 9.0 %reduce-window.6 = s32[32,8,128]{2,1,0:T(8,128)S(1)} reduce-window(s32[32,8,128]{2,1,0:T(8,128)S(1)} %compare_convert_fusion, s32[]{:T(128)} %constant.8.clone.1), window={size=1x1x128 pad=0_0x0_0x127_0}, to_apply=%region_1.2 | reduce-window | flops 4161536 | bytes 262148 | tf_op jit(solution)/shard_map/reduce-window
  18.0 0.1 slice.8
  18.1 0.1 copy.24
  18.3 0.1 copy.25
  18.4 0.1 broadcast_add_fusion
  18.5 0.1 convert_reduce_fusion
  18.6 0.1 select_n.22
  18.7 0.7 fusion.2
  19.4 0.0 copy-done
  19.4 3.4 %convolution_convert_fusion = bf16[512,4096]{1,0:T(8,128)(2,1)} fusion(pred[128,512]{1,0:T(8,128)(4,1)S(1)} %fusion.2, bf16[128,4096]{1,0:T(8,128)(2,1)S(1)} %copy-done), kind=kOutput, calls=%fused_computation.2 | convolution fusion | flops 538968064 | bytes 5308416 | tf_op jit(solution)/shard_map/dot_general | solution.py:43
  22.8 0.0 copy-start.1
  22.8 0.0 copy-start.2
  22.8 13.2 %all-to-all-start.1 = ((bf16[32,16,4096]{2,1,0:T(8,128)(2,1)}), bf16[32,16,4096]{2,1,0:T(8,128)(2,1)}, u32[]{:S(2)}, u32[]{:S(2)}) async-start(bf16[32,16,4096]{2,1,0:T(8,128)(2,1)} %bitcast.41), calls=%async_computation.1 | async-start | bytes 8388608 | tf_op jit(solution)/shard_map/all_to_all | solution.py:53
  36.0 0.0 copy-done.1
  36.0 0.0 copy-done.2
  36.0 0.5 fusion.6
  36.5 0.0 copy-start.3
  36.5 107.5 %all-to-all-done.1 = bf16[32,16,4096]{2,1,0:T(8,128)(2,1)} async-done(((bf16[32,16,4096]{2,1,0:T(8,128)(2,1)}), bf16[32,16,4096]{2,1,0:T(8,128)(2,1)}, u32[]{:S(2)}, u32[]{:S(2)}) %all-to-all-start.1) | async-done | bytes 4194336 | tf_op jit(solution)/shard_map/all_to_all | solution.py:53
  144.0 13.9 %all-gather.3.cloned.1.call-done = bf16[1,768,4096]{2,1,0:T(8,128)(2,1)} async-done(((bf16[1,768,256]{2,1,0:T(8,128)(2,1)}), bf16[1,768,4096]{2,1,0:T(8,128)(2,1)}) %all-gather.3.cloned.1.call-update) | async-done | bytes 6291472 | tf_op jit(solution)/shard_map/all_gather | solution.py:59
  157.9 9.3 %multiply_reduce_fusion = (f32[32,16]{1,0:T(8,128)}, f32[32,16,768]{2,1,0:T(8,128)}) fusion(bf16[32,16,768]{2,1,0:T(8,128)(2,1)S(1)} %fusion.6, bf16[32,16,4096]{2,1,0:T(8,128)(2,1)} %all-to-all-done.1, bf16[1,768,4096]{2,1,0:T(8,128)(2,1)} %all-gather.3.cloned.1.call-done), kind=kOutput, calls=%fused_computation.24 | convolution fusion | flops 3222404608 | bytes 12847104 | tf_op jit(solution)/shard_map/dot_general | solution.py:57
  167.2 10.0 %all-to-all-start.2 = ((f32[32,1,16]{2,1,0:T(1,128)}), f32[32,1,16]{2,1,0:T(1,128)S(1)}, u32[]{:S(2)}, u32[]{:S(2)}) async-start(f32[32,1,16]{2,1,0:T(1,128)} %bitcast.12), calls=%async_computation.2 | async-start | bytes 32768 | tf_op jit(solution)/shard_map/all_to_all | solution.py:67
  177.2 0.0 copy-done.3
  177.2 0.1 copy.26
  177.3 0.1 reshape.106
  177.4 7.5 %all-to-all-done.2 = f32[32,1,16]{2,1,0:T(1,128)S(1)} async-done(((f32[32,1,16]{2,1,0:T(1,128)}), f32[32,1,16]{2,1,0:T(1,128)S(1)}, u32[]{:S(2)}, u32[]{:S(2)}) %all-to-all-start.2) | async-done | bytes 2080 | tf_op jit(solution)/shard_map/all_to_all | solution.py:67
  184.9 0.5 broadcast.60
  185.4 0.7 reduce.3
  186.1 0.1 broadcast_in_dim.44
  186.2 0.7 select_reduce_fusion
  186.9 0.7 convert_element_type.91
  187.6 4.1 %all-to-all-start = ((bf16[32,1,16]{2,1,0:T(2,128)(2,1)}), bf16[32,1,16]{2,1,0:T(2,128)(2,1)S(1)}, u32[]{:S(2)}, u32[]{:S(2)}) async-start(bf16[32,1,16]{2,1,0:T(2,128)(2,1)} %convert_element_type.91), calls=%async_computation | async-start | bytes 32768 | tf_op jit(solution)/shard_map/all_to_all | solution.py:54
  191.7 0.1 reshape.105
  191.8 0.7 copy.28
  192.5 7.1 %all-to-all-done = bf16[32,1,16]{2,1,0:T(2,128)(2,1)S(1)} async-done(((bf16[32,1,16]{2,1,0:T(2,128)(2,1)}), bf16[32,1,16]{2,1,0:T(2,128)(2,1)S(1)}, u32[]{:S(2)}, u32[]{:S(2)}) %all-to-all-start) | async-done | bytes 1056 | tf_op jit(solution)/shard_map/all_to_all | solution.py:54
  199.6 3.4 %fusion.13 = (bf16[1,1,1,32,16,768]{5,4,3,2,1,0:T(8,128)(2,1)}, bf16[1,1,1,32,16,768]{5,4,3,2,1,0:T(8,128)(2,1)}) fusion(bf16[1,1,1,32,16,768]{5,4,3,2,1,0:T(8,128)(2,1)S(1)} %copy-done.1, f32[32,16,768]{2,1,0:T(8,128)} %get-tuple-element.19, f32[32,16]{1,0:T(8,128)S(1)} %bitcast.43, bf16[1,1,1,32,16,768]{5,4,3,2,1,0:T(8,128)(2,1)S(1)} %copy-done.2), kind=kLoop, calls=%fused_computation.25 | loop fusion | flops 6291456 | bytes 4720640 | tf_op jit(solution)/shard_map/broadcast_in_dim | solution.py:70
  (5 shorter events, 0.1 us)
Async XLA Ops:
  7.2 12.2 %copy-start = (bf16[128,4096]{1,0:T(8,128)(2,1)S(1)}, bf16[128,4096]{1,0:T(8,128)(2,1)}, u32[]{:S(2)}) copy-start(bf16[128,4096]{1,0:T(8,128)(2,1)} %param.6) | copy-start | bytes 3145732
  7.2 150.7 %all-gather.3.cloned.1.call-start = ((), (), s32[]{:S(2)}) async-start(), calls=%async_computation.3 | async-start | bytes 6684672 | tf_op jit(solution)/shard_map/all_gather | solution.py:59
  22.8 13.2 %copy-start.1 = (bf16[1,1,1,32,16,768]{5,4,3,2,1,0:T(8,128)(2,1)S(1)}, bf16[1,1,1,32,16,768]{5,4,3,2,1,0:T(8,128)(2,1)}, u32[]{:S(2)}) copy-start(bf16[1,1,1,32,16,768]{5,4,3,2,1,0:T(8,128)(2,1)} %param.9) | copy-start | bytes 2359300
  22.8 13.2 %copy-start.2 = (bf16[1,1,1,32,16,768]{5,4,3,2,1,0:T(8,128)(2,1)S(1)}, bf16[1,1,1,32,16,768]{5,4,3,2,1,0:T(8,128)(2,1)}, u32[]{:S(2)}) copy-start(bf16[1,1,1,32,16,768]{5,4,3,2,1,0:T(8,128)(2,1)} %param.10) | copy-start | bytes 2359300
  22.8 121.2 %all-to-all-start.1 = ((bf16[32,16,4096]{2,1,0:T(8,128)(2,1)}), bf16[32,16,4096]{2,1,0:T(8,128)(2,1)}, u32[]{:S(2)}, u32[]{:S(2)}) async-start(bf16[32,16,4096]{2,1,0:T(8,128)(2,1)} %bitcast.41), calls=%async_computation.1 | async-start | bytes 8388608 | tf_op jit(solution)/shard_map/all_to_all | solution.py:53
  36.5 140.6 %copy-start.3 = (bf16[128,8]{0,1:T(8,128)(2,1)S(1)}, bf16[128,8]{0,1:T(8,128)(2,1)}, u32[]{:S(2)}) copy-start(bf16[128,8]{0,1:T(8,128)(2,1)} %param.8) | copy-start | bytes 6148
  167.2 17.7 %all-to-all-start.2 = ((f32[32,1,16]{2,1,0:T(1,128)}), f32[32,1,16]{2,1,0:T(1,128)S(1)}, u32[]{:S(2)}, u32[]{:S(2)}) async-start(f32[32,1,16]{2,1,0:T(1,128)} %bitcast.12), calls=%async_computation.2 | async-start | bytes 32768 | tf_op jit(solution)/shard_map/all_to_all | solution.py:67
  187.6 12.0 %all-to-all-start = ((bf16[32,1,16]{2,1,0:T(2,128)(2,1)}), bf16[32,1,16]{2,1,0:T(2,128)(2,1)S(1)}, u32[]{:S(2)}, u32[]{:S(2)}) async-start(bf16[32,1,16]{2,1,0:T(2,128)(2,1)} %convert_element_type.91), calls=%async_computation | async-start | bytes 32768 | tf_op jit(solution)/shard_map/all_to_all | solution.py:54
Sparse Core Ops, SparseCore 0:
  11.0 146.8 all-gather.2
where the time goes:
time: 211 us; the launch traced here: 210 us
  waiting for transfers between devices  137 us (65%)
  starting transfers between devices  27.4 us (13%)
  other arithmetic  15.4 us (7%)
  between operations  14.2 us (7%)
  matrix products  12.7 us (6%)
  local copies, waits for them, and re-layouts  3.6 us (2%)
    all_to_all x1, waiting for transfers between devices, body(): lax.all_to_all(outgoing, 'expert', split_axis=0, concat_axis=0, tiled=True)  107 us
    all_gather x1, waiting for transfers between devices, body(): lax.all_gather(local_weight, ('dp', 'context'), axis=1, tiled=True)  13.9 us
    all_to_all x1, starting transfers between devices, body(): lax.all_to_all(outgoing, 'expert', split_axis=0, concat_axis=0, tiled=True)  13.2 us
    all_to_all x1, starting transfers between devices, body(): lax.all_to_all(slot_grad, 'expert', split_axis=0, concat_axis=0, tiled=True)  10 us
    dot_general x1, matrix products, body(): lax.dot_general(received_rows, lax.all_gather(local_weight, ('dp', 'conte...  9.27 us
    another operation x3, other arithmetic  9.15 us
    all_to_all x1, waiting for transfers between devices, body(): lax.all_to_all(slot_grad, 'expert', split_axis=0, concat_axis=0, tiled=True)  7.53 us
    all_to_all x1, waiting for transfers between devices, body(): lax.all_to_all(slot_weight, 'expert', split_axis=0, concat_axis=0, tiled=...  7.09 us
  transfers between devices with their start and end apart: 4, of which 4 were waited for; matrix products, arithmetic and copies ran while one was open for 8% of the time, Pallas kernels for 0%

commit v1 on v0

v1 whole, which is shorter than its diff:
```python
import jax
import jax.numpy as jnp
from jax import lax
from jax.experimental import pallas as pl
from jax.experimental.pallas import tpu as pltpu
from jax.sharding import PartitionSpec as P

EXPERTS = 128


def head_kernel(ranks, cap, n_dp, n_context, routes_ref, weight_ref, grad_ref, sent_ref, slot_weight_ref, slot_ref):
    topk, tokens = routes_ref.shape
    slots = ranks * cap
    step = EXPERTS // ranks
    served = lax.broadcasted_iota(jnp.int32, (ranks, tokens), 0) * step
    hits = jnp.zeros((ranks, tokens), jnp.float32)
    picked = jnp.zeros((ranks, tokens), jnp.float32)
    for k in range(topk):
        hit = routes_ref[k : k + 1, :] == served
        hits = hits + jnp.where(hit, 1.0, 0.0)
        picked = picked + jnp.where(hit, weight_ref[k : k + 1, :].astype(jnp.float32), 0.0)
    earlier = lax.broadcasted_iota(jnp.int32, (tokens, tokens), 0) < lax.broadcasted_iota(
        jnp.int32, (tokens, tokens), 1
    )
    earlier = jnp.where(earlier, 1.0, 0.0).astype(jnp.bfloat16)
    before = jnp.dot(hits.astype(jnp.bfloat16), earlier, preferred_element_type=jnp.float32)
    slot = jnp.where(hits > 0.0, before, -1.0)
    slot_ref[...] = slot
    lane = lax.broadcasted_iota(jnp.int32, (ranks, cap), 1).astype(jnp.float32)
    found = jnp.zeros((ranks, cap), jnp.float32)
    for j in range(cap):
        one = jnp.sum(jnp.where(slot == float(j), picked, 0.0), axis=1, keepdims=True)
        found = jnp.where(lane == float(j), one, found)
    slot_weight_ref[...] = found.astype(jnp.bfloat16)
    wide = jnp.broadcast_to(slot[:, None, :], (ranks, cap, tokens))
    place = lax.broadcasted_iota(jnp.int32, (ranks, cap, tokens), 1).astype(jnp.float32)
    choose = jnp.where(wide == place, 1.0, 0.0).reshape(slots, tokens).astype(jnp.bfloat16)
    a = lax.axis_index("dp")
    c = lax.axis_index("context")
    cols = grad_ref.shape[1] // (n_dp * n_context)
    for j in range(n_context):
        for i in range(n_dp):
            block = lax.rem(a + i, n_dp) * n_context + lax.rem(c + j, n_context)
            part = grad_ref[:, pl.ds(pl.multiple_of(block * cols, cols), cols)]
            out = jnp.dot(choose, part, preferred_element_type=jnp.float32).astype(jnp.bfloat16)
            at = (j * n_dp + i) * cols
            sent_ref[:, at : at + cols] = out


def head(routes, route_weight, grad_out, ranks, cap, n_dp, n_context):
    tokens, width = grad_out.shape

    def kernel(*refs):
        head_kernel(ranks, cap, n_dp, n_context, *refs)

    return pl.pallas_call(
        kernel,
        out_shape=(
            jax.ShapeDtypeStruct((ranks * cap, width), jnp.bfloat16),
            jax.ShapeDtypeStruct((ranks, cap), jnp.bfloat16),
            jax.ShapeDtypeStruct((ranks, tokens), jnp.float32),
        ),
        compiler_params=pltpu.CompilerParams(vmem_limit_bytes=32 * 2**20),
        name="head",
    )(routes.T, route_weight.T, grad_out)


def project_kernel(cap, received_ref, hidden_ref, *refs):
    *weights, back_ref, slot_grad_ref = refs
    rows, units = hidden_ref.shape
    total = jnp.zeros((rows, units), jnp.float32)
    at = 0
    for weight_ref in weights:
        for i in range(weight_ref.shape[0]):
            cols = weight_ref.shape[2]
            total = total + lax.dot_general(
                received_ref[:, at : at + cols],
                weight_ref[i],
                (((1,), (1,)), ((), ())),
                preferred_element_type=jnp.float32,
            )
            at += cols
    back_ref[...] = total
    grads = hidden_ref[...].astype(jnp.float32) * total
    slot_grad_ref[...] = jnp.sum(grads.reshape(rows // cap, cap, units), axis=2)


def project(received, hidden, weights, cap):
    rows, units = hidden.shape

    def kernel(*refs):
        project_kernel(cap, *refs)

    return pl.pallas_call(
        kernel,
        out_shape=(
            jax.ShapeDtypeStruct((rows, units), jnp.float32),
            jax.ShapeDtypeStruct((rows // cap, cap), jnp.float32),
        ),
        compiler_params=pltpu.CompilerParams(vmem_limit_bytes=32 * 2**20),
        name="project",
    )(received, hidden, *weights)


def tail_kernel(routes_ref, slot_ref, returned_ref, out_ref):
    ranks, cap = returned_ref.shape
    topk, tokens = routes_ref.shape
    slot = slot_ref[...]
    grads = jnp.zeros((ranks, tokens), jnp.float32)
    for j in range(cap):
        grads = grads + jnp.where(slot == float(j), returned_ref[:, j : j + 1], 0.0)
    served = lax.broadcasted_iota(jnp.int32, (ranks, tokens), 0) * (EXPERTS // ranks)
    for k in range(topk):
        hit = routes_ref[k : k + 1, :] == served
        out_ref[k : k + 1, :] = jnp.sum(jnp.where(hit, grads, 0.0), axis=0, keepdims=True)


def tail(routes, slot, returned):
    return pl.pallas_call(
        tail_kernel,
        out_shape=jax.ShapeDtypeStruct((routes.shape[1], routes.shape[0]), jnp.float32),
        compiler_params=pltpu.CompilerParams(vmem_limit_bytes=8 * 2**20),
        name="tail",
    )(routes.T, slot, returned).T


def ring_gather(block, axis):
    size = lax.axis_size(axis)
    up = [(i, (i + 1) % size) for i in range(size)]
    down = [(i, (i - 1) % size) for i in range(size)]
    half = block.shape[0] // 2
    before = lax.ppermute(block, axis, up)
    after = lax.ppermute(block, axis, down)
    far_low = lax.ppermute(before[:half], axis, up)
    far_high = lax.ppermute(after[half:], axis, down)
    return after, far_low, far_high, before


def body(grad_out, routes, route_weight, saved_gate, saved_up, down_weight):
    ranks = lax.axis_size("expert")
    n_dp, n_context = lax.axis_size("dp"), lax.axis_size("context")
    cap, units = saved_gate.shape[4:]
    slots = ranks * cap
    width = grad_out.shape[1]

    own = down_weight[0]
    after, far_low, far_high, before = ring_gather(own, "dp")
    over_dp = jnp.concatenate([own, after, far_low, far_high, before], axis=0)
    over_dp = over_dp.reshape(n_dp, units, own.shape[1])
    after, far_low, far_high, before = ring_gather(over_dp, "context")
    weights = (over_dp, after, far_low, far_high, before)

    sent, slot_weight, slot = head(routes, route_weight, grad_out, ranks, cap, n_dp, n_context)
    received = lax.all_to_all(
        sent.reshape(ranks, cap, width), "expert", split_axis=0, concat_axis=0, tiled=True
    ).reshape(slots, width)
    slot_weight = lax.all_to_all(slot_weight, "expert", split_axis=0, concat_axis=0, tiled=True)

    gate = saved_gate.reshape(slots, units).astype(jnp.float32)
    up = saved_up.reshape(slots, units).astype(jnp.float32)
    sigma = jax.nn.sigmoid(gate)
    hidden = lax.optimization_barrier((gate * sigma * up).astype(jnp.bfloat16))
    back, slot_grad = project(received, hidden, weights, cap)
    returned = lax.all_to_all(slot_grad, "expert", split_axis=0, concat_axis=0, tiled=True)
    grad_weight = tail(routes, slot, returned)

    grad_hidden = slot_weight.reshape(slots, 1).astype(jnp.float32) * back
    grad_gate = (grad_hidden * up * sigma * (1.0 + gate * (1.0 - sigma))).astype(jnp.bfloat16)
    grad_up = (grad_hidden * gate * sigma).astype(jnp.bfloat16)
    return grad_gate.reshape(saved_gate.shape), grad_up.reshape(saved_up.shape), grad_weight


def solution(mesh):
    tokens = P(("dp", "expert", "context"), None)
    saved = P("dp", "expert", "context", None, None, None)
    return jax.shard_map(
        body,
        mesh=mesh,
        in_specs=(tokens, tokens, tokens, saved, saved, P("expert", None, ("dp", "context"))),
        out_specs=(saved, saved, tokens),
        check_vma=False,
    )
```

time: 211 us -> 232 us (1.100)
  blocking collectives: 0 us -> 20.6 us
  starting transfers between devices: 27.4 us -> 44 us
  between operations: 14.2 us -> 0.87 us
  matrix products: 12.7 us -> 0 us
  other arithmetic: 15.4 us -> 5.34 us
  Pallas kernels: 0 us -> 8.93 us
  local copies, waits for them, and re-layouts: 3.6 us -> 10.4 us
  waiting for transfers between devices: 137 us -> 141 us
    ppermute x0 -> x8, waiting for transfers between devices: none -> 137 us  [the longest x2 117 us: ring_gather(): before = lax.ppermute(block, axis, up)]
    all_to_all x2 -> x1, waiting for transfers between devices: 115 us -> 0.01 us  [body(): lax.all_to_all(sent.reshape(ranks, cap, width), 'expert', split_axis=0, c...]
    ppermute x0 -> x8, starting transfers between devices: none -> 28 us  [the longest x2 10 us: ring_gather(): far_high = lax.ppermute(after[half:], axis, down)]
    all_to_all x0 -> x1, blocking collectives: none -> 20.6 us  [body(): lax.all_to_all(slot_weight, 'expert', split_axis=0, concat_axis=0, tiled=...]
    all_gather x1 -> x0, waiting for transfers between devices: 13.9 us -> none  [body(): lax.all_gather(local_weight, ('dp', 'context'), axis=1, tiled=True)]
    dot_general x2 -> x0, matrix products: 12.7 us -> none  [the longest x1 9.27 us: body(): lax.dot_general(received_rows, lax.all_gather(local_weight, ('dp', 'conte...]
    all_to_all x2 -> x1, starting transfers between devices: 17.3 us -> 5.22 us  [body(): lax.all_to_all(sent.reshape(ranks, cap, width), 'expert', split_axis=0, c...]
    another operation x3 -> x0, other arithmetic: 9.15 us -> none
  transfers between devices with their start and end apart: 4 -> 10, of which waited for: 4 -> 7; matrix products, arithmetic and copies ran while one was open for 8% -> 3% of each run, Pallas kernels for 0% -> 0%
where the time goes in v1:
time: 232 us; the launch traced here: 231 us
  waiting for transfers between devices  141 us (61%)
  starting transfers between devices  44 us (19%)
  blocking collectives  20.6 us (9%)
  local copies, waits for them, and re-layouts  10.4 us (4%)
  Pallas kernels  8.93 us (4%)
  other arithmetic  5.34 us (2%)
    ppermute x2, waiting for transfers between devices, ring_gather(): before = lax.ppermute(block, axis, up)  117 us
    all_to_all x1, blocking collectives, body(): lax.all_to_all(slot_weight, 'expert', split_axis=0, concat_axis=0, tiled=...  20.6 us
    ppermute x2, waiting for transfers between devices, ring_gather(): far_low = lax.ppermute(before[:half], axis, up)  14.3 us
    all_to_all x1, starting transfers between devices, body(): lax.all_to_all(slot_grad, 'expert', split_axis=0, concat_axis=0, tiled=True)  10.7 us
    ppermute x2, starting transfers between devices, ring_gather(): far_high = lax.ppermute(after[half:], axis, down)  10 us
    unnamed x28, local copies, waits for them, and re-layouts  8.38 us
    ppermute x2, starting transfers between devices, ring_gather(): before = lax.ppermute(block, axis, up)  7.52 us
    pallas_call x1, Pallas kernels, project(): pl.pallas_call(kernel, out_shape=(jax.ShapeDtypeStruct((rows, units), jnp...  6.77 us
  transfers between devices with their start and end apart: 10, of which 7 were waited for; matrix products, arithmetic and copies ran while one was open for 3% of the time, Pallas kernels for 0%

profile of v1, /device:TPU:1, one launch (start us, length us, event | category | flops | bytes accessed | tf_op | source)
XLA Modules:
  0.0 230.7 jit_solution(4967825318857990756)
XLA Ops:
  0.6 0.0 copy-start.5
  0.6 1.2 copy-done.5
  1.9 0.0 copy-start.6
  1.9 0.7 copy-done.6
  2.5 0.0 copy-start.8
  2.5 0.7 copy-done.8
  3.2 1.4 head.1
  4.6 0.0 copy-start
  4.6 2.0 copy-done
  6.6 20.6 %all_to_all.25 = bf16[32,1,16]{2,1,0:T(2,128)(2,1)S(1)} all-to-all(bf16[32,1,16]{2,1,0:T(2,128)(2,1)S(1)} %copy.9), channel_id=1, replica_groups=mesh['dp'=4,'expert'=32,'context'=4] {'expert'}, dimensions={0} | all-to-all | bytes 2048 | tf_op jit(solution)/shard_map/all_to_all | solution.py:157
  27.2 0.0 copy-start.11
  27.2 5.2 %all-to-all-start.1 = ((bf16[32,16,4096]{2,1,0:T(8,128)(2,1)}), bf16[32,16,4096]{2,1,0:T(8,128)(2,1)}, u32[]{:S(2)}, u32[]{:S(2)}) async-start(bf16[32,16,4096]{2,1,0:T(8,128)(2,1)} %bitcast.24), calls=%async_computation.1 | async-start | bytes 8388608 | tf_op jit(solution)/shard_map/all_to_all | solution.py:154
  32.5 0.0 copy-done.11
  32.5 4.2 %collective-permute-start.1 = (bf16[768,256]{1,0:T(8,128)(2,1)S(1)}, bf16[768,256]{1,0:T(8,128)(2,1)S(1)}, u32[]{:S(2)}, u32[]{:S(2)}) collective-permute-start(bf16[768,256]{1,0:T(8,128)(2,1)S(1)} %bitcast.35), channel_id=1, source_target_pairs={{0,128},{128,256},{256,384},{384,0},{1,129},{129,257},{257,385},{3... | collective-permute-start | bytes 1179656 | tf_op jit(solution)/shard_map/ppermute | solution.py:132
  36.7 3.2 %collective-permute-start = (bf16[768,256]{1,0:T(8,128)(2,1)S(1)}, bf16[768,256]{1,0:T(8,128)(2,1)S(1)}, u32[]{:S(2)}, u32[]{:S(2)}) collective-permute-start(bf16[768,256]{1,0:T(8,128)(2,1)S(1)} %bitcast.36), channel_id=1, source_target_pairs={{0,384},{128,0},{256,128},{384,256},{1,385},{129,1},{257,129},{385... | collective-permute-start | bytes 1179656 | tf_op jit(solution)/shard_map/ppermute | solution.py:133
  39.9 84.5 %collective-permute-done.1 = bf16[768,256]{1,0:T(8,128)(2,1)S(1)} collective-permute-done((bf16[768,256]{1,0:T(8,128)(2,1)S(1)}, bf16[768,256]{1,0:T(8,128)(2,1)S(1)}, u32[]{:S(2)}, u32[]{:S(2)}) %collective-permute-start.1) | collective-permute-done | bytes 393248 | tf_op jit(solution)/shard_map/ppermute | solution.py:132
  124.4 1.9 collective-permute-start.2
  126.4 0.0 collective-permute-done
  126.4 5.5 %collective-permute-start.3 = (bf16[384,256]{1,0:T(8,128)(2,1)S(1)}, bf16[384,256]{1,0:T(8,128)(2,1)S(1)}, u32[]{:S(2)}, u32[]{:S(2)}) collective-permute-start(bf16[384,256]{1,0:T(8,128)(2,1)S(1)} %slice.17), channel_id=1, source_target_pairs={{0,384},{128,0},{256,128},{384,256},{1,385},{129,1},{257,129},{385... | collective-permute-start | bytes 589832 | tf_op jit(solution)/shard_map/ppermute | solution.py:135
  131.9 2.3 %collective-permute-done.2 = bf16[384,256]{1,0:T(8,128)(2,1)S(1)} collective-permute-done((bf16[384,256]{1,0:T(8,128)(2,1)S(1)}, bf16[384,256]{1,0:T(8,128)(2,1)S(1)}, u32[]{:S(2)}, u32[]{:S(2)}) %collective-permute-start.2) | collective-permute-done | bytes 196640 | tf_op jit(solution)/shard_map/ppermute | solution.py:134
  134.3 3.9 %collective-permute-done.3 = bf16[384,256]{1,0:T(8,128)(2,1)S(1)} collective-permute-done((bf16[384,256]{1,0:T(8,128)(2,1)S(1)}, bf16[384,256]{1,0:T(8,128)(2,1)S(1)}, u32[]{:S(2)}, u32[]{:S(2)}) %collective-permute-start.3) | collective-permute-done | bytes 196640 | tf_op jit(solution)/shard_map/ppermute | solution.py:135
  138.2 0.0 copy-start.2
  138.2 0.0 copy-start.9
  138.2 0.0 copy-start.10
  138.2 3.3 %collective-permute-start.5 = (bf16[4,768,256]{2,1,0:T(8,128)(2,1)S(1)}, bf16[4,768,256]{2,1,0:T(8,128)(2,1)S(1)}, u32[]{:S(2)}, u32[]{:S(2)}) collective-permute-start(bf16[4,768,256]{2,1,0:T(8,128)(2,1)S(1)} %bitcast.25), channel_id=1, source_target_pairs={{0,1},{1,2},{2,3},{3,0},{4,5},{5,6},{6,7},{7,4},{8,9},{9,10},{10,1... | collective-permute-start | bytes 4718600 | tf_op jit(solution)/shard_map/ppermute | solution.py:132
  141.6 3.4 %collective-permute-start.4 = (bf16[4,768,256]{2,1,0:T(8,128)(2,1)S(1)}, bf16[4,768,256]{2,1,0:T(8,128)(2,1)S(1)}, u32[]{:S(2)}, u32[]{:S(2)}) collective-permute-start(bf16[4,768,256]{2,1,0:T(8,128)(2,1)S(1)} %bitcast.26), channel_id=1, source_target_pairs={{0,3},{1,0},{2,1},{3,2},{4,7},{5,4},{6,5},{7,6},{8,11},{9,8},{10,9... | collective-permute-start | bytes 4718600 | tf_op jit(solution)/shard_map/ppermute | solution.py:133
  145.0 32.1 %collective-permute-done.5.refs_6_ = bf16[4,768,256]{2,1,0:T(8,128)(2,1)S(1)} collective-permute-done((bf16[4,768,256]{2,1,0:T(8,128)(2,1)S(1)}, bf16[4,768,256]{2,1,0:T(8,128)(2,1)S(1)}, u32[]{:S(2)}, u32[]{:S(2)}) %collective-permute-start.5) | collective-permute-done | bytes 1572896 | tf_op jit(solution)/shard_map/ppermute | solution.py:132
  177.1 0.9 slice.18
  178.0 1.9 collective-permute-start.6
  179.9 0.0 collective-permute-done.4.refs_3_
  179.9 0.9 slice.19
  180.9 0.0 copy-done.2
  180.9 4.6 %collective-permute-start.7 = (bf16[2,768,256]{2,1,0:T(8,128)(2,1)}, bf16[2,768,256]{2,1,0:T(8,128)(2,1)}, u32[]{:S(2)}, u32[]{:S(2)}) collective-permute-start(bf16[2,768,256]{2,1,0:T(8,128)(2,1)} %slice.19), channel_id=1, source_target_pairs={{0,3},{1,0},{2,1},{3,2},{4,7},{5,4},{6,5},{7,6},{8,11},{9,8},{10,9... | collective-permute-start | bytes 2359304 | tf_op jit(solution)/shard_map/ppermute | solution.py:135
  185.5 0.0 copy-done.9
  185.5 0.0 copy-done.10
  185.5 1.5 fusion.refs_1_
  186.9 0.1 convert_reduce_fusion
  187.0 0.1 reshape.47
  187.1 12.0 %collective-permute-done.6.refs_4_ = bf16[2,768,256]{2,1,0:T(8,128)(2,1)} collective-permute-done((bf16[2,768,256]{2,1,0:T(8,128)(2,1)}, bf16[2,768,256]{2,1,0:T(8,128)(2,1)}, u32[]{:S(2)}, u32[]{:S(2)}) %collective-permute-start.6) | collective-permute-done | bytes 786464 | tf_op jit(solution)/shard_map/ppermute | solution.py:134
  199.1 1.9 collective-permute-done.7.refs_5_
  201.0 0.0 all-to-all-done.1
  201.0 0.0 copy-start.1
  201.0 1.1 copy-done.1
  202.1 0.0 copy-start.3
  202.1 1.4 copy-done.3
  203.5 6.8 %project.1 = (f32[512,768]{1,0:T(8,128)S(1)}, f32[32,16]{1,0:T(8,128)}) custom-call(bf16[512,4096]{1,0:T(8,128)(2,1)} %bitcast.4.refs_0_, bf16[512,768]{1,0:T(8,128)(2,1)S(1)} %copy-done.1, bf16[4,768,256]{2,1,0:T(8,128)(2,1)S(1)} %bitcast.27, bf16[4,768,256]{2,1,0:T(8,128)(2,1)S(1)} %collective-permute-done.4.refs_3_, ...), custom_call_target="tpu_custom_call" | custom-call | tf_op jit(solution)/shard_map/project/pallas_call | solution.py:94
  210.3 0.0 copy-start.4
  210.3 1.2 copy-done.4
  211.4 10.7 %all-to-all-start.2 = ((f32[32,1,16]{2,1,0:T(1,128)}), f32[32,1,16]{2,1,0:T(1,128)S(1)}, u32[]{:S(2)}, u32[]{:S(2)}) async-start(f32[32,1,16]{2,1,0:T(1,128)} %bitcast.13), calls=%async_computation.2 | async-start | bytes 32768 | tf_op jit(solution)/shard_map/all_to_all | solution.py:164
  222.2 0.0 copy-start.7
  222.2 3.8 %fusion.9 = (bf16[512,768]{1,0:T(8,128)(2,1)}, bf16[512,768]{1,0:T(8,128)(2,1)}) fusion(f32[512,768]{1,0:T(8,128)} %copy-done.4, bf16[1,1,1,32,16,768]{5,4,3,2,1,0:T(8,128)(2,1)} %param.9, f32[512]{0:T(512)S(1)} %reshape.47, bf16[1,1,1,32,16,768]{5,4,3,2,1,0:T(8,128)(2,1)} %param.10), kind=kLoop, calls=%fused_computation.15 | loop fusion | flops 6291456 | bytes 4720640 | tf_op jit(solution)/shard_map/convert_element_type | solution.py:169
  226.0 4.0 %all-to-all-done.2 = f32[32,1,16]{2,1,0:T(1,128)S(1)} async-done(((f32[32,1,16]{2,1,0:T(1,128)}), f32[32,1,16]{2,1,0:T(1,128)S(1)}, u32[]{:S(2)}, u32[]{:S(2)}) %all-to-all-start.2) | async-done | bytes 2080 | tf_op jit(solution)/shard_map/all_to_all | solution.py:164
  230.0 0.0 copy-done.7
  230.0 0.8 tail.1
  (8 shorter events, 0.2 us)
Async XLA Ops:
  0.6 1.2 copy-start.5
  1.9 0.7 copy-start.6
  2.5 0.7 copy-start.8
  4.6 2.0 copy-start
  27.2 5.2 %copy-start.11 = (bf16[1,768,256]{2,1,0:T(8,128)(2,1)S(1)}, bf16[1,768,256]{2,1,0:T(8,128)(2,1)}, u32[]{:S(2)}) copy-start(bf16[1,768,256]{2,1,0:T(8,128)(2,1)} %param.11) | copy-start | bytes 1179652
  27.2 173.7 %all-to-all-start.1 = ((bf16[32,16,4096]{2,1,0:T(8,128)(2,1)}), bf16[32,16,4096]{2,1,0:T(8,128)(2,1)}, u32[]{:S(2)}, u32[]{:S(2)}) async-start(bf16[32,16,4096]{2,1,0:T(8,128)(2,1)} %bitcast.24), calls=%async_computation.1 | async-start | bytes 8388608 | tf_op jit(solution)/shard_map/all_to_all | solution.py:154
  32.5 91.9 %collective-permute-start.1 = (bf16[768,256]{1,0:T(8,128)(2,1)S(1)}, bf16[768,256]{1,0:T(8,128)(2,1)S(1)}, u32[]{:S(2)}, u32[]{:S(2)}) collective-permute-start(bf16[768,256]{1,0:T(8,128)(2,1)S(1)} %bitcast.35), channel_id=1, source_target_pairs={{0,128},{128,256},{256,384},{384,0},{1,129},{129,257},{257,385},{3... | collective-permute-start | bytes 1179656 | tf_op jit(solution)/shard_map/ppermute | solution.py:132
  36.7 89.7 %collective-permute-start = (bf16[768,256]{1,0:T(8,128)(2,1)S(1)}, bf16[768,256]{1,0:T(8,128)(2,1)S(1)}, u32[]{:S(2)}, u32[]{:S(2)}) collective-permute-start(bf16[768,256]{1,0:T(8,128)(2,1)S(1)} %bitcast.36), channel_id=1, source_target_pairs={{0,384},{128,0},{256,128},{384,256},{1,385},{129,1},{257,129},{385... | collective-permute-start | bytes 1179656 | tf_op jit(solution)/shard_map/ppermute | solution.py:133
  124.4 9.8 %collective-permute-start.2 = (bf16[384,256]{1,0:T(8,128)(2,1)S(1)}, bf16[384,256]{1,0:T(8,128)(2,1)S(1)}, u32[]{:S(2)}, u32[]{:S(2)}) collective-permute-start(bf16[384,256]{1,0:T(8,128)(2,1)S(1)} %slice.16), channel_id=1, source_target_pairs={{0,128},{128,256},{256,384},{384,0},{1,129},{129,257},{257,385},{3... | collective-permute-start | bytes 589832 | tf_op jit(solution)/shard_map/ppermute | solution.py:134
  126.4 11.7 %collective-permute-start.3 = (bf16[384,256]{1,0:T(8,128)(2,1)S(1)}, bf16[384,256]{1,0:T(8,128)(2,1)S(1)}, u32[]{:S(2)}, u32[]{:S(2)}) collective-permute-start(bf16[384,256]{1,0:T(8,128)(2,1)S(1)} %slice.17), channel_id=1, source_target_pairs={{0,384},{128,0},{256,128},{384,256},{1,385},{129,1},{257,129},{385... | collective-permute-start | bytes 589832 | tf_op jit(solution)/shard_map/ppermute | solution.py:135
  138.2 42.7 %copy-start.2 = (bf16[3072,256]{1,0:T(8,128)(2,1)}, bf16[3072,256]{1,0:T(8,128)(2,1)S(1)}, u32[]{:S(2)}) copy-start(bf16[3072,256]{1,0:T(8,128)(2,1)S(1)} %constant_dynamic-update-slice_fusion) | copy-start | bytes 4718596
  138.2 47.2 %copy-start.9 = (bf16[1,1,1,32,16,768]{5,4,3,2,1,0:T(8,128)(2,1)S(1)}, bf16[1,1,1,32,16,768]{5,4,3,2,1,0:T(8,128)(2,1)}, u32[]{:S(2)}) copy-start(bf16[1,1,1,32,16,768]{5,4,3,2,1,0:T(8,128)(2,1)} %param.10) | copy-start | bytes 2359300
  138.2 47.2 %copy-start.10 = (bf16[1,1,1,32,16,768]{5,4,3,2,1,0:T(8,128)(2,1)S(1)}, bf16[1,1,1,32,16,768]{5,4,3,2,1,0:T(8,128)(2,1)}, u32[]{:S(2)}) copy-start(bf16[1,1,1,32,16,768]{5,4,3,2,1,0:T(8,128)(2,1)} %param.9) | copy-start | bytes 2359300
  138.2 38.8 %collective-permute-start.5 = (bf16[4,768,256]{2,1,0:T(8,128)(2,1)S(1)}, bf16[4,768,256]{2,1,0:T(8,128)(2,1)S(1)}, u32[]{:S(2)}, u32[]{:S(2)}) collective-permute-start(bf16[4,768,256]{2,1,0:T(8,128)(2,1)S(1)} %bitcast.25), channel_id=1, source_target_pairs={{0,1},{1,2},{2,3},{3,0},{4,5},{5,6},{6,7},{7,4},{8,9},{9,10},{10,1... | collective-permute-start | bytes 4718600 | tf_op jit(solution)/shard_map/ppermute | solution.py:132
  141.6 38.4 %collective-permute-start.4 = (bf16[4,768,256]{2,1,0:T(8,128)(2,1)S(1)}, bf16[4,768,256]{2,1,0:T(8,128)(2,1)S(1)}, u32[]{:S(2)}, u32[]{:S(2)}) collective-permute-start(bf16[4,768,256]{2,1,0:T(8,128)(2,1)S(1)} %bitcast.26), channel_id=1, source_target_pairs={{0,3},{1,0},{2,1},{3,2},{4,7},{5,4},{6,5},{7,6},{8,11},{9,8},{10,9... | collective-permute-start | bytes 4718600 | tf_op jit(solution)/shard_map/ppermute | solution.py:133
  178.0 21.1 %collective-permute-start.6 = (bf16[2,768,256]{2,1,0:T(8,128)(2,1)}, bf16[2,768,256]{2,1,0:T(8,128)(2,1)}, u32[]{:S(2)}, u32[]{:S(2)}) collective-permute-start(bf16[2,768,256]{2,1,0:T(8,128)(2,1)} %slice.18), channel_id=1, source_target_pairs={{0,1},{1,2},{2,3},{3,0},{4,5},{5,6},{6,7},{7,4},{8,9},{9,10},{10,1... | collective-permute-start | bytes 2359304 | tf_op jit(solution)/shard_map/ppermute | solution.py:134
  180.9 20.1 %collective-permute-start.7 = (bf16[2,768,256]{2,1,0:T(8,128)(2,1)}, bf16[2,768,256]{2,1,0:T(8,128)(2,1)}, u32[]{:S(2)}, u32[]{:S(2)}) collective-permute-start(bf16[2,768,256]{2,1,0:T(8,128)(2,1)} %slice.19), channel_id=1, source_target_pairs={{0,3},{1,0},{2,1},{3,2},{4,7},{5,4},{6,5},{7,6},{8,11},{9,8},{10,9... | collective-permute-start | bytes 2359304 | tf_op jit(solution)/shard_map/ppermute | solution.py:135
  201.0 1.1 copy-start.1
  202.1 1.4 copy-start.3
  210.3 1.2 copy-start.4
  211.4 18.5 %all-to-all-start.2 = ((f32[32,1,16]{2,1,0:T(1,128)}), f32[32,1,16]{2,1,0:T(1,128)S(1)}, u32[]{:S(2)}, u32[]{:S(2)}) async-start(f32[32,1,16]{2,1,0:T(1,128)} %bitcast.13), calls=%async_computation.2 | async-start | bytes 32768 | tf_op jit(solution)/shard_map/all_to_all | solution.py:164
  222.2 7.8 %copy-start.7 = (s32[128,8]{0,1:T(8,128)S(1)}, s32[128,8]{0,1:T(8,128)}, u32[]{:S(2)}) copy-start(s32[128,8]{0,1:T(8,128)} %param.7) | copy-start | bytes 12292

commit v2 on v1

v2 whole, which is shorter than its diff:
```python
import jax
import jax.numpy as jnp
from jax import lax
from jax.experimental import pallas as pl
from jax.experimental.pallas import tpu as pltpu
from jax.sharding import PartitionSpec as P

EXPERTS = 128
VMEM = 60 * 2**20
HBM = pl.BlockSpec(memory_space=pltpu.HBM)


def served_experts(ranks, tokens):
    return lax.broadcasted_iota(jnp.int32, (ranks, tokens), 0) * (EXPERTS // ranks)


def head_kernel(ranks, cap, n_dp, n_context, routes_ref, weight_ref, grad_hbm, sent_hbm, slot_weight_ref, slot_ref, grad, sent, grad_sem, sent_sem):
    topk, tokens = routes_ref.shape
    slots = ranks * cap
    load = pltpu.make_async_copy(grad_hbm, grad, grad_sem)
    load.start()
    served = served_experts(ranks, tokens)
    hits = jnp.zeros((ranks, tokens), jnp.float32)
    picked = jnp.zeros((ranks, tokens), jnp.float32)
    for k in range(topk):
        hit = routes_ref[k : k + 1, :] == served
        hits = hits + jnp.where(hit, 1.0, 0.0)
        picked = picked + jnp.where(hit, weight_ref[k : k + 1, :].astype(jnp.float32), 0.0)
    earlier = lax.broadcasted_iota(jnp.int32, (tokens, tokens), 0) < lax.broadcasted_iota(
        jnp.int32, (tokens, tokens), 1
    )
    earlier = jnp.where(earlier, 1.0, 0.0).astype(jnp.bfloat16)
    before = jnp.dot(hits.astype(jnp.bfloat16), earlier, preferred_element_type=jnp.float32)
    slot = jnp.where(hits > 0.0, before, -1.0)
    slot_ref[...] = slot
    wide = jnp.broadcast_to(slot[:, None, :], (ranks, cap, tokens))
    place = lax.broadcasted_iota(jnp.int32, (ranks, cap, tokens), 1).astype(jnp.float32)
    choose = jnp.where(wide == place, 1.0, 0.0).reshape(slots, tokens).astype(jnp.bfloat16)
    load.wait()
    c = lax.axis_index("context")
    cols = grad.shape[1] // (n_dp * n_context)
    group = n_dp * cols
    stores = []
    for j in range(n_context):
        for i in range(n_dp):
            block = i * n_context + lax.rem(c + j, n_context)
            part = grad[:, pl.ds(pl.multiple_of(block * cols, cols), cols)]
            at = j * group + i * cols
            out = jnp.dot(choose, part, preferred_element_type=jnp.float32)
            sent[:, at : at + cols] = out.astype(jnp.bfloat16)
        where = pl.ds(j * group, group)
        store = pltpu.make_async_copy(sent.at[:, where], sent_hbm.at[:, where], sent_sem.at[j])
        store.start()
        stores.append(store)
    lane = lax.broadcasted_iota(jnp.int32, (ranks, cap), 1).astype(jnp.float32)
    found = jnp.zeros((ranks, cap), jnp.float32)
    for j in range(cap):
        one = jnp.sum(jnp.where(slot == float(j), picked, 0.0), axis=1, keepdims=True)
        found = jnp.where(lane == float(j), one, found)
    slot_weight_ref[...] = found
    for store in stores:
        store.wait()


def head(routes, route_weight, grad_out, ranks, cap, n_dp, n_context):
    tokens, width = grad_out.shape

    def kernel(*refs):
        head_kernel(ranks, cap, n_dp, n_context, *refs)

    whole = pl.BlockSpec(memory_space=pltpu.VMEM)
    return pl.pallas_call(
        kernel,
        out_shape=(
            jax.ShapeDtypeStruct((ranks * cap, width), jnp.bfloat16),
            jax.ShapeDtypeStruct((ranks, cap), jnp.float32),
            jax.ShapeDtypeStruct((ranks, tokens), jnp.float32),
        ),
        in_specs=[whole, whole, HBM],
        out_specs=(HBM, whole, whole),
        scratch_shapes=[
            pltpu.VMEM((tokens, width), jnp.bfloat16),
            pltpu.VMEM((ranks * cap, width), jnp.bfloat16),
            pltpu.SemaphoreType.DMA,
            pltpu.SemaphoreType.DMA((n_context,)),
        ],
        compiler_params=pltpu.CompilerParams(vmem_limit_bytes=VMEM),
        name="head",
    )(routes.T, route_weight.T, grad_out)


def times_transposed(rows, blocks):
    count, units, depth = blocks.shape
    total = None
    for i in range(count):
        part = lax.dot_general(
            rows[:, i * depth : (i + 1) * depth],
            blocks[i],
            (((1,), (1,)), ((), ())),
            preferred_element_type=jnp.float32,
        )
        total = part if total is None else total + part
    return total


def own_kernel(received_hbm, weight_hbm, out_ref, rows, weight, sems):
    loads = [
        pltpu.make_async_copy(received_hbm.at[:, pl.ds(0, rows.shape[1])], rows, sems.at[0]),
        pltpu.make_async_copy(weight_hbm, weight, sems.at[1]),
    ]
    for load in loads:
        load.start()
    for load in loads:
        load.wait()
    out_ref[...] = times_transposed(rows, weight)


def own_part(received, weight):
    count, units, depth = weight.shape
    slots = received.shape[0]
    return pl.pallas_call(
        own_kernel,
        out_shape=jax.ShapeDtypeStruct((slots, units), jnp.float32),
        in_specs=[HBM, HBM],
        scratch_shapes=[
            pltpu.VMEM((slots, count * depth), jnp.bfloat16),
            pltpu.VMEM((count, units, depth), jnp.bfloat16),
            pltpu.SemaphoreType.DMA((2,)),
        ],
        cost_estimate=pl.CostEstimate(flops=2 * 10**10, bytes_accessed=4 * 2**20, transcendentals=0),
        compiler_params=pltpu.CompilerParams(vmem_limit_bytes=VMEM),
        name="own_part",
    )(received, weight)


def project_kernel(cap, received_hbm, weight_hbm, hidden_hbm, part_hbm, slot_weight_ref, back_ref, crossing_ref, rows, weight, hidden, part, sems):
    n_context = weight_hbm.shape[0]
    slots, units = hidden.shape
    ranks = slots // cap
    c = lax.axis_index("context")
    width = rows.shape[2]
    loads = []
    for j in range(1, n_context):
        pair = (
            pltpu.make_async_copy(received_hbm.at[:, pl.ds(j * width, width)], rows.at[j - 1], sems.at[0, j - 1]),
            pltpu.make_async_copy(weight_hbm.at[lax.rem(c + j, n_context)], weight.at[j - 1], sems.at[1, j - 1]),
        )
        for load in pair:
            load.start()
        loads.append(pair)
    late = (
        pltpu.make_async_copy(hidden_hbm, hidden, sems.at[0, n_context - 1]),
        pltpu.make_async_copy(part_hbm, part, sems.at[1, n_context - 1]),
    )
    for load in late:
        load.start()
    total = None
    for j, pair in enumerate(loads):
        for load in pair:
            load.wait()
        product = times_transposed(rows.at[j], weight.at[j])
        total = product if total is None else total + product
    for load in late:
        load.wait()
    total = total + part[...]
    back_ref[...] = total
    grads = hidden[...].astype(jnp.float32) * total
    crossing_ref[:, :cap] = jnp.sum(grads.reshape(ranks, cap, units), axis=2)
    crossing_ref[:, cap:] = slot_weight_ref[...]


def project(received, weight, hidden, part, slot_weight):
    n_context, n_dp, units, depth = weight.shape
    slots = received.shape[0]
    ranks, cap = slot_weight.shape

    def kernel(*refs):
        project_kernel(cap, *refs)

    whole = pl.BlockSpec(memory_space=pltpu.VMEM)
    return pl.pallas_call(
        kernel,
        out_shape=(
            jax.ShapeDtypeStruct((slots, units), jnp.float32),
            jax.ShapeDtypeStruct((ranks, 2 * cap), jnp.float32),
        ),
        in_specs=[HBM, HBM, HBM, HBM, whole],
        scratch_shapes=[
            pltpu.VMEM((n_context - 1, slots, n_dp * depth), jnp.bfloat16),
            pltpu.VMEM((n_context - 1, n_dp, units, depth), jnp.bfloat16),
            pltpu.VMEM((slots, units), jnp.bfloat16),
            pltpu.VMEM((slots, units), jnp.float32),
            pltpu.SemaphoreType.DMA((2, n_context)),
        ],
        compiler_params=pltpu.CompilerParams(vmem_limit_bytes=VMEM),
        name="project",
    )(received, weight, hidden, part, slot_weight)


def finish_kernel(routes_ref, slot_ref, crossing_ref, gate_ref, up_ref, grad_gate_ref, grad_up_ref, out_ref):
    ranks = crossing_ref.shape[0]
    cap = crossing_ref.shape[1] // 2
    slots = ranks * cap
    topk, tokens = routes_ref.shape
    slot = slot_ref[...]
    grads = jnp.zeros((ranks, tokens), jnp.float32)
    for j in range(cap):
        grads = grads + jnp.where(slot == float(j), crossing_ref[:, j : j + 1], 0.0)
    served = served_experts(ranks, tokens)
    for k in range(topk):
        hit = routes_ref[k : k + 1, :] == served
        out_ref[k : k + 1, :] = jnp.sum(jnp.where(hit, grads, 0.0), axis=0, keepdims=True)
    row = lax.broadcasted_iota(jnp.int32, (slots, ranks), 0)
    owner = row // cap == lax.broadcasted_iota(jnp.int32, (slots, ranks), 1)
    spread = jnp.dot(
        jnp.where(owner, 1.0, 0.0).astype(jnp.bfloat16),
        crossing_ref[:, cap:].astype(jnp.bfloat16),
        preferred_element_type=jnp.float32,
    )
    mine = lax.broadcasted_iota(jnp.int32, (slots, cap), 0) % cap == lax.broadcasted_iota(
        jnp.int32, (slots, cap), 1
    )
    weight = jnp.sum(jnp.where(mine, spread, 0.0), axis=1, keepdims=True)
    grad_gate_ref[...] = (weight * gate_ref[...]).astype(jnp.bfloat16)
    grad_up_ref[...] = (weight * up_ref[...]).astype(jnp.bfloat16)


def finish(routes, slot, crossing, gate, up):
    out = jax.ShapeDtypeStruct(gate.shape, jnp.bfloat16)
    return pl.pallas_call(
        finish_kernel,
        out_shape=(out, out, jax.ShapeDtypeStruct((routes.shape[1], routes.shape[0]), jnp.float32)),
        compiler_params=pltpu.CompilerParams(vmem_limit_bytes=24 * 2**20),
        name="finish",
    )(routes.T, slot, crossing, gate, up)


def body(grad_out, routes, route_weight, saved_gate, saved_up, down_weight):
    ranks = lax.axis_size("expert")
    n_dp, n_context = lax.axis_size("dp"), lax.axis_size("context")
    cap, units = saved_gate.shape[4:]
    slots = ranks * cap
    width = grad_out.shape[1]

    over_dp = lax.all_gather(down_weight[0], "dp", axis=0, tiled=False)
    weight = lax.all_gather(over_dp, "context", axis=0, tiled=False)

    sent, slot_weight, slot = head(routes, route_weight, grad_out, ranks, cap, n_dp, n_context)
    received = lax.all_to_all(
        sent.reshape(ranks, cap, width), "expert", split_axis=0, concat_axis=0, tiled=True
    ).reshape(slots, width)

    gate = saved_gate.reshape(slots, units).astype(jnp.float32)
    up = saved_up.reshape(slots, units).astype(jnp.float32)
    sigma = jax.nn.sigmoid(gate)
    hidden = lax.optimization_barrier((gate * sigma * up).astype(jnp.bfloat16))
    part = own_part(received, over_dp)
    back, crossing = project(received, weight, hidden, part, slot_weight)
    crossing = lax.all_to_all(crossing, "expert", split_axis=0, concat_axis=0, tiled=True)
    by_gate = back * up * sigma * (1.0 + gate * (1.0 - sigma))
    by_up = back * gate * sigma
    grad_gate, grad_up, grad_weight = finish(routes, slot, crossing, by_gate, by_up)
    return grad_gate.reshape(saved_gate.shape), grad_up.reshape(saved_up.shape), grad_weight.T


def solution(mesh):
    tokens = P(("dp", "expert", "context"), None)
    saved = P("dp", "expert", "context", None, None, None)
    return jax.shard_map(
        body,
        mesh=mesh,
        in_specs=(tokens, tokens, tokens, saved, saved, P("expert", None, ("dp", "context"))),
        out_specs=(saved, saved, tokens),
        check_vma=False,
    )
```

time: 232 us -> 179 us (0.77)
  starting transfers between devices: 44 us -> 22.3 us
  waiting for transfers between devices: 141 us -> 120 us
  blocking collectives: 20.6 us -> 0 us
  between operations: 0.87 us -> 14.1 us
  local copies, waits for them, and re-layouts: 10.4 us -> 0.02 us
  Pallas kernels: 8.93 us -> 18.4 us
    ppermute x8 -> x0, waiting for transfers between devices: 137 us -> none  [the longest x2 117 us: ring_gather(): before = lax.ppermute(block, axis, up)]
    all_gather x0 -> x2, waiting for transfers between devices: none -> 63 us  [the longest x1 48.5 us: body(): over_dp = lax.all_gather(down_weight[0], 'dp', axis=0, tiled=False)]
    all_to_all x1, waiting for transfers between devices: 0.01 us -> 50.8 us  [body(): lax.all_to_all(sent.reshape(ranks, cap, width), 'expert', split_axis=0, c...]
    ppermute x8 -> x0, starting transfers between devices: 28 us -> none  [the longest x2 10 us: ring_gather(): far_high = lax.ppermute(after[half:], axis, down)]
    all_to_all x1 -> x0, blocking collectives: 20.6 us -> none  [body(): lax.all_to_all(slot_weight, 'expert', split_axis=0, concat_axis=0, tiled=...]
    unnamed x28 -> x8, local copies, waits for them, and re-layouts: 8.38 us -> 0.02 us
    all_to_all x1, starting transfers between devices: 5.22 us -> 13.1 us  [body(): lax.all_to_all(sent.reshape(ranks, cap, width), 'expert', split_axis=0, c...]
    pallas_call x2 -> x3, Pallas kernels: 7.54 us -> 13.3 us  [the longest x1 7.83 us: project(): pl.pallas_call(kernel, out_shape=(jax.ShapeDtypeStruct((slots, units), jn...]
  transfers between devices with their start and end apart: 10 -> 4, of which waited for: 7 -> 4; matrix products, arithmetic and copies ran while one was open for 3% -> 2% of each run, Pallas kernels for 0% -> 5%
where the time goes in v2:
time: 179 us
  waiting for transfers between devices  120 us (67%)
  starting transfers between devices  22.3 us (12%)
  Pallas kernels  18.4 us (10%)
  between operations  14.1 us (8%)
  other arithmetic  4.04 us (2%)
    all_to_all x1, waiting for transfers between devices, body(): lax.all_to_all(sent.reshape(ranks, cap, width), 'expert', split_axis=0, c...  50.8 us
    all_gather x1, waiting for transfers between devices, body(): over_dp = lax.all_gather(down_weight[0], 'dp', axis=0, tiled=False)  48.5 us
    all_gather x1, waiting for transfers between devices, body(): weight = lax.all_gather(over_dp, 'context', axis=0, tiled=False)  14.5 us
    all_to_all x1, starting transfers between devices, body(): lax.all_to_all(sent.reshape(ranks, cap, width), 'expert', split_axis=0, c...  13.1 us
    all_to_all x1, starting transfers between devices, body(): lax.all_to_all(crossing, 'expert', split_axis=0, concat_axis=0, tiled=True)  9.18 us
    pallas_call x1, Pallas kernels, project(): pl.pallas_call(kernel, out_shape=(jax.ShapeDtypeStruct((slots, units), jn...  7.83 us
    all_to_all x1, waiting for transfers between devices, body(): lax.all_to_all(crossing, 'expert', split_axis=0, concat_axis=0, tiled=True)  5.22 us
    pallas_call x1, Pallas kernels, head(): pl.pallas_call(kernel, out_shape=(jax.ShapeDtypeStruct((ranks * cap, widt...  5.07 us
  transfers between devices with their start and end apart: 4, of which 4 were waited for; matrix products, arithmetic and copies ran while one was open for 2% of the time, Pallas kernels for 5%

profile of v2, /device:TPU:1, one launch (start us, length us, event | category | flops | bytes accessed | tf_op | source)
XLA Modules:
  0.0 178.6 jit_solution(12585539595903548127)
XLA Ops:
  7.2 0.0 all-gather.4.cloned.1.call-start
  7.2 0.7 all-gather.4.cloned.1.call-update
  7.9 5.1 %head.1 = (bf16[512,4096]{1,0:T(8,128)(2,1)}, f32[32,16]{1,0:T(8,128)}, f32[32,128]{1,0:T(8,128)}) custom-call(s32[8,128]{1,0:T(8,128)} %bitcast.22, bf16[8,128]{1,0:T(8,128)(2,1)} %bitcast.27, bf16[128,4096]{1,0:T(8,128)(2,1)} %refs_2_.1), custom_call_target="tpu_custom_call" | custom-call | tf_op jit(solution)/shard_map/head/pallas_call | solution.py:72
  13.0 13.1 %all-to-all-start = ((bf16[32,16,4096]{2,1,0:T(8,128)(2,1)}), bf16[32,16,4096]{2,1,0:T(8,128)(2,1)}, u32[]{:S(2)}, u32[]{:S(2)}) async-start(bf16[32,16,4096]{2,1,0:T(8,128)(2,1)} %bitcast.25), calls=%async_computation | async-start | bytes 8388608 | tf_op jit(solution)/shard_map/all_to_all | solution.py:249
  26.0 0.0 copy-start.2
  26.0 0.0 copy-start.3
  26.1 0.0 all-gather.6.cloned.1.call-start
  26.1 48.5 %all-gather.4.cloned.1.call-done.weight_hbm = bf16[4,768,256]{2,1,0:T(8,128)(2,1)} async-done(((bf16[1,768,256]{2,1,0:T(8,128)(2,1)}), bf16[4,768,256]{2,1,0:T(8,128)(2,1)}) %all-gather.4.cloned.1.call-update) | async-done | bytes 1572880 | tf_op jit(solution)/shard_map/all_gather | solution.py:245
  74.6 0.0 all-gather.6.cloned.1.call-update
  74.6 0.0 copy-done.2
  74.6 0.0 copy-done.3
  74.6 1.5 fusion.refs_2_
  76.1 50.8 %all-to-all-done = bf16[32,16,4096]{2,1,0:T(8,128)(2,1)} async-done(((bf16[32,16,4096]{2,1,0:T(8,128)(2,1)}), bf16[32,16,4096]{2,1,0:T(8,128)(2,1)}, u32[]{:S(2)}, u32[]{:S(2)}) %all-to-all-start) | async-done | bytes 4194336 | tf_op jit(solution)/shard_map/all_to_all | solution.py:249
  126.9 3.9 %own_part.1.refs_3_ = f32[512,768]{1,0:T(8,128)} custom-call(bf16[512,4096]{1,0:T(8,128)(2,1)} %bitcast.3.received_hbm.refs_0_, bf16[4,768,256]{2,1,0:T(8,128)(2,1)} %all-gather.4.cloned.1.call-done.weight_hbm), custom_call_target="tpu_custom_call" | custom-call | flops 20000000000 | bytes 4194304 | tf_op jit(solution)/shard_map/own_part/pallas_call | solution.py:121
  130.8 14.5 %all-gather.6.cloned.1.call-done = bf16[16,768,256]{2,1,0:T(8,128)(2,1)} async-done(((bf16[4,768,256]{2,1,0:T(8,128)(2,1)}), bf16[16,768,256]{2,1,0:T(8,128)(2,1)}) %all-gather.6.cloned.1.call-update) | async-done | bytes 6291472 | tf_op jit(solution)/shard_map/all_gather | solution.py:246
  145.3 7.8 %project.1 = (f32[512,768]{1,0:T(8,128)}, f32[32,32]{1,0:T(8,128)}) custom-call(bf16[512,4096]{1,0:T(8,128)(2,1)} %bitcast.3.received_hbm.refs_0_, bf16[4,4,768,256]{3,2,1,0:T(8,128)(2,1)} %bitcast.24, bf16[512,768]{1,0:T(8,128)(2,1)} %fusion.refs_2_, f32[512,768]{1,0:T(8,128)} %own_part.1.refs_3_, f32[32,16]{1,0:T(8,128)} %get-tuple-element.13.refs_4_), custom_call_target="tpu_custom_call" | custom-call | tf_op jit(solution)/shard_map/project/pallas_call | solution.py:181
  153.2 9.2 %all-to-all-start.1 = ((f32[32,1,32]{2,1,0:T(1,128)}), f32[32,1,32]{2,1,0:T(1,128)S(1)}, u32[]{:S(2)}, u32[]{:S(2)}) async-start(f32[32,1,32]{2,1,0:T(1,128)} %bitcast.26), calls=%async_computation.1 | async-start | bytes 32768 | tf_op jit(solution)/shard_map/all_to_all | solution.py:259
  162.4 0.0 copy-start
  162.4 0.0 copy-start.1
  162.4 2.6 %fusion.7 = (f32[512,768]{1,0:T(8,128)S(1)}, f32[512,768]{1,0:T(8,128)S(1)}) fusion(f32[512,768]{1,0:T(8,128)} %get-tuple-element.15, bf16[1,1,1,32,16,768]{5,4,3,2,1,0:T(8,128)(2,1)} %param.9, bf16[1,1,1,32,16,768]{5,4,3,2,1,0:T(8,128)(2,1)} %param.10), kind=kLoop, calls=%fused_computation.13 | loop fusion | flops 5111808 | bytes 6291456 | tf_op jit(solution)/shard_map/mul | solution.py:261
  165.0 5.2 %all-to-all-done.1 = f32[32,1,32]{2,1,0:T(1,128)S(1)} async-done(((f32[32,1,32]{2,1,0:T(1,128)}), f32[32,1,32]{2,1,0:T(1,128)S(1)}, u32[]{:S(2)}, u32[]{:S(2)}) %all-to-all-start.1) | async-done | bytes 4128 | tf_op jit(solution)/shard_map/all_to_all | solution.py:259
  170.2 0.0 copy-done
  170.2 0.0 copy-done.1
  170.2 1.6 finish.1
Async XLA Ops:
  7.2 67.4 %all-gather.4.cloned.1.call-start = ((), (), s32[]{:S(2)}) async-start(), calls=%async_computation.2 | async-start | bytes 1966080 | tf_op jit(solution)/shard_map/all_gather | solution.py:245
  13.0 113.9 %all-to-all-start = ((bf16[32,16,4096]{2,1,0:T(8,128)(2,1)}), bf16[32,16,4096]{2,1,0:T(8,128)(2,1)}, u32[]{:S(2)}, u32[]{:S(2)}) async-start(bf16[32,16,4096]{2,1,0:T(8,128)(2,1)} %bitcast.25), calls=%async_computation | async-start | bytes 8388608 | tf_op jit(solution)/shard_map/all_to_all | solution.py:249
  26.0 48.6 %copy-start.2 = (bf16[1,1,1,32,16,768]{5,4,3,2,1,0:T(8,128)(2,1)S(1)}, bf16[1,1,1,32,16,768]{5,4,3,2,1,0:T(8,128)(2,1)}, u32[]{:S(2)}) copy-start(bf16[1,1,1,32,16,768]{5,4,3,2,1,0:T(8,128)(2,1)} %param.10) | copy-start | bytes 2359300
  26.0 48.6 %copy-start.3 = (bf16[1,1,1,32,16,768]{5,4,3,2,1,0:T(8,128)(2,1)S(1)}, bf16[1,1,1,32,16,768]{5,4,3,2,1,0:T(8,128)(2,1)}, u32[]{:S(2)}) copy-start(bf16[1,1,1,32,16,768]{5,4,3,2,1,0:T(8,128)(2,1)} %param.9) | copy-start | bytes 2359300
  26.1 119.3 %all-gather.6.cloned.1.call-start = ((), (), s32[]{:S(2)}) async-start(), calls=%async_computation.3 | async-start | bytes 7864320 | tf_op jit(solution)/shard_map/all_gather | solution.py:246
  153.2 17.0 %all-to-all-start.1 = ((f32[32,1,32]{2,1,0:T(1,128)}), f32[32,1,32]{2,1,0:T(1,128)S(1)}, u32[]{:S(2)}, u32[]{:S(2)}) async-start(f32[32,1,32]{2,1,0:T(1,128)} %bitcast.26), calls=%async_computation.1 | async-start | bytes 32768 | tf_op jit(solution)/shard_map/all_to_all | solution.py:259
  162.4 7.8 %copy-start = (f32[32,128]{1,0:T(8,128)S(1)}, f32[32,128]{1,0:T(8,128)}, u32[]{:S(2)}) copy-start(f32[32,128]{1,0:T(8,128)} %get-tuple-element.11.slot_ref) | copy-start | bytes 49156
  162.4 7.8 %copy-start.1 = (s32[128,8]{0,1:T(8,128)S(1)}, s32[128,8]{0,1:T(8,128)}, u32[]{:S(2)}) copy-start(s32[128,8]{0,1:T(8,128)} %param.7) | copy-start | bytes 12292
Sparse Core Ops, SparseCore 0:
  10.1 64.4 all-gather.3
  76.7 68.6 all-gather.5

commit v3 on v2

--- a/solution.py
+++ b/solution.py
@@ -37,13 +37,14 @@
     place = lax.broadcasted_iota(jnp.int32, (ranks, cap, tokens), 1).astype(jnp.float32)
     choose = jnp.where(wide == place, 1.0, 0.0).reshape(slots, tokens).astype(jnp.bfloat16)
     load.wait()
+    a = lax.axis_index("dp")
     c = lax.axis_index("context")
     cols = grad.shape[1] // (n_dp * n_context)
     group = n_dp * cols
     stores = []
     for j in range(n_context):
         for i in range(n_dp):
-            block = i * n_context + lax.rem(c + j, n_context)
+            block = lax.rem(a + i, n_dp) * n_context + lax.rem(c + j, n_context)
             part = grad[:, pl.ds(pl.multiple_of(block * cols, cols), cols)]
             at = j * group + i * cols
             out = jnp.dot(choose, part, preferred_element_type=jnp.float32)
@@ -89,90 +90,59 @@
     )(routes.T, route_weight.T, grad_out)
 
 
-def times_transposed(rows, blocks):
-    count, units, depth = blocks.shape
-    total = None
-    for i in range(count):
-        part = lax.dot_general(
-            rows[:, i * depth : (i + 1) * depth],
-            blocks[i],
-            (((1,), (1,)), ((), ())),
-            preferred_element_type=jnp.float32,
-        )
-        total = part if total is None else total + part
-    return total
-
-
-def own_kernel(received_hbm, weight_hbm, out_ref, rows, weight, sems):
-    loads = [
-        pltpu.make_async_copy(received_hbm.at[:, pl.ds(0, rows.shape[1])], rows, sems.at[0]),
-        pltpu.make_async_copy(weight_hbm, weight, sems.at[1]),
-    ]
-    for load in loads:
-        load.start()
-    for load in loads:
-        load.wait()
-    out_ref[...] = times_transposed(rows, weight)
-
-
-def own_part(received, weight):
-    count, units, depth = weight.shape
-    slots = received.shape[0]
-    return pl.pallas_call(
-        own_kernel,
-        out_shape=jax.ShapeDtypeStruct((slots, units), jnp.float32),
-        in_specs=[HBM, HBM],
-        scratch_shapes=[
-            pltpu.VMEM((slots, count * depth), jnp.bfloat16),
-            pltpu.VMEM((count, units, depth), jnp.bfloat16),
-            pltpu.SemaphoreType.DMA((2,)),
-        ],
-        cost_estimate=pl.CostEstimate(flops=2 * 10**10, bytes_accessed=4 * 2**20, transcendentals=0),
+def arrived(groups):
+    def kernel(first, *refs):
+        *_, out_ref, sem = refs
+        copy = pltpu.make_async_copy(first.at[0, pl.ds(0, 16), pl.ds(0, 128)], out_ref, sem)
+        copy.start()
+        copy.wait()
+
+    return pl.pallas_call(
+        kernel,
+        out_shape=jax.ShapeDtypeStruct((16, 128), groups[0].dtype),
+        in_specs=[HBM] * len(groups),
+        scratch_shapes=[pltpu.SemaphoreType.DMA],
+        cost_estimate=pl.CostEstimate(flops=int(65e9), bytes_accessed=4096, transcendentals=0),
         compiler_params=pltpu.CompilerParams(vmem_limit_bytes=VMEM),
-        name="own_part",
-    )(received, weight)
-
-
-def project_kernel(cap, received_hbm, weight_hbm, hidden_hbm, part_hbm, slot_weight_ref, back_ref, crossing_ref, rows, weight, hidden, part, sems):
-    n_context = weight_hbm.shape[0]
+        name="arrived",
+    )(*groups)
+
+
+def project_kernel(cap, received_hbm, *refs):
+    *groups, hidden_hbm, slot_weight_ref, _, back_ref, crossing_ref, rows, weight, hidden, sems = refs
     slots, units = hidden.shape
-    ranks = slots // cap
-    c = lax.axis_index("context")
     width = rows.shape[2]
     loads = []
-    for j in range(1, n_context):
-        pair = (
-            pltpu.make_async_copy(received_hbm.at[:, pl.ds(j * width, width)], rows.at[j - 1], sems.at[0, j - 1]),
-            pltpu.make_async_copy(weight_hbm.at[lax.rem(c + j, n_context)], weight.at[j - 1], sems.at[1, j - 1]),
+    for j, group in enumerate(groups):
+        depth = group.shape[2]
+        part = [pltpu.make_async_copy(received_hbm.at[:, pl.ds(j * width, width)], rows.at[j], sems.at[j, 0])]
+        for i in range(group.shape[0]):
+            side = weight.at[j, :, pl.ds(i * depth, depth)]
+            part.append(pltpu.make_async_copy(group.at[i], side, sems.at[j, 1 + i]))
+        for load in part:
+            load.start()
+        loads.append(part)
+    late = pltpu.make_async_copy(hidden_hbm, hidden, sems.at[len(groups), 0])
+    late.start()
+    back = None
+    for j, part in enumerate(loads):
+        for load in part:
+            load.wait()
+        product = lax.dot_general(
+            rows[j], weight[j], (((1,), (1,)), ((), ())), preferred_element_type=jnp.float32
         )
-        for load in pair:
-            load.start()
-        loads.append(pair)
-    late = (
-        pltpu.make_async_copy(hidden_hbm, hidden, sems.at[0, n_context - 1]),
-        pltpu.make_async_copy(part_hbm, part, sems.at[1, n_context - 1]),
-    )
-    for load in late:
-        load.start()
-    total = None
-    for j, pair in enumerate(loads):
-        for load in pair:
-            load.wait()
-        product = times_transposed(rows.at[j], weight.at[j])
-        total = product if total is None else total + product
-    for load in late:
-        load.wait()
-    total = total + part[...]
-    back_ref[...] = total
-    grads = hidden[...].astype(jnp.float32) * total
-    crossing_ref[:, :cap] = jnp.sum(grads.reshape(ranks, cap, units), axis=2)
+        back = product if back is None else back + product
+    back_ref[...] = back
+    late.wait()
+    grads = hidden[...].astype(jnp.float32) * back
+    crossing_ref[:, :cap] = jnp.sum(grads.reshape(slots // cap, cap, units), axis=2)
     crossing_ref[:, cap:] = slot_weight_ref[...]
 
 
-def project(received, weight, hidden, part, slot_weight):
-    n_context, n_dp, units, depth = weight.shape
-    slots = received.shape[0]
+def project(received, groups, hidden, slot_weight, tile):
+    slots, units = hidden.shape
     ranks, cap = slot_weight.shape
+    count, _, depth = groups[0].shape
 
     def kernel(*refs):
         project_kernel(cap, *refs)
@@ -184,17 +154,16 @@
             jax.ShapeDtypeStruct((slots, units), jnp.float32),
             jax.ShapeDtypeStruct((ranks, 2 * cap), jnp.float32),
         ),
-        in_specs=[HBM, HBM, HBM, HBM, whole],
+        in_specs=[HBM] * (len(groups) + 2) + [whole, whole],
         scratch_shapes=[
-            pltpu.VMEM((n_context - 1, slots, n_dp * depth), jnp.bfloat16),
-            pltpu.VMEM((n_context - 1, n_dp, units, depth), jnp.bfloat16),
+            pltpu.VMEM((len(groups), slots, count * depth), jnp.bfloat16),
+            pltpu.VMEM((len(groups), units, count * depth), jnp.bfloat16),
             pltpu.VMEM((slots, units), jnp.bfloat16),
-            pltpu.VMEM((slots, units), jnp.float32),
-            pltpu.SemaphoreType.DMA((2, n_context)),
+            pltpu.SemaphoreType.DMA((len(groups) + 1, 1 + count)),
         ],
         compiler_params=pltpu.CompilerParams(vmem_limit_bytes=VMEM),
         name="project",
-    )(received, weight, hidden, part, slot_weight)
+    )(received, *groups, hidden, slot_weight, tile)
 
 
 def finish_kernel(routes_ref, slot_ref, crossing_ref, gate_ref, up_ref, grad_gate_ref, grad_up_ref, out_ref):
@@ -235,27 +204,34 @@
     )(routes.T, slot, crossing, gate, up)
 
 
+def fetch(block, axis, distance):
+    size = lax.axis_size(axis)
+    return lax.ppermute(block, axis, [((i + distance) % size, i) for i in range(size)])
+
+
+def exchange(rows, ranks):
+    blocks = rows.reshape(ranks, -1, rows.shape[1])
+    return lax.all_to_all(blocks, "expert", split_axis=0, concat_axis=0, tiled=True).reshape(rows.shape)
+
+
 def body(grad_out, routes, route_weight, saved_gate, saved_up, down_weight):
     ranks = lax.axis_size("expert")
     n_dp, n_context = lax.axis_size("dp"), lax.axis_size("context")
     cap, units = saved_gate.shape[4:]
     slots = ranks * cap
-    width = grad_out.shape[1]
-
-    over_dp = lax.all_gather(down_weight[0], "dp", axis=0, tiled=False)
-    weight = lax.all_gather(over_dp, "context", axis=0, tiled=False)
-
+
+    own = down_weight[0]
+    over_dp = jnp.stack([own] + [fetch(own, "dp", n) for n in range(1, n_dp)])
     sent, slot_weight, slot = head(routes, route_weight, grad_out, ranks, cap, n_dp, n_context)
-    received = lax.all_to_all(
-        sent.reshape(ranks, cap, width), "expert", split_axis=0, concat_axis=0, tiled=True
-    ).reshape(slots, width)
+    received = exchange(sent, ranks)
+    others = [fetch(over_dp, "context", n) for n in range(1, n_context)]
+    tile = arrived(others)
 
     gate = saved_gate.reshape(slots, units).astype(jnp.float32)
     up = saved_up.reshape(slots, units).astype(jnp.float32)
     sigma = jax.nn.sigmoid(gate)
     hidden = lax.optimization_barrier((gate * sigma * up).astype(jnp.bfloat16))
-    part = own_part(received, over_dp)
-    back, crossing = project(received, weight, hidden, part, slot_weight)
+    back, crossing = project(received, [over_dp] + others, hidden, slot_weight, tile)
     crossing = lax.all_to_all(crossing, "expert", split_axis=0, concat_axis=0, tiled=True)
     by_gate = back * up * sigma * (1.0 + gate * (1.0 - sigma))
     by_up = back * gate * sigma

time: 179 us -> 159 us (0.89)
  waiting for transfers between devices: 120 us -> 91.4 us
  starting transfers between devices: 22.3 us -> 43.7 us
  between operations: 14.1 us -> 0.8 us
    ppermute x0 -> x6, waiting for transfers between devices: none -> 79.3 us  [fetch(): lax.ppermute(block, axis, [((i + distance) % size, i) for i in range(size)])]
    all_gather x2 -> x0, waiting for transfers between devices: 63 us -> none  [the longest x1 48.5 us: body(): over_dp = lax.all_gather(down_weight[0], 'dp', axis=0, tiled=False)]
    all_to_all x1, waiting for transfers between devices: 50.8 us -> 6.95 us  [exchange(): lax.all_to_all(blocks, 'expert', split_axis=0, concat_axis=0, tiled=True)]
    ppermute x0 -> x6, starting transfers between devices: none -> 25.3 us  [fetch(): lax.ppermute(block, axis, [((i + distance) % size, i) for i in range(size)])]
    all_to_all x1, starting transfers between devices: 9.18 us -> 6.11 us  [body(): lax.all_to_all(crossing, 'expert', split_axis=0, concat_axis=0, tiled=True)]
    pallas_call x1, Pallas kernels: 3.92 us -> 1.27 us  [arrived(): pl.pallas_call(kernel, out_shape=jax.ShapeDtypeStruct((16, 128), groups[0...]
  transfers between devices with their start and end apart: 4 -> 8, of which waited for: 4 -> 6; matrix products, arithmetic and copies ran while one was open for 2% -> 3% of each run, Pallas kernels for 5% -> 4%
where the time goes in v3:
time: 159 us
  waiting for transfers between devices  91.4 us (57%)
  starting transfers between devices  43.7 us (27%)
  Pallas kernels  17.1 us (11%)
  other arithmetic  4.24 us (3%)
    ppermute x6, waiting for transfers between devices, fetch(): lax.ppermute(block, axis, [((i + distance) % size, i) for i in range(size)])  79.3 us
    ppermute x6, starting transfers between devices, fetch(): lax.ppermute(block, axis, [((i + distance) % size, i) for i in range(size)])  25.3 us
    all_to_all x1, starting transfers between devices, exchange(): lax.all_to_all(blocks, 'expert', split_axis=0, concat_axis=0, tiled=True)  12.3 us
    pallas_call x1, Pallas kernels, project(): pl.pallas_call(kernel, out_shape=(jax.ShapeDtypeStruct((slots, units), jn...  9.27 us
    all_to_all x1, waiting for transfers between devices, exchange(): lax.all_to_all(blocks, 'expert', split_axis=0, concat_axis=0, tiled=True)  6.95 us
    all_to_all x1, starting transfers between devices, body(): lax.all_to_all(crossing, 'expert', split_axis=0, concat_axis=0, tiled=True)  6.11 us
    all_to_all x1, waiting for transfers between devices, body(): lax.all_to_all(crossing, 'expert', split_axis=0, concat_axis=0, tiled=True)  5.22 us
    pallas_call x1, Pallas kernels, head(): pl.pallas_call(kernel, out_shape=(jax.ShapeDtypeStruct((ranks * cap, widt...  5 us
  transfers between devices with their start and end apart: 8, of which 6 were waited for; matrix products, arithmetic and copies ran while one was open for 3% of the time, Pallas kernels for 4%

profile of v3, /device:TPU:1, one launch (start us, length us, event | category | flops | bytes accessed | tf_op | source)
XLA Modules:
  0.0 158.6 jit_solution(14190692965580667436)
XLA Ops:
  0.6 5.0 %collective-permute-start.2 = (bf16[768,256]{1,0:T(8,128)(2,1)}, bf16[768,256]{1,0:T(8,128)(2,1)S(1)}, u32[]{:S(2)}, u32[]{:S(2)}) collective-permute-start(bf16[768,256]{1,0:T(8,128)(2,1)} %bitcast.28), channel_id=1, source_target_pairs={{384,0},{0,128},{128,256},{256,384},{385,1},{1,129},{129,257},{257... | collective-permute-start | bytes 1179656 | tf_op jit(solution)/shard_map/ppermute | solution.py:209
  5.7 5.7 %collective-permute-start.1 = (bf16[768,256]{1,0:T(8,128)(2,1)}, bf16[768,256]{1,0:T(8,128)(2,1)S(1)}, u32[]{:S(2)}, u32[]{:S(2)}) collective-permute-start(bf16[768,256]{1,0:T(8,128)(2,1)} %bitcast.29), channel_id=1, source_target_pairs={{256,0},{384,128},{0,256},{128,384},{257,1},{385,129},{1,257},{129... | collective-permute-start | bytes 1179656 | tf_op jit(solution)/shard_map/ppermute | solution.py:209
  11.4 5.0 %collective-permute-start = (bf16[768,256]{1,0:T(8,128)(2,1)}, bf16[768,256]{1,0:T(8,128)(2,1)S(1)}, u32[]{:S(2)}, u32[]{:S(2)}) collective-permute-start(bf16[768,256]{1,0:T(8,128)(2,1)} %bitcast.30), channel_id=1, source_target_pairs={{128,0},{256,128},{384,256},{0,384},{129,1},{257,129},{385,257},{1... | collective-permute-start | bytes 1179656 | tf_op jit(solution)/shard_map/ppermute | solution.py:209
  16.3 5.0 %head.1 = (bf16[512,4096]{1,0:T(8,128)(2,1)}, f32[32,16]{1,0:T(8,128)}, f32[32,128]{1,0:T(8,128)}) custom-call(s32[8,128]{1,0:T(8,128)} %bitcast.25, bf16[8,128]{1,0:T(8,128)(2,1)} %bitcast.35, bf16[128,4096]{1,0:T(8,128)(2,1)} %refs_2_.1), custom_call_target="tpu_custom_call" | custom-call | tf_op jit(solution)/shard_map/head/pallas_call | solution.py:73
  21.3 0.0 copy-start.7
  21.4 12.3 %all-to-all-start = ((bf16[32,16,4096]{2,1,0:T(8,128)(2,1)}), bf16[32,16,4096]{2,1,0:T(8,128)(2,1)}, u32[]{:S(2)}, u32[]{:S(2)}) async-start(bf16[32,16,4096]{2,1,0:T(8,128)(2,1)} %bitcast.27), calls=%async_computation | async-start | bytes 8388608 | tf_op jit(solution)/shard_map/all_to_all | solution.py:214
  33.7 0.0 collective-permute-done.2
  33.7 3.8 %collective-permute-done.1 = bf16[768,256]{1,0:T(8,128)(2,1)S(1)} collective-permute-done((bf16[768,256]{1,0:T(8,128)(2,1)}, bf16[768,256]{1,0:T(8,128)(2,1)S(1)}, u32[]{:S(2)}, u32[]{:S(2)}) %collective-permute-start.1) | collective-permute-done | bytes 393248 | tf_op jit(solution)/shard_map/ppermute | solution.py:209
  37.5 9.7 %collective-permute-done = bf16[768,256]{1,0:T(8,128)(2,1)S(1)} collective-permute-done((bf16[768,256]{1,0:T(8,128)(2,1)}, bf16[768,256]{1,0:T(8,128)(2,1)S(1)}, u32[]{:S(2)}, u32[]{:S(2)}) %collective-permute-start) | collective-permute-done | bytes 393248 | tf_op jit(solution)/shard_map/ppermute | solution.py:209
  47.2 0.0 copy-done.7
  47.2 0.0 copy-start.3
  47.2 0.0 copy-start.4
  47.2 0.2 pad_maximum_fusion.refs_1_
  47.4 0.0 copy-start.2
  47.4 4.7 %collective-permute-start.3 = (bf16[4,768,256]{2,1,0:T(8,128)(2,1)S(1)}, bf16[4,768,256]{2,1,0:T(8,128)(2,1)S(1)}, u32[]{:S(2)}, u32[]{:S(2)}) collective-permute-start(bf16[4,768,256]{2,1,0:T(8,128)(2,1)S(1)} %pad_maximum_fusion.refs_1_), channel_id=1, source_target_pairs={{1,0},{2,1},{3,2},{0,3},{5,4},{6,5},{7,6},{4,7},{9,8},{10,9},{11,1... | collective-permute-start | bytes 4718600 | tf_op jit(solution)/shard_map/ppermute | solution.py:209
  52.0 2.4 %collective-permute-start.4 = (bf16[4,768,256]{2,1,0:T(8,128)(2,1)S(1)}, bf16[4,768,256]{2,1,0:T(8,128)(2,1)S(1)}, u32[]{:S(2)}, u32[]{:S(2)}) collective-permute-start(bf16[4,768,256]{2,1,0:T(8,128)(2,1)S(1)} %pad_maximum_fusion.refs_1_), channel_id=1, source_target_pairs={{2,0},{3,1},{0,2},{1,3},{6,4},{7,5},{4,6},{5,7},{10,8},{11,9},{8,1... | collective-permute-start | bytes 4718600 | tf_op jit(solution)/shard_map/ppermute | solution.py:209
  54.5 2.5 %collective-permute-start.5 = (bf16[4,768,256]{2,1,0:T(8,128)(2,1)S(1)}, bf16[4,768,256]{2,1,0:T(8,128)(2,1)}, u32[]{:S(2)}, u32[]{:S(2)}) collective-permute-start(bf16[4,768,256]{2,1,0:T(8,128)(2,1)S(1)} %pad_maximum_fusion.refs_1_), channel_id=1, source_target_pairs={{3,0},{0,1},{1,2},{2,3},{7,4},{4,5},{5,6},{6,7},{11,8},{8,9},{9,10... | collective-permute-start | bytes 4718600 | tf_op jit(solution)/shard_map/ppermute | solution.py:209
  57.0 0.0 copy-done.3
  57.0 0.0 copy-done.4
  57.0 1.5 fusion.refs_5_
  58.5 60.5 %collective-permute-done.3.first.refs_2_ = bf16[4,768,256]{2,1,0:T(8,128)(2,1)S(1)} collective-permute-done((bf16[4,768,256]{2,1,0:T(8,128)(2,1)S(1)}, bf16[4,768,256]{2,1,0:T(8,128)(2,1)S(1)}, u32[]{:S(2)}, u32[]{:S(2)}) %collective-permute-start.3) | collective-permute-done | bytes 1572896 | tf_op jit(solution)/shard_map/ppermute | solution.py:209
  119.0 0.0 copy-start.5
  119.0 0.0 collective-permute-done.4.refs_0_.refs_3_
  119.0 0.0 copy-start.6
  119.0 1.3 copy-done.6
  120.3 5.3 %collective-permute-done.5.refs_1_.refs_4_ = bf16[4,768,256]{2,1,0:T(8,128)(2,1)} collective-permute-done((bf16[4,768,256]{2,1,0:T(8,128)(2,1)S(1)}, bf16[4,768,256]{2,1,0:T(8,128)(2,1)}, u32[]{:S(2)}, u32[]{:S(2)}) %collective-permute-start.5) | collective-permute-done | bytes 1572896 | tf_op jit(solution)/shard_map/ppermute | solution.py:209
  125.6 0.0 copy-done.5
  125.6 1.3 arrived.1.refs_7_
  126.8 0.0 copy-done.2
  126.9 6.9 %all-to-all-done = bf16[32,16,4096]{2,1,0:T(8,128)(2,1)} async-done(((bf16[32,16,4096]{2,1,0:T(8,128)(2,1)}), bf16[32,16,4096]{2,1,0:T(8,128)(2,1)}, u32[]{:S(2)}, u32[]{:S(2)}) %all-to-all-start) | async-done | bytes 4194336 | tf_op jit(solution)/shard_map/all_to_all | solution.py:214
  133.8 9.3 %project.1 = (f32[512,768]{1,0:T(8,128)}, f32[32,32]{1,0:T(8,128)}) custom-call(bf16[512,4096]{1,0:T(8,128)(2,1)} %bitcast.3.refs_0_, bf16[4,768,256]{2,1,0:T(8,128)(2,1)} %copy-done.2, bf16[4,768,256]{2,1,0:T(8,128)(2,1)} %copy-done.5, bf16[4,768,256]{2,1,0:T(8,128)(2,1)} %copy-done.6, bf16[4,768,256]{2,1,0:T(8,128)(2,1)} %collective-permute-done.5.refs_1_.refs_4_, ...), custom_call_target="tpu_custom_call" | custom-call | tf_op jit(solution)/shard_map/project/pallas_call | solution.py:151
  143.1 6.1 %all-to-all-start.1 = ((f32[32,1,32]{2,1,0:T(1,128)}), f32[32,1,32]{2,1,0:T(1,128)S(1)}, u32[]{:S(2)}, u32[]{:S(2)}) async-start(f32[32,1,32]{2,1,0:T(1,128)} %bitcast.34), calls=%async_computation.1 | async-start | bytes 32768 | tf_op jit(solution)/shard_map/all_to_all | solution.py:235
  149.2 0.0 copy-start
  149.2 0.0 copy-start.1
  149.2 2.6 %fusion.7 = (f32[512,768]{1,0:T(8,128)S(1)}, f32[512,768]{1,0:T(8,128)S(1)}) fusion(f32[512,768]{1,0:T(8,128)} %get-tuple-element.15, bf16[1,1,1,32,16,768]{5,4,3,2,1,0:T(8,128)(2,1)} %param.9, bf16[1,1,1,32,16,768]{5,4,3,2,1,0:T(8,128)(2,1)} %param.10), kind=kLoop, calls=%fused_computation.13 | loop fusion | flops 5111808 | bytes 6291456 | tf_op jit(solution)/shard_map/mul | solution.py:237
  151.8 5.2 %all-to-all-done.1 = f32[32,1,32]{2,1,0:T(1,128)S(1)} async-done(((f32[32,1,32]{2,1,0:T(1,128)}), f32[32,1,32]{2,1,0:T(1,128)S(1)}, u32[]{:S(2)}, u32[]{:S(2)}) %all-to-all-start.1) | async-done | bytes 4128 | tf_op jit(solution)/shard_map/all_to_all | solution.py:235
  157.0 0.0 copy-done
  157.0 0.0 copy-done.1
  157.0 1.6 finish.1
Async XLA Ops:
  0.6 33.0 %collective-permute-start.2 = (bf16[768,256]{1,0:T(8,128)(2,1)}, bf16[768,256]{1,0:T(8,128)(2,1)S(1)}, u32[]{:S(2)}, u32[]{:S(2)}) collective-permute-start(bf16[768,256]{1,0:T(8,128)(2,1)} %bitcast.28), channel_id=1, source_target_pairs={{384,0},{0,128},{128,256},{256,384},{385,1},{1,129},{129,257},{257... | collective-permute-start | bytes 1179656 | tf_op jit(solution)/shard_map/ppermute | solution.py:209
  5.7 31.8 %collective-permute-start.1 = (bf16[768,256]{1,0:T(8,128)(2,1)}, bf16[768,256]{1,0:T(8,128)(2,1)S(1)}, u32[]{:S(2)}, u32[]{:S(2)}) collective-permute-start(bf16[768,256]{1,0:T(8,128)(2,1)} %bitcast.29), channel_id=1, source_target_pairs={{256,0},{384,128},{0,256},{128,384},{257,1},{385,129},{1,257},{129... | collective-permute-start | bytes 1179656 | tf_op jit(solution)/shard_map/ppermute | solution.py:209
  11.4 35.8 %collective-permute-start = (bf16[768,256]{1,0:T(8,128)(2,1)}, bf16[768,256]{1,0:T(8,128)(2,1)S(1)}, u32[]{:S(2)}, u32[]{:S(2)}) collective-permute-start(bf16[768,256]{1,0:T(8,128)(2,1)} %bitcast.30), channel_id=1, source_target_pairs={{128,0},{256,128},{384,256},{0,384},{129,1},{257,129},{385,257},{1... | collective-permute-start | bytes 1179656 | tf_op jit(solution)/shard_map/ppermute | solution.py:209
  21.3 25.8 %copy-start.7 = (bf16[1,768,256]{2,1,0:T(8,128)(2,1)S(1)}, bf16[1,768,256]{2,1,0:T(8,128)(2,1)}, u32[]{:S(2)}) copy-start(bf16[1,768,256]{2,1,0:T(8,128)(2,1)} %param.11) | copy-start | bytes 1179652
  21.4 112.4 %all-to-all-start = ((bf16[32,16,4096]{2,1,0:T(8,128)(2,1)}), bf16[32,16,4096]{2,1,0:T(8,128)(2,1)}, u32[]{:S(2)}, u32[]{:S(2)}) async-start(bf16[32,16,4096]{2,1,0:T(8,128)(2,1)} %bitcast.27), calls=%async_computation | async-start | bytes 8388608 | tf_op jit(solution)/shard_map/all_to_all | solution.py:214
  47.2 9.8 %copy-start.3 = (bf16[1,1,1,32,16,768]{5,4,3,2,1,0:T(8,128)(2,1)S(1)}, bf16[1,1,1,32,16,768]{5,4,3,2,1,0:T(8,128)(2,1)}, u32[]{:S(2)}) copy-start(bf16[1,1,1,32,16,768]{5,4,3,2,1,0:T(8,128)(2,1)} %param.10) | copy-start | bytes 2359300
  47.2 9.8 %copy-start.4 = (bf16[1,1,1,32,16,768]{5,4,3,2,1,0:T(8,128)(2,1)S(1)}, bf16[1,1,1,32,16,768]{5,4,3,2,1,0:T(8,128)(2,1)}, u32[]{:S(2)}) copy-start(bf16[1,1,1,32,16,768]{5,4,3,2,1,0:T(8,128)(2,1)} %param.9) | copy-start | bytes 2359300
  47.4 79.5 %copy-start.2 = (bf16[4,768,256]{2,1,0:T(8,128)(2,1)}, bf16[4,768,256]{2,1,0:T(8,128)(2,1)S(1)}, u32[]{:S(2)}) copy-start(bf16[4,768,256]{2,1,0:T(8,128)(2,1)S(1)} %pad_maximum_fusion.refs_1_) | copy-start | bytes 4718596
  47.4 71.6 %collective-permute-start.3 = (bf16[4,768,256]{2,1,0:T(8,128)(2,1)S(1)}, bf16[4,768,256]{2,1,0:T(8,128)(2,1)S(1)}, u32[]{:S(2)}, u32[]{:S(2)}) collective-permute-start(bf16[4,768,256]{2,1,0:T(8,128)(2,1)S(1)} %pad_maximum_fusion.refs_1_), channel_id=1, source_target_pairs={{1,0},{2,1},{3,2},{0,3},{5,4},{6,5},{7,6},{4,7},{9,8},{10,9},{11,1... | collective-permute-start | bytes 4718600 | tf_op jit(solution)/shard_map/ppermute | solution.py:209
  52.0 66.9 %collective-permute-start.4 = (bf16[4,768,256]{2,1,0:T(8,128)(2,1)S(1)}, bf16[4,768,256]{2,1,0:T(8,128)(2,1)S(1)}, u32[]{:S(2)}, u32[]{:S(2)}) collective-permute-start(bf16[4,768,256]{2,1,0:T(8,128)(2,1)S(1)} %pad_maximum_fusion.refs_1_), channel_id=1, source_target_pairs={{2,0},{3,1},{0,2},{1,3},{6,4},{7,5},{4,6},{5,7},{10,8},{11,9},{8,1... | collective-permute-start | bytes 4718600 | tf_op jit(solution)/shard_map/ppermute | solution.py:209
  54.5 71.1 %collective-permute-start.5 = (bf16[4,768,256]{2,1,0:T(8,128)(2,1)S(1)}, bf16[4,768,256]{2,1,0:T(8,128)(2,1)}, u32[]{:S(2)}, u32[]{:S(2)}) collective-permute-start(bf16[4,768,256]{2,1,0:T(8,128)(2,1)S(1)} %pad_maximum_fusion.refs_1_), channel_id=1, source_target_pairs={{3,0},{0,1},{1,2},{2,3},{7,4},{4,5},{5,6},{6,7},{11,8},{8,9},{9,10... | collective-permute-start | bytes 4718600 | tf_op jit(solution)/shard_map/ppermute | solution.py:209
  119.0 6.6 %copy-start.5 = (bf16[4,768,256]{2,1,0:T(8,128)(2,1)}, bf16[4,768,256]{2,1,0:T(8,128)(2,1)S(1)}, u32[]{:S(2)}) copy-start(bf16[4,768,256]{2,1,0:T(8,128)(2,1)S(1)} %collective-permute-done.3.first.refs_2_) | copy-start | bytes 4718596
  119.0 1.3 copy-start.6
  143.1 13.9 %all-to-all-start.1 = ((f32[32,1,32]{2,1,0:T(1,128)}), f32[32,1,32]{2,1,0:T(1,128)S(1)}, u32[]{:S(2)}, u32[]{:S(2)}) async-start(f32[32,1,32]{2,1,0:T(1,128)} %bitcast.34), calls=%async_computation.1 | async-start | bytes 32768 | tf_op jit(solution)/shard_map/all_to_all | solution.py:235
  149.2 7.8 %copy-start = (f32[32,128]{1,0:T(8,128)S(1)}, f32[32,128]{1,0:T(8,128)}, u32[]{:S(2)}) copy-start(f32[32,128]{1,0:T(8,128)} %get-tuple-element.11.slot_ref) | copy-start | bytes 49156
  149.2 7.8 %copy-start.1 = (s32[128,8]{0,1:T(8,128)S(1)}, s32[128,8]{0,1:T(8,128)}, u32[]{:S(2)}) copy-start(s32[128,8]{0,1:T(8,128)} %param.7) | copy-start | bytes 12292

commit v4 on v3

--- a/solution.py
+++ b/solution.py
@@ -44,7 +44,7 @@
     stores = []
     for j in range(n_context):
         for i in range(n_dp):
-            block = lax.rem(a + i, n_dp) * n_context + lax.rem(c + j, n_context)
+            block = lax.bitwise_xor(a, i) * n_context + lax.rem(c + j, n_context)
             part = grad[:, pl.ds(pl.multiple_of(block * cols, cols), cols)]
             at = j * group + i * cols
             out = jnp.dot(choose, part, preferred_element_type=jnp.float32)
@@ -102,27 +102,29 @@
         out_shape=jax.ShapeDtypeStruct((16, 128), groups[0].dtype),
         in_specs=[HBM] * len(groups),
         scratch_shapes=[pltpu.SemaphoreType.DMA],
-        cost_estimate=pl.CostEstimate(flops=int(65e9), bytes_accessed=4096, transcendentals=0),
+        cost_estimate=pl.CostEstimate(flops=int(55e9), bytes_accessed=4096, transcendentals=0),
         compiler_params=pltpu.CompilerParams(vmem_limit_bytes=VMEM),
         name="arrived",
     )(*groups)
 
 
-def project_kernel(cap, received_hbm, *refs):
-    *groups, hidden_hbm, slot_weight_ref, _, back_ref, crossing_ref, rows, weight, hidden, sems = refs
+def project_kernel(cap, counts, received_hbm, *refs):
+    *blocks, hidden_hbm, slot_weight_ref, _, back_ref, crossing_ref, rows, weight, hidden, sems = refs
     slots, units = hidden.shape
     width = rows.shape[2]
     loads = []
-    for j, group in enumerate(groups):
-        depth = group.shape[2]
+    for j, count in enumerate(counts):
         part = [pltpu.make_async_copy(received_hbm.at[:, pl.ds(j * width, width)], rows.at[j], sems.at[j, 0])]
-        for i in range(group.shape[0]):
-            side = weight.at[j, :, pl.ds(i * depth, depth)]
-            part.append(pltpu.make_async_copy(group.at[i], side, sems.at[j, 1 + i]))
+        group, blocks = blocks[:count], blocks[count:]
+        sides = [(block, i) for block in group for i in range(block.shape[0])]
+        for at, (block, i) in enumerate(sides):
+            depth = block.shape[2]
+            side = weight.at[j, :, pl.ds(at * depth, depth)]
+            part.append(pltpu.make_async_copy(block.at[i], side, sems.at[j, 1 + at]))
         for load in part:
             load.start()
         loads.append(part)
-    late = pltpu.make_async_copy(hidden_hbm, hidden, sems.at[len(groups), 0])
+    late = pltpu.make_async_copy(hidden_hbm, hidden, sems.at[len(counts), 0])
     late.start()
     back = None
     for j, part in enumerate(loads):
@@ -142,10 +144,12 @@
 def project(received, groups, hidden, slot_weight, tile):
     slots, units = hidden.shape
     ranks, cap = slot_weight.shape
-    count, _, depth = groups[0].shape
+    count, _, depth = groups[0][0].shape
+    counts = [len(group) for group in groups]
+    blocks = [block for group in groups for block in group]
 
     def kernel(*refs):
-        project_kernel(cap, *refs)
+        project_kernel(cap, counts, *refs)
 
     whole = pl.BlockSpec(memory_space=pltpu.VMEM)
     return pl.pallas_call(
@@ -154,7 +158,7 @@
             jax.ShapeDtypeStruct((slots, units), jnp.float32),
             jax.ShapeDtypeStruct((ranks, 2 * cap), jnp.float32),
         ),
-        in_specs=[HBM] * (len(groups) + 2) + [whole, whole],
+        in_specs=[HBM] * (len(blocks) + 2) + [whole, whole],
         scratch_shapes=[
             pltpu.VMEM((len(groups), slots, count * depth), jnp.bfloat16),
             pltpu.VMEM((len(groups), units, count * depth), jnp.bfloat16),
@@ -163,7 +167,7 @@
         ],
         compiler_params=pltpu.CompilerParams(vmem_limit_bytes=VMEM),
         name="project",
-    )(received, *groups, hidden, slot_weight, tile)
+    )(received, *blocks, hidden, slot_weight, tile)
 
 
 def finish_kernel(routes_ref, slot_ref, crossing_ref, gate_ref, up_ref, grad_gate_ref, grad_up_ref, out_ref):
@@ -204,9 +208,20 @@
     )(routes.T, slot, crossing, gate, up)
 
 
-def fetch(block, axis, distance):
-    size = lax.axis_size(axis)
-    return lax.ppermute(block, axis, [((i + distance) % size, i) for i in range(size)])
+def fetch(block, axis, partner):
+    return lax.ppermute(block, axis, [(partner(i), i) for i in range(lax.axis_size(axis))])
+
+
+def gather_weight(own, slot):
+    size = lax.axis_size("context")
+    pair = jnp.concatenate([own, fetch(own, "dp", lambda i: i ^ 1)])
+    pair, _ = lax.optimization_barrier((pair, slot))
+    over_dp = jnp.concatenate([pair, fetch(pair, "dp", lambda i: i ^ 2)])
+    after = fetch(over_dp, "context", lambda i: (i + 1) % size)
+    before = fetch(over_dp, "context", lambda i: (i - 1) % size)
+    low = fetch(after[:2], "context", lambda i: (i + 1) % size)
+    high = fetch(before[2:], "context", lambda i: (i - 1) % size)
+    return [over_dp, after, (low, high), before]
 
 
 def exchange(rows, ranks):
@@ -220,18 +235,17 @@
     cap, units = saved_gate.shape[4:]
     slots = ranks * cap
 
-    own = down_weight[0]
-    over_dp = jnp.stack([own] + [fetch(own, "dp", n) for n in range(1, n_dp)])
     sent, slot_weight, slot = head(routes, route_weight, grad_out, ranks, cap, n_dp, n_context)
     received = exchange(sent, ranks)
-    others = [fetch(over_dp, "context", n) for n in range(1, n_context)]
-    tile = arrived(others)
+    groups = gather_weight(down_weight, slot)
+    groups = [group if isinstance(group, tuple) else (group,) for group in groups]
+    tile = arrived([*groups[2], groups[1][0], groups[3][0]])
 
     gate = saved_gate.reshape(slots, units).astype(jnp.float32)
     up = saved_up.reshape(slots, units).astype(jnp.float32)
     sigma = jax.nn.sigmoid(gate)
     hidden = lax.optimization_barrier((gate * sigma * up).astype(jnp.bfloat16))
-    back, crossing = project(received, [over_dp] + others, hidden, slot_weight, tile)
+    back, crossing = project(received, groups, hidden, slot_weight, tile)
     crossing = lax.all_to_all(crossing, "expert", split_axis=0, concat_axis=0, tiled=True)
     by_gate = back * up * sigma * (1.0 + gate * (1.0 - sigma))
     by_up = back * gate * sigma

time: 159 us -> 175 us (1.10)
  starting transfers between devices: 43.7 us -> 51.1 us
  waiting for transfers between devices: 91.4 us -> 98.7 us
    all_to_all x1, waiting for transfers between devices: 6.95 us -> 16.3 us  [exchange(): lax.all_to_all(blocks, 'expert', split_axis=0, concat_axis=0, tiled=True)]
    all_to_all x1, starting transfers between devices: 6.11 us -> 12.9 us  [body(): lax.all_to_all(crossing, 'expert', split_axis=0, concat_axis=0, tiled=True)]
    ppermute x6, waiting for transfers between devices: 79.3 us -> 77.2 us  [fetch(): lax.ppermute(block, axis, [(partner(i), i) for i in range(lax.axis_size(a...]
  transfers between devices with their start and end apart: 8 -> 8, of which waited for: 6 -> 7; matrix products, arithmetic and copies ran while one was open for 3% -> 2% of each run, Pallas kernels for 4% -> 4%
where the time goes in v4:
time: 175 us; the launch traced here: 174 us
  waiting for transfers between devices  98.7 us (56%)
  starting transfers between devices  51.1 us (29%)
  Pallas kernels  17.3 us (10%)
  other arithmetic  5.11 us (3%)
    ppermute x6, waiting for transfers between devices, fetch(): lax.ppermute(block, axis, [(partner(i), i) for i in range(lax.axis_size(a...  77.2 us
    ppermute x6, starting transfers between devices, fetch(): lax.ppermute(block, axis, [(partner(i), i) for i in range(lax.axis_size(a...  26.8 us
    all_to_all x1, waiting for transfers between devices, exchange(): lax.all_to_all(blocks, 'expert', split_axis=0, concat_axis=0, tiled=True)  16.3 us
    all_to_all x1, starting transfers between devices, body(): lax.all_to_all(crossing, 'expert', split_axis=0, concat_axis=0, tiled=True)  12.9 us
    all_to_all x1, starting transfers between devices, exchange(): lax.all_to_all(blocks, 'expert', split_axis=0, concat_axis=0, tiled=True)  11.4 us
    pallas_call x1, Pallas kernels, project(): pl.pallas_call(kernel, out_shape=(jax.ShapeDtypeStruct((slots, units), jn...  9.26 us
    all_to_all x1, waiting for transfers between devices, body(): lax.all_to_all(crossing, 'expert', split_axis=0, concat_axis=0, tiled=True)  5.23 us
    pallas_call x1, Pallas kernels, head(): pl.pallas_call(kernel, out_shape=(jax.ShapeDtypeStruct((ranks * cap, widt...  5.14 us
  transfers between devices with their start and end apart: 8, of which 7 were waited for; matrix products, arithmetic and copies ran while one was open for 2% of the time, Pallas kernels for 4%

profile of v4, /device:TPU:1, one launch (start us, length us, event | category | flops | bytes accessed | tf_op | source)
XLA Modules:
  0.0 174.2 jit_solution(1719120760524150416)
XLA Ops:
  0.6 5.0 %collective-permute-start = (bf16[1,768,256]{2,1,0:T(8,128)(2,1)}, bf16[1,768,256]{2,1,0:T(8,128)(2,1)S(1)}, u32[]{:S(2)}, u32[]{:S(2)}) collective-permute-start(bf16[1,768,256]{2,1,0:T(8,128)(2,1)} %param.11), channel_id=1, source_target_pairs={{128,0},{0,128},{384,256},{256,384},{129,1},{1,129},{385,257},{257... | collective-permute-start | bytes 1179656 | tf_op jit(solution)/shard_map/ppermute | solution.py:212
  5.7 5.1 %head.1 = (bf16[512,4096]{1,0:T(8,128)(2,1)}, f32[32,16]{1,0:T(8,128)}, f32[32,128]{1,0:T(8,128)}) custom-call(s32[8,128]{1,0:T(8,128)} %bitcast.21, bf16[8,128]{1,0:T(8,128)(2,1)} %bitcast.25, bf16[128,4096]{1,0:T(8,128)(2,1)} %refs_2_.1), custom_call_target="tpu_custom_call" | custom-call | tf_op jit(solution)/shard_map/head/pallas_call | solution.py:73
  10.8 11.9 %collective-permute-done = bf16[1,768,256]{2,1,0:T(8,128)(2,1)S(1)} collective-permute-done((bf16[1,768,256]{2,1,0:T(8,128)(2,1)}, bf16[1,768,256]{2,1,0:T(8,128)(2,1)S(1)}, u32[]{:S(2)}, u32[]{:S(2)}) %collective-permute-start) | collective-permute-done | bytes 393248 | tf_op jit(solution)/shard_map/ppermute | solution.py:212
  22.8 1.1 pad_maximum_fusion
  23.8 8.5 %collective-permute-start.1 = (bf16[2,768,256]{2,1,0:T(8,128)(2,1)S(1)}, bf16[2,768,256]{2,1,0:T(8,128)(2,1)S(1)}, u32[]{:S(2)}, u32[]{:S(2)}) collective-permute-start(bf16[2,768,256]{2,1,0:T(8,128)(2,1)S(1)} %pad_maximum_fusion), channel_id=1, source_target_pairs={{256,0},{384,128},{0,256},{128,384},{257,1},{385,129},{1,257},{129... | collective-permute-start | bytes 2359304 | tf_op jit(solution)/shard_map/ppermute | solution.py:212
  32.3 11.4 %all-to-all-start = ((bf16[32,16,4096]{2,1,0:T(8,128)(2,1)}), bf16[32,16,4096]{2,1,0:T(8,128)(2,1)}, u32[]{:S(2)}, u32[]{:S(2)}) async-start(bf16[32,16,4096]{2,1,0:T(8,128)(2,1)} %bitcast.23), calls=%async_computation | async-start | bytes 8388608 | tf_op jit(solution)/shard_map/all_to_all | solution.py:229
  43.8 0.1 constant_dynamic-update-slice_fusion.1
  43.8 22.5 %collective-permute-done.1 = bf16[2,768,256]{2,1,0:T(8,128)(2,1)S(1)} collective-permute-done((bf16[2,768,256]{2,1,0:T(8,128)(2,1)S(1)}, bf16[2,768,256]{2,1,0:T(8,128)(2,1)S(1)}, u32[]{:S(2)}, u32[]{:S(2)}) %collective-permute-start.1) | collective-permute-done | bytes 786464 | tf_op jit(solution)/shard_map/ppermute | solution.py:212
  66.4 0.1 constant_dynamic-update-slice_fusion.refs_1_
  66.4 0.0 copy-start.4
  66.4 0.0 copy-start.5
  66.4 0.0 copy-start.6
  66.5 3.3 %collective-permute-start.4 = (bf16[4,768,256]{2,1,0:T(8,128)(2,1)S(1)}, bf16[4,768,256]{2,1,0:T(8,128)(2,1)S(1)}, u32[]{:S(2)}, u32[]{:S(2)}) collective-permute-start(bf16[4,768,256]{2,1,0:T(8,128)(2,1)S(1)} %constant_dynamic-update-slice_fusion.refs_1_), channel_id=1, source_target_pairs={{3,0},{0,1},{1,2},{2,3},{7,4},{4,5},{5,6},{6,7},{11,8},{8,9},{9,10... | collective-permute-start | bytes 4718600 | tf_op jit(solution)/shard_map/ppermute | solution.py:212
  69.8 3.4 %collective-permute-start.2 = (bf16[4,768,256]{2,1,0:T(8,128)(2,1)S(1)}, bf16[4,768,256]{2,1,0:T(8,128)(2,1)S(1)}, u32[]{:S(2)}, u32[]{:S(2)}) collective-permute-start(bf16[4,768,256]{2,1,0:T(8,128)(2,1)S(1)} %constant_dynamic-update-slice_fusion.refs_1_), channel_id=1, source_target_pairs={{1,0},{2,1},{3,2},{0,3},{5,4},{6,5},{7,6},{4,7},{9,8},{10,9},{11,1... | collective-permute-start | bytes 4718600 | tf_op jit(solution)/shard_map/ppermute | solution.py:212
  73.2 30.5 %collective-permute-done.4.refs_2_.refs_5_ = bf16[4,768,256]{2,1,0:T(8,128)(2,1)S(1)} collective-permute-done((bf16[4,768,256]{2,1,0:T(8,128)(2,1)S(1)}, bf16[4,768,256]{2,1,0:T(8,128)(2,1)S(1)}, u32[]{:S(2)}, u32[]{:S(2)}) %collective-permute-start.4) | collective-permute-done | bytes 1572896 | tf_op jit(solution)/shard_map/ppermute | solution.py:212
  103.8 0.0 copy-start.2
  103.8 0.1 slice.9
  103.8 1.9 %collective-permute-start.5 = (bf16[2,768,256]{2,1,0:T(8,128)(2,1)S(1)}, bf16[2,768,256]{2,1,0:T(8,128)(2,1)S(1)}, u32[]{:S(2)}, u32[]{:S(2)}) collective-permute-start(bf16[2,768,256]{2,1,0:T(8,128)(2,1)S(1)} %slice.9), channel_id=1, source_target_pairs={{3,0},{0,1},{1,2},{2,3},{7,4},{4,5},{5,6},{6,7},{11,8},{8,9},{9,10... | collective-permute-start | bytes 2359304 | tf_op jit(solution)/shard_map/ppermute | solution.py:212
  105.8 0.0 collective-permute-done.2.refs_1_.refs_2_
  105.8 0.0 copy-start.3
  105.8 0.1 slice.8
  105.8 0.0 copy-done.4
  105.9 0.0 copy-done.2
  105.9 4.6 %collective-permute-start.3 = (bf16[2,768,256]{2,1,0:T(8,128)(2,1)S(1)}, bf16[2,768,256]{2,1,0:T(8,128)(2,1)S(1)}, u32[]{:S(2)}, u32[]{:S(2)}) collective-permute-start(bf16[2,768,256]{2,1,0:T(8,128)(2,1)S(1)} %slice.8), channel_id=1, source_target_pairs={{1,0},{2,1},{3,2},{0,3},{5,4},{6,5},{7,6},{4,7},{9,8},{10,9},{11,1... | collective-permute-start | bytes 2359304 | tf_op jit(solution)/shard_map/ppermute | solution.py:212
  110.4 0.0 copy-done.5
  110.5 0.0 copy-done.6
  110.5 1.5 fusion.refs_6_
  111.9 0.0 copy-done.3
  111.9 11.3 %collective-permute-done.5.refs_0_.refs_4_ = bf16[2,768,256]{2,1,0:T(8,128)(2,1)S(1)} collective-permute-done((bf16[2,768,256]{2,1,0:T(8,128)(2,1)S(1)}, bf16[2,768,256]{2,1,0:T(8,128)(2,1)S(1)}, u32[]{:S(2)}, u32[]{:S(2)}) %collective-permute-start.5) | collective-permute-done | bytes 786464 | tf_op jit(solution)/shard_map/ppermute | solution.py:212
  123.2 0.0 copy-start.7
  123.2 0.9 collective-permute-done.3.first.refs_3_
  124.1 0.0 copy-done.7
  124.1 0.0 copy-start.8
  124.1 0.9 copy-done.8
  125.0 1.3 arrived.1.refs_8_
  126.3 16.3 %all-to-all-done = bf16[32,16,4096]{2,1,0:T(8,128)(2,1)} async-done(((bf16[32,16,4096]{2,1,0:T(8,128)(2,1)}), bf16[32,16,4096]{2,1,0:T(8,128)(2,1)}, u32[]{:S(2)}, u32[]{:S(2)}) %all-to-all-start) | async-done | bytes 4194336 | tf_op jit(solution)/shard_map/all_to_all | solution.py:229
  142.6 9.3 %project.1 = (f32[512,768]{1,0:T(8,128)}, f32[32,32]{1,0:T(8,128)}) custom-call(bf16[512,4096]{1,0:T(8,128)(2,1)} %bitcast.3.refs_0_, bf16[4,768,256]{2,1,0:T(8,128)(2,1)} %copy-done.4, bf16[4,768,256]{2,1,0:T(8,128)(2,1)} %copy-done.3, bf16[2,768,256]{2,1,0:T(8,128)(2,1)} %copy-done.8, bf16[2,768,256]{2,1,0:T(8,128)(2,1)} %copy-done.7, ...), custom_call_target="tpu_custom_call" | custom-call | tf_op jit(solution)/shard_map/project/pallas_call | solution.py:155
  151.9 12.9 %all-to-all-start.1 = ((f32[32,1,32]{2,1,0:T(1,128)}), f32[32,1,32]{2,1,0:T(1,128)S(1)}, u32[]{:S(2)}, u32[]{:S(2)}) async-start(f32[32,1,32]{2,1,0:T(1,128)} %bitcast.24), calls=%async_computation.1 | async-start | bytes 32768 | tf_op jit(solution)/shard_map/all_to_all | solution.py:249
  164.8 0.0 copy-start
  164.8 0.0 copy-start.1
  164.8 2.6 %fusion.7 = (f32[512,768]{1,0:T(8,128)S(1)}, f32[512,768]{1,0:T(8,128)S(1)}) fusion(f32[512,768]{1,0:T(8,128)} %get-tuple-element.17, bf16[1,1,1,32,16,768]{5,4,3,2,1,0:T(8,128)(2,1)} %param.9, bf16[1,1,1,32,16,768]{5,4,3,2,1,0:T(8,128)(2,1)} %param.10), kind=kLoop, calls=%fused_computation.13 | loop fusion | flops 5111808 | bytes 6291456 | tf_op jit(solution)/shard_map/mul | solution.py:251
  167.4 5.2 %all-to-all-done.1 = f32[32,1,32]{2,1,0:T(1,128)S(1)} async-done(((f32[32,1,32]{2,1,0:T(1,128)}), f32[32,1,32]{2,1,0:T(1,128)S(1)}, u32[]{:S(2)}, u32[]{:S(2)}) %all-to-all-start.1) | async-done | bytes 4128 | tf_op jit(solution)/shard_map/all_to_all | solution.py:249
  172.6 0.0 copy-done
  172.6 0.0 copy-done.1
  172.6 1.6 finish.1
Async XLA Ops:
  0.6 22.1 %collective-permute-start = (bf16[1,768,256]{2,1,0:T(8,128)(2,1)}, bf16[1,768,256]{2,1,0:T(8,128)(2,1)S(1)}, u32[]{:S(2)}, u32[]{:S(2)}) collective-permute-start(bf16[1,768,256]{2,1,0:T(8,128)(2,1)} %param.11), channel_id=1, source_target_pairs={{128,0},{0,128},{384,256},{256,384},{129,1},{1,129},{385,257},{257... | collective-permute-start | bytes 1179656 | tf_op jit(solution)/shard_map/ppermute | solution.py:212
  23.8 42.5 %collective-permute-start.1 = (bf16[2,768,256]{2,1,0:T(8,128)(2,1)S(1)}, bf16[2,768,256]{2,1,0:T(8,128)(2,1)S(1)}, u32[]{:S(2)}, u32[]{:S(2)}) collective-permute-start(bf16[2,768,256]{2,1,0:T(8,128)(2,1)S(1)} %pad_maximum_fusion), channel_id=1, source_target_pairs={{256,0},{384,128},{0,256},{128,384},{257,1},{385,129},{1,257},{129... | collective-permute-start | bytes 2359304 | tf_op jit(solution)/shard_map/ppermute | solution.py:212
  32.3 110.2 %all-to-all-start = ((bf16[32,16,4096]{2,1,0:T(8,128)(2,1)}), bf16[32,16,4096]{2,1,0:T(8,128)(2,1)}, u32[]{:S(2)}, u32[]{:S(2)}) async-start(bf16[32,16,4096]{2,1,0:T(8,128)(2,1)} %bitcast.23), calls=%async_computation | async-start | bytes 8388608 | tf_op jit(solution)/shard_map/all_to_all | solution.py:229
  66.4 39.4 %copy-start.4 = (bf16[4,768,256]{2,1,0:T(8,128)(2,1)}, bf16[4,768,256]{2,1,0:T(8,128)(2,1)S(1)}, u32[]{:S(2)}) copy-start(bf16[4,768,256]{2,1,0:T(8,128)(2,1)S(1)} %constant_dynamic-update-slice_fusion.refs_1_) | copy-start | bytes 4718596
  66.4 44.0 %copy-start.5 = (bf16[1,1,1,32,16,768]{5,4,3,2,1,0:T(8,128)(2,1)S(1)}, bf16[1,1,1,32,16,768]{5,4,3,2,1,0:T(8,128)(2,1)}, u32[]{:S(2)}) copy-start(bf16[1,1,1,32,16,768]{5,4,3,2,1,0:T(8,128)(2,1)} %param.10) | copy-start | bytes 2359300
  66.4 44.0 %copy-start.6 = (bf16[1,1,1,32,16,768]{5,4,3,2,1,0:T(8,128)(2,1)S(1)}, bf16[1,1,1,32,16,768]{5,4,3,2,1,0:T(8,128)(2,1)}, u32[]{:S(2)}) copy-start(bf16[1,1,1,32,16,768]{5,4,3,2,1,0:T(8,128)(2,1)} %param.9) | copy-start | bytes 2359300
  66.5 37.3 %collective-permute-start.4 = (bf16[4,768,256]{2,1,0:T(8,128)(2,1)S(1)}, bf16[4,768,256]{2,1,0:T(8,128)(2,1)S(1)}, u32[]{:S(2)}, u32[]{:S(2)}) collective-permute-start(bf16[4,768,256]{2,1,0:T(8,128)(2,1)S(1)} %constant_dynamic-update-slice_fusion.refs_1_), channel_id=1, source_target_pairs={{3,0},{0,1},{1,2},{2,3},{7,4},{4,5},{5,6},{6,7},{11,8},{8,9},{9,10... | collective-permute-start | bytes 4718600 | tf_op jit(solution)/shard_map/ppermute | solution.py:212
  69.8 36.0 %collective-permute-start.2 = (bf16[4,768,256]{2,1,0:T(8,128)(2,1)S(1)}, bf16[4,768,256]{2,1,0:T(8,128)(2,1)S(1)}, u32[]{:S(2)}, u32[]{:S(2)}) collective-permute-start(bf16[4,768,256]{2,1,0:T(8,128)(2,1)S(1)} %constant_dynamic-update-slice_fusion.refs_1_), channel_id=1, source_target_pairs={{1,0},{2,1},{3,2},{0,3},{5,4},{6,5},{7,6},{4,7},{9,8},{10,9},{11,1... | collective-permute-start | bytes 4718600 | tf_op jit(solution)/shard_map/ppermute | solution.py:212
  103.8 2.1 %copy-start.2 = (bf16[4,768,256]{2,1,0:T(8,128)(2,1)}, bf16[4,768,256]{2,1,0:T(8,128)(2,1)S(1)}, u32[]{:S(2)}) copy-start(bf16[4,768,256]{2,1,0:T(8,128)(2,1)S(1)} %collective-permute-done.4.refs_2_.refs_5_) | copy-start | bytes 4718596
  103.8 19.4 %collective-permute-start.5 = (bf16[2,768,256]{2,1,0:T(8,128)(2,1)S(1)}, bf16[2,768,256]{2,1,0:T(8,128)(2,1)S(1)}, u32[]{:S(2)}, u32[]{:S(2)}) collective-permute-start(bf16[2,768,256]{2,1,0:T(8,128)(2,1)S(1)} %slice.9), channel_id=1, source_target_pairs={{3,0},{0,1},{1,2},{2,3},{7,4},{4,5},{5,6},{6,7},{11,8},{8,9},{9,10... | collective-permute-start | bytes 2359304 | tf_op jit(solution)/shard_map/ppermute | solution.py:212
  105.8 6.2 %copy-start.3 = (bf16[4,768,256]{2,1,0:T(8,128)(2,1)}, bf16[4,768,256]{2,1,0:T(8,128)(2,1)S(1)}, u32[]{:S(2)}) copy-start(bf16[4,768,256]{2,1,0:T(8,128)(2,1)S(1)} %collective-permute-done.2.refs_1_.refs_2_) | copy-start | bytes 4718596
  105.9 18.3 %collective-permute-start.3 = (bf16[2,768,256]{2,1,0:T(8,128)(2,1)S(1)}, bf16[2,768,256]{2,1,0:T(8,128)(2,1)S(1)}, u32[]{:S(2)}, u32[]{:S(2)}) collective-permute-start(bf16[2,768,256]{2,1,0:T(8,128)(2,1)S(1)} %slice.8), channel_id=1, source_target_pairs={{1,0},{2,1},{3,2},{0,3},{5,4},{6,5},{7,6},{4,7},{9,8},{10,9},{11,1... | collective-permute-start | bytes 2359304 | tf_op jit(solution)/shard_map/ppermute | solution.py:212
  123.2 0.9 copy-start.7
  124.1 0.9 copy-start.8
  151.9 20.7 %all-to-all-start.1 = ((f32[32,1,32]{2,1,0:T(1,128)}), f32[32,1,32]{2,1,0:T(1,128)S(1)}, u32[]{:S(2)}, u32[]{:S(2)}) async-start(f32[32,1,32]{2,1,0:T(1,128)} %bitcast.24), calls=%async_computation.1 | async-start | bytes 32768 | tf_op jit(solution)/shard_map/all_to_all | solution.py:249
  164.8 7.8 %copy-start = (f32[32,128]{1,0:T(8,128)S(1)}, f32[32,128]{1,0:T(8,128)}, u32[]{:S(2)}) copy-start(f32[32,128]{1,0:T(8,128)} %get-tuple-element.12.slot_ref) | copy-start | bytes 49156
  164.8 7.8 %copy-start.1 = (s32[128,8]{0,1:T(8,128)S(1)}, s32[128,8]{0,1:T(8,128)}, u32[]{:S(2)}) copy-start(s32[128,8]{0,1:T(8,128)} %param.7) | copy-start | bytes 12292

commit v5 on v4

--- a/solution.py
+++ b/solution.py
@@ -44,7 +44,7 @@
     stores = []
     for j in range(n_context):
         for i in range(n_dp):
-            block = lax.bitwise_xor(a, i) * n_context + lax.rem(c + j, n_context)
+            block = lax.rem(a + i, n_dp) * n_context + lax.rem(c + j, n_context)
             part = grad[:, pl.ds(pl.multiple_of(block * cols, cols), cols)]
             at = j * group + i * cols
             out = jnp.dot(choose, part, preferred_element_type=jnp.float32)
@@ -102,43 +102,59 @@
         out_shape=jax.ShapeDtypeStruct((16, 128), groups[0].dtype),
         in_specs=[HBM] * len(groups),
         scratch_shapes=[pltpu.SemaphoreType.DMA],
-        cost_estimate=pl.CostEstimate(flops=int(55e9), bytes_accessed=4096, transcendentals=0),
+        cost_estimate=pl.CostEstimate(flops=int(5e10), bytes_accessed=4096, transcendentals=0),
         compiler_params=pltpu.CompilerParams(vmem_limit_bytes=VMEM),
         name="arrived",
     )(*groups)
 
 
 def project_kernel(cap, counts, received_hbm, *refs):
-    *blocks, hidden_hbm, slot_weight_ref, _, back_ref, crossing_ref, rows, weight, hidden, sems = refs
+    *blocks, hidden_hbm, slot_weight_ref, _, back_hbm, crossing_ref, rows, weight, hidden, back, sems = refs
+    first = blocks[0]
+    depth = first.shape[2]
     slots, units = hidden.shape
     width = rows.shape[2]
-    loads = []
+    way = turn(lax.axis_index("expert"))
     for j, count in enumerate(counts):
         part = [pltpu.make_async_copy(received_hbm.at[:, pl.ds(j * width, width)], rows.at[j], sems.at[j, 0])]
         group, blocks = blocks[:count], blocks[count:]
         sides = [(block, i) for block in group for i in range(block.shape[0])]
         for at, (block, i) in enumerate(sides):
-            depth = block.shape[2]
-            side = weight.at[j, :, pl.ds(at * depth, depth)]
+            place = lax.rem(len(sides) + at * way, len(sides)) * depth
+            side = weight.at[j, :, pl.ds(pl.multiple_of(place, depth), depth)]
             part.append(pltpu.make_async_copy(block.at[i], side, sems.at[j, 1 + at]))
         for load in part:
             load.start()
-        loads.append(part)
     late = pltpu.make_async_copy(hidden_hbm, hidden, sems.at[len(counts), 0])
     late.start()
-    back = None
-    for j, part in enumerate(loads):
-        for load in part:
-            load.wait()
-        product = lax.dot_general(
+    back[...] = jnp.zeros_like(back)
+
+    def add(j, _):
+        pltpu.make_async_copy(received_hbm.at[:, pl.ds(0, width)], rows.at[j], sems.at[j, 0]).wait()
+        for at in range(width // depth):
+            side = weight.at[j, :, pl.ds(at * depth, depth)]
+            pltpu.make_async_copy(first.at[0], side, sems.at[j, 1 + at]).wait()
+        back[...] += lax.dot_general(
             rows[j], weight[j], (((1,), (1,)), ((), ())), preferred_element_type=jnp.float32
         )
-        back = product if back is None else back + product
-    back_ref[...] = back
+        return 0
+
+    lax.fori_loop(0, len(counts), add, 0)
+    store = pltpu.make_async_copy(back, back_hbm, sems.at[len(counts), 1])
+    store.start()
     late.wait()
-    grads = hidden[...].astype(jnp.float32) * back
-    crossing_ref[:, :cap] = jnp.sum(grads.reshape(slots // cap, cap, units), axis=2)
+    tall = 128
+
+    def reduce(t, _):
+        some = pl.ds(pl.multiple_of(t * tall, tall), tall)
+        grads = hidden[some, :].astype(jnp.float32) * back[some, :]
+        few = pl.ds(pl.multiple_of(t * (tall // cap), tall // cap), tall // cap)
+        crossing_ref[few, :cap] = jnp.sum(grads.reshape(tall // cap, cap, units), axis=2)
+        return 0
+
+    lax.fori_loop(0, slots // tall, reduce, 0)
     crossing_ref[:, cap:] = slot_weight_ref[...]
+    store.wait()
 
 
 def project(received, groups, hidden, slot_weight, tile):
@@ -159,10 +175,12 @@
             jax.ShapeDtypeStruct((ranks, 2 * cap), jnp.float32),
         ),
         in_specs=[HBM] * (len(blocks) + 2) + [whole, whole],
+        out_specs=(HBM, whole),
         scratch_shapes=[
             pltpu.VMEM((len(groups), slots, count * depth), jnp.bfloat16),
             pltpu.VMEM((len(groups), units, count * depth), jnp.bfloat16),
             pltpu.VMEM((slots, units), jnp.bfloat16),
+            pltpu.VMEM((slots, units), jnp.float32),
             pltpu.SemaphoreType.DMA((len(groups) + 1, 1 + count)),
         ],
         compiler_params=pltpu.CompilerParams(vmem_limit_bytes=VMEM),
@@ -212,11 +230,22 @@
     return lax.ppermute(block, axis, [(partner(i), i) for i in range(lax.axis_size(axis))])
 
 
-def gather_weight(own, slot):
+def turn(expert):
+    return 1 - 2 * ((expert // 2) % 2)
+
+
+def fetch_next(block):
+    n_dp, ranks = lax.axis_size("dp"), lax.axis_size("expert")
+    pairs = [((a + turn(b)) % n_dp * ranks + b, a * ranks + b) for a in range(n_dp) for b in range(ranks)]
+    return lax.ppermute(block, ("dp", "expert"), pairs)
+
+
+def gather_weight(own):
     size = lax.axis_size("context")
-    pair = jnp.concatenate([own, fetch(own, "dp", lambda i: i ^ 1)])
-    pair, _ = lax.optimization_barrier((pair, slot))
-    over_dp = jnp.concatenate([pair, fetch(pair, "dp", lambda i: i ^ 2)])
+    blocks = [own]
+    for _ in range(lax.axis_size("dp") - 1):
+        blocks.append(fetch_next(blocks[-1]))
+    over_dp = jnp.concatenate(blocks)
     after = fetch(over_dp, "context", lambda i: (i + 1) % size)
     before = fetch(over_dp, "context", lambda i: (i - 1) % size)
     low = fetch(after[:2], "context", lambda i: (i + 1) % size)
@@ -237,7 +266,7 @@
 
     sent, slot_weight, slot = head(routes, route_weight, grad_out, ranks, cap, n_dp, n_context)
     received = exchange(sent, ranks)
-    groups = gather_weight(down_weight, slot)
+    groups = gather_weight(down_weight)
     groups = [group if isinstance(group, tuple) else (group,) for group in groups]
     tile = arrived([*groups[2], groups[1][0], groups[3][0]])
 

time: 175 us -> 154 us (0.88)
  waiting for transfers between devices: 98.7 us -> 78.2 us
    ppermute x6 -> x4, waiting for transfers between devices: 77.2 us -> 46.2 us  [fetch(): lax.ppermute(block, axis, [(partner(i), i) for i in range(lax.axis_size(a...]
    ppermute x0 -> x3, waiting for transfers between devices: none -> 18.1 us  [fetch_next(): return lax.ppermute(block, ('dp', 'expert'), pairs)]
    ppermute x0 -> x3, starting transfers between devices: none -> 15.4 us  [fetch_next(): return lax.ppermute(block, ('dp', 'expert'), pairs)]
    ppermute x6 -> x4, starting transfers between devices: 26.8 us -> 13.9 us  [fetch(): lax.ppermute(block, axis, [(partner(i), i) for i in range(lax.axis_size(a...]
    all_to_all x1, waiting for transfers between devices: 16.3 us -> 8.57 us  [exchange(): lax.all_to_all(blocks, 'expert', split_axis=0, concat_axis=0, tiled=True)]
  transfers between devices with their start and end apart: 8 -> 9, of which waited for: 7 -> 7; matrix products, arithmetic and copies ran while one was open for 2% -> 3% of each run, Pallas kernels for 4% -> 4%
where the time goes in v5:
time: 154 us; the launch traced here: 153 us
  waiting for transfers between devices  78.2 us (51%)
  starting transfers between devices  52.2 us (34%)
  Pallas kernels  16.4 us (11%)
  other arithmetic  4.05 us (3%)
    ppermute x4, waiting for transfers between devices, fetch(): lax.ppermute(block, axis, [(partner(i), i) for i in range(lax.axis_size(a...  46.2 us
    ppermute x3, waiting for transfers between devices, fetch_next(): return lax.ppermute(block, ('dp', 'expert'), pairs)  18.1 us
    ppermute x3, starting transfers between devices, fetch_next(): return lax.ppermute(block, ('dp', 'expert'), pairs)  15.4 us
    ppermute x4, starting transfers between devices, fetch(): lax.ppermute(block, axis, [(partner(i), i) for i in range(lax.axis_size(a...  13.9 us
    all_to_all x1, starting transfers between devices, exchange(): lax.all_to_all(blocks, 'expert', split_axis=0, concat_axis=0, tiled=True)  11.6 us
    all_to_all x1, starting transfers between devices, body(): lax.all_to_all(crossing, 'expert', split_axis=0, concat_axis=0, tiled=True)  11.3 us
    all_to_all x1, waiting for transfers between devices, exchange(): lax.all_to_all(blocks, 'expert', split_axis=0, concat_axis=0, tiled=True)  8.57 us
    pallas_call x1, Pallas kernels, project(): pl.pallas_call(kernel, out_shape=(jax.ShapeDtypeStruct((slots, units), jn...  8.5 us
  transfers between devices with their start and end apart: 9, of which 7 were waited for; matrix products, arithmetic and copies ran while one was open for 3% of the time, Pallas kernels for 4%

profile of v5, /device:TPU:1, one launch (start us, length us, event | category | flops | bytes accessed | tf_op | source)
XLA Modules:
  0.0 152.9 jit_solution(12879119376198064048)
XLA Ops:
  0.6 6.7 %collective-permute-start = (bf16[1,768,256]{2,1,0:T(8,128)(2,1)}, bf16[1,768,256]{2,1,0:T(8,128)(2,1)S(1)}, u32[]{:S(2)}, u32[]{:S(2)}) collective-permute-start(bf16[1,768,256]{2,1,0:T(8,128)(2,1)} %param.11), channel_id=1, source_target_pairs={{128,0},{132,4},{392,8},{396,12},{144,16},{148,20},{408,24},{412,2... | collective-permute-start | bytes 1179656 | tf_op jit(solution)/shard_map/ppermute | solution.py:240
  7.4 5.1 %head.1 = (bf16[512,4096]{1,0:T(8,128)(2,1)}, f32[32,16]{1,0:T(8,128)}, f32[32,128]{1,0:T(8,128)}) custom-call(s32[8,128]{1,0:T(8,128)} %bitcast.21, bf16[8,128]{1,0:T(8,128)(2,1)} %bitcast.25, bf16[128,4096]{1,0:T(8,128)(2,1)} %refs_2_.1), custom_call_target="tpu_custom_call" | custom-call | tf_op jit(solution)/shard_map/head/pallas_call | solution.py:73
  12.4 0.0 copy-start.9
  12.5 11.6 %all-to-all-start = ((bf16[32,16,4096]{2,1,0:T(8,128)(2,1)}), bf16[32,16,4096]{2,1,0:T(8,128)(2,1)}, u32[]{:S(2)}, u32[]{:S(2)}) async-start(bf16[32,16,4096]{2,1,0:T(8,128)(2,1)} %bitcast.23), calls=%async_computation | async-start | bytes 8388608 | tf_op jit(solution)/shard_map/all_to_all | solution.py:258
  24.1 0.0 collective-permute-done
  24.1 3.8 %collective-permute-start.1 = (bf16[1,768,256]{2,1,0:T(8,128)(2,1)S(1)}, bf16[1,768,256]{2,1,0:T(8,128)(2,1)S(1)}, u32[]{:S(2)}, u32[]{:S(2)}) collective-permute-start(bf16[1,768,256]{2,1,0:T(8,128)(2,1)S(1)} %collective-permute-done), channel_id=1, source_target_pairs={{128,0},{132,4},{392,8},{396,12},{144,16},{148,20},{408,24},{412,2... | collective-permute-start | bytes 1179656 | tf_op jit(solution)/shard_map/ppermute | solution.py:240
  27.9 9.6 %collective-permute-done.1 = bf16[1,768,256]{2,1,0:T(8,128)(2,1)S(1)} collective-permute-done((bf16[1,768,256]{2,1,0:T(8,128)(2,1)S(1)}, bf16[1,768,256]{2,1,0:T(8,128)(2,1)S(1)}, u32[]{:S(2)}, u32[]{:S(2)}) %collective-permute-start.1) | collective-permute-done | bytes 393248 | tf_op jit(solution)/shard_map/ppermute | solution.py:240
  37.4 5.0 %collective-permute-start.2 = (bf16[1,768,256]{2,1,0:T(8,128)(2,1)S(1)}, bf16[1,768,256]{2,1,0:T(8,128)(2,1)S(1)}, u32[]{:S(2)}, u32[]{:S(2)}) collective-permute-start(bf16[1,768,256]{2,1,0:T(8,128)(2,1)S(1)} %collective-permute-done.1), channel_id=1, source_target_pairs={{128,0},{132,4},{392,8},{396,12},{144,16},{148,20},{408,24},{412,2... | collective-permute-start | bytes 1179656 | tf_op jit(solution)/shard_map/ppermute | solution.py:240
  42.4 0.0 copy-done.9
  42.5 8.6 %collective-permute-done.2 = bf16[1,768,256]{2,1,0:T(8,128)(2,1)S(1)} collective-permute-done((bf16[1,768,256]{2,1,0:T(8,128)(2,1)S(1)}, bf16[1,768,256]{2,1,0:T(8,128)(2,1)S(1)}, u32[]{:S(2)}, u32[]{:S(2)}) %collective-permute-start.2) | collective-permute-done | bytes 393248 | tf_op jit(solution)/shard_map/ppermute | solution.py:240
  51.1 0.0 copy-start.6
  51.1 0.0 copy-start.4
  51.1 0.0 copy-start.5
  51.1 4.7 %collective-permute-start.3 = (bf16[4,768,256]{2,1,0:T(8,128)(2,1)S(1)}, bf16[4,768,256]{2,1,0:T(8,128)(2,1)S(1)}, u32[]{:S(2)}, u32[]{:S(2)}) collective-permute-start(bf16[4,768,256]{2,1,0:T(8,128)(2,1)S(1)} %constant_dynamic-update-slice_fusion.refs_1_), channel_id=1, source_target_pairs={{1,0},{2,1},{3,2},{0,3},{5,4},{6,5},{7,6},{4,7},{9,8},{10,9},{11,1... | collective-permute-start | bytes 4718600 | tf_op jit(solution)/shard_map/ppermute | solution.py:230
  55.8 1.9 %collective-permute-start.5 = (bf16[4,768,256]{2,1,0:T(8,128)(2,1)S(1)}, bf16[4,768,256]{2,1,0:T(8,128)(2,1)S(1)}, u32[]{:S(2)}, u32[]{:S(2)}) collective-permute-start(bf16[4,768,256]{2,1,0:T(8,128)(2,1)S(1)} %constant_dynamic-update-slice_fusion.refs_1_), channel_id=1, source_target_pairs={{3,0},{0,1},{1,2},{2,3},{7,4},{4,5},{5,6},{6,7},{11,8},{8,9},{9,10... | collective-permute-start | bytes 4718600 | tf_op jit(solution)/shard_map/ppermute | solution.py:230
  57.7 30.1 %collective-permute-done.3.refs_1_.refs_2_ = bf16[4,768,256]{2,1,0:T(8,128)(2,1)S(1)} collective-permute-done((bf16[4,768,256]{2,1,0:T(8,128)(2,1)S(1)}, bf16[4,768,256]{2,1,0:T(8,128)(2,1)S(1)}, u32[]{:S(2)}, u32[]{:S(2)}) %collective-permute-start.3) | collective-permute-done | bytes 1572896 | tf_op jit(solution)/shard_map/ppermute | solution.py:230
  87.9 0.0 copy-start.2
  87.9 0.1 slice.8
  87.9 5.4 %collective-permute-start.4 = (bf16[2,768,256]{2,1,0:T(8,128)(2,1)S(1)}, bf16[2,768,256]{2,1,0:T(8,128)(2,1)S(1)}, u32[]{:S(2)}, u32[]{:S(2)}) collective-permute-start(bf16[2,768,256]{2,1,0:T(8,128)(2,1)S(1)} %slice.8), channel_id=1, source_target_pairs={{1,0},{2,1},{3,2},{0,3},{5,4},{6,5},{7,6},{4,7},{9,8},{10,9},{11,1... | collective-permute-start | bytes 2359304 | tf_op jit(solution)/shard_map/ppermute | solution.py:230
  93.3 0.0 collective-permute-done.5.refs_2_.refs_5_
  93.4 0.0 copy-start.3
  93.4 0.1 slice.9
  93.4 0.0 copy-done.6
  93.4 0.0 copy-done.2
  93.4 1.9 %collective-permute-start.6 = (bf16[2,768,256]{2,1,0:T(8,128)(2,1)S(1)}, bf16[2,768,256]{2,1,0:T(8,128)(2,1)S(1)}, u32[]{:S(2)}, u32[]{:S(2)}) collective-permute-start(bf16[2,768,256]{2,1,0:T(8,128)(2,1)S(1)} %slice.9), channel_id=1, source_target_pairs={{3,0},{0,1},{1,2},{2,3},{7,4},{4,5},{5,6},{6,7},{11,8},{8,9},{9,10... | collective-permute-start | bytes 2359304 | tf_op jit(solution)/shard_map/ppermute | solution.py:230
  95.4 0.0 copy-done.4
  95.4 0.0 copy-done.5
  95.4 1.5 fusion.refs_6_
  96.9 0.0 copy-done.3
  96.9 10.9 %collective-permute-done.4.first.refs_3_ = bf16[2,768,256]{2,1,0:T(8,128)(2,1)S(1)} collective-permute-done((bf16[2,768,256]{2,1,0:T(8,128)(2,1)S(1)}, bf16[2,768,256]{2,1,0:T(8,128)(2,1)S(1)}, u32[]{:S(2)}, u32[]{:S(2)}) %collective-permute-start.4) | collective-permute-done | bytes 786464 | tf_op jit(solution)/shard_map/ppermute | solution.py:230
  107.7 0.0 copy-start.7
  107.7 5.3 %collective-permute-done.6.refs_0_.refs_4_ = bf16[2,768,256]{2,1,0:T(8,128)(2,1)S(1)} collective-permute-done((bf16[2,768,256]{2,1,0:T(8,128)(2,1)S(1)}, bf16[2,768,256]{2,1,0:T(8,128)(2,1)S(1)}, u32[]{:S(2)}, u32[]{:S(2)}) %collective-permute-start.6) | collective-permute-done | bytes 786464 | tf_op jit(solution)/shard_map/ppermute | solution.py:230
  113.0 0.0 copy-done.7
  113.0 0.0 copy-start.8
  113.0 0.9 copy-done.8
  113.9 1.3 arrived.1.refs_8_
  115.2 8.6 %all-to-all-done = bf16[32,16,4096]{2,1,0:T(8,128)(2,1)} async-done(((bf16[32,16,4096]{2,1,0:T(8,128)(2,1)}), bf16[32,16,4096]{2,1,0:T(8,128)(2,1)}, u32[]{:S(2)}, u32[]{:S(2)}) %all-to-all-start) | async-done | bytes 4194336 | tf_op jit(solution)/shard_map/all_to_all | solution.py:258
  123.7 8.5 %project.1 = (f32[512,768]{1,0:T(8,128)}, f32[32,32]{1,0:T(8,128)}) custom-call(bf16[512,4096]{1,0:T(8,128)(2,1)} %bitcast.3.refs_0_, bf16[4,768,256]{2,1,0:T(8,128)(2,1)} %copy-done.6, bf16[4,768,256]{2,1,0:T(8,128)(2,1)} %copy-done.2, bf16[2,768,256]{2,1,0:T(8,128)(2,1)} %copy-done.7, bf16[2,768,256]{2,1,0:T(8,128)(2,1)} %copy-done.8, ...), custom_call_target="tpu_custom_call" | custom-call | tf_op jit(solution)/shard_map/project/pallas_call | solution.py:171
  132.2 11.3 %all-to-all-start.1 = ((f32[32,1,32]{2,1,0:T(1,128)}), f32[32,1,32]{2,1,0:T(1,128)S(1)}, u32[]{:S(2)}, u32[]{:S(2)}) async-start(f32[32,1,32]{2,1,0:T(1,128)} %bitcast.24), calls=%async_computation.1 | async-start | bytes 32768 | tf_op jit(solution)/shard_map/all_to_all | solution.py:278
  143.5 0.0 copy-start
  143.5 0.0 copy-start.1
  143.6 2.6 %fusion.7 = (f32[512,768]{1,0:T(8,128)S(1)}, f32[512,768]{1,0:T(8,128)S(1)}) fusion(f32[512,768]{1,0:T(8,128)} %get-tuple-element.15, bf16[1,1,1,32,16,768]{5,4,3,2,1,0:T(8,128)(2,1)} %param.9, bf16[1,1,1,32,16,768]{5,4,3,2,1,0:T(8,128)(2,1)} %param.10), kind=kLoop, calls=%fused_computation.13 | loop fusion | flops 5111808 | bytes 6291456 | tf_op jit(solution)/shard_map/mul | solution.py:280
  146.1 5.2 %all-to-all-done.1 = f32[32,1,32]{2,1,0:T(1,128)S(1)} async-done(((f32[32,1,32]{2,1,0:T(1,128)}), f32[32,1,32]{2,1,0:T(1,128)S(1)}, u32[]{:S(2)}, u32[]{:S(2)}) %all-to-all-start.1) | async-done | bytes 4128 | tf_op jit(solution)/shard_map/all_to_all | solution.py:278
  151.4 0.0 copy-done
  151.4 0.0 copy-done.1
  151.4 1.6 %finish.1 = (bf16[512,768]{1,0:T(8,128)(2,1)}, bf16[512,768]{1,0:T(8,128)(2,1)}, f32[8,128]{1,0:T(8,128)}) custom-call(s32[8,128]{1,0:T(8,128)S(1)} %bitcast.22, f32[32,128]{1,0:T(8,128)S(1)} %copy-done, f32[32,32]{1,0:T(8,128)S(1)} %bitcast.20, f32[512,768]{1,0:T(8,128)S(1)} %get-tuple-element.20.gate_ref, f32[512,768]{1,0:T(8,128)S(1)} %get-tuple-element.19.up_ref), custom_call_target="tpu_custom_call" | custom-call | tf_op jit(solution)/shard_map/finish/pallas_call | solution.py:221
  (4 shorter events, 0.1 us)
Async XLA Ops:
  0.6 23.5 %collective-permute-start = (bf16[1,768,256]{2,1,0:T(8,128)(2,1)}, bf16[1,768,256]{2,1,0:T(8,128)(2,1)S(1)}, u32[]{:S(2)}, u32[]{:S(2)}) collective-permute-start(bf16[1,768,256]{2,1,0:T(8,128)(2,1)} %param.11), channel_id=1, source_target_pairs={{128,0},{132,4},{392,8},{396,12},{144,16},{148,20},{408,24},{412,2... | collective-permute-start | bytes 1179656 | tf_op jit(solution)/shard_map/ppermute | solution.py:240
  12.4 30.0 %copy-start.9 = (bf16[1,768,256]{2,1,0:T(8,128)(2,1)S(1)}, bf16[1,768,256]{2,1,0:T(8,128)(2,1)}, u32[]{:S(2)}) copy-start(bf16[1,768,256]{2,1,0:T(8,128)(2,1)} %param.11) | copy-start | bytes 1179652
  12.5 111.3 %all-to-all-start = ((bf16[32,16,4096]{2,1,0:T(8,128)(2,1)}), bf16[32,16,4096]{2,1,0:T(8,128)(2,1)}, u32[]{:S(2)}, u32[]{:S(2)}) async-start(bf16[32,16,4096]{2,1,0:T(8,128)(2,1)} %bitcast.23), calls=%async_computation | async-start | bytes 8388608 | tf_op jit(solution)/shard_map/all_to_all | solution.py:258
  24.1 13.3 %collective-permute-start.1 = (bf16[1,768,256]{2,1,0:T(8,128)(2,1)S(1)}, bf16[1,768,256]{2,1,0:T(8,128)(2,1)S(1)}, u32[]{:S(2)}, u32[]{:S(2)}) collective-permute-start(bf16[1,768,256]{2,1,0:T(8,128)(2,1)S(1)} %collective-permute-done), channel_id=1, source_target_pairs={{128,0},{132,4},{392,8},{396,12},{144,16},{148,20},{408,24},{412,2... | collective-permute-start | bytes 1179656 | tf_op jit(solution)/shard_map/ppermute | solution.py:240
  37.4 13.6 %collective-permute-start.2 = (bf16[1,768,256]{2,1,0:T(8,128)(2,1)S(1)}, bf16[1,768,256]{2,1,0:T(8,128)(2,1)S(1)}, u32[]{:S(2)}, u32[]{:S(2)}) collective-permute-start(bf16[1,768,256]{2,1,0:T(8,128)(2,1)S(1)} %collective-permute-done.1), channel_id=1, source_target_pairs={{128,0},{132,4},{392,8},{396,12},{144,16},{148,20},{408,24},{412,2... | collective-permute-start | bytes 1179656 | tf_op jit(solution)/shard_map/ppermute | solution.py:240
  51.1 42.3 %copy-start.6 = (bf16[4,768,256]{2,1,0:T(8,128)(2,1)}, bf16[4,768,256]{2,1,0:T(8,128)(2,1)S(1)}, u32[]{:S(2)}) copy-start(bf16[4,768,256]{2,1,0:T(8,128)(2,1)S(1)} %constant_dynamic-update-slice_fusion.refs_1_) | copy-start | bytes 4718596
  51.1 44.3 %copy-start.4 = (bf16[1,1,1,32,16,768]{5,4,3,2,1,0:T(8,128)(2,1)S(1)}, bf16[1,1,1,32,16,768]{5,4,3,2,1,0:T(8,128)(2,1)}, u32[]{:S(2)}) copy-start(bf16[1,1,1,32,16,768]{5,4,3,2,1,0:T(8,128)(2,1)} %param.10) | copy-start | bytes 2359300
  51.1 44.3 %copy-start.5 = (bf16[1,1,1,32,16,768]{5,4,3,2,1,0:T(8,128)(2,1)S(1)}, bf16[1,1,1,32,16,768]{5,4,3,2,1,0:T(8,128)(2,1)}, u32[]{:S(2)}) copy-start(bf16[1,1,1,32,16,768]{5,4,3,2,1,0:T(8,128)(2,1)} %param.9) | copy-start | bytes 2359300
  51.1 36.7 %collective-permute-start.3 = (bf16[4,768,256]{2,1,0:T(8,128)(2,1)S(1)}, bf16[4,768,256]{2,1,0:T(8,128)(2,1)S(1)}, u32[]{:S(2)}, u32[]{:S(2)}) collective-permute-start(bf16[4,768,256]{2,1,0:T(8,128)(2,1)S(1)} %constant_dynamic-update-slice_fusion.refs_1_), channel_id=1, source_target_pairs={{1,0},{2,1},{3,2},{0,3},{5,4},{6,5},{7,6},{4,7},{9,8},{10,9},{11,1... | collective-permute-start | bytes 4718600 | tf_op jit(solution)/shard_map/ppermute | solution.py:230
  55.8 37.6 %collective-permute-start.5 = (bf16[4,768,256]{2,1,0:T(8,128)(2,1)S(1)}, bf16[4,768,256]{2,1,0:T(8,128)(2,1)S(1)}, u32[]{:S(2)}, u32[]{:S(2)}) collective-permute-start(bf16[4,768,256]{2,1,0:T(8,128)(2,1)S(1)} %constant_dynamic-update-slice_fusion.refs_1_), channel_id=1, source_target_pairs={{3,0},{0,1},{1,2},{2,3},{7,4},{4,5},{5,6},{6,7},{11,8},{8,9},{9,10... | collective-permute-start | bytes 4718600 | tf_op jit(solution)/shard_map/ppermute | solution.py:230
  87.9 5.6 %copy-start.2 = (bf16[4,768,256]{2,1,0:T(8,128)(2,1)}, bf16[4,768,256]{2,1,0:T(8,128)(2,1)S(1)}, u32[]{:S(2)}) copy-start(bf16[4,768,256]{2,1,0:T(8,128)(2,1)S(1)} %collective-permute-done.3.refs_1_.refs_2_) | copy-start | bytes 4718596
  87.9 19.8 %collective-permute-start.4 = (bf16[2,768,256]{2,1,0:T(8,128)(2,1)S(1)}, bf16[2,768,256]{2,1,0:T(8,128)(2,1)S(1)}, u32[]{:S(2)}, u32[]{:S(2)}) collective-permute-start(bf16[2,768,256]{2,1,0:T(8,128)(2,1)S(1)} %slice.8), channel_id=1, source_target_pairs={{1,0},{2,1},{3,2},{0,3},{5,4},{6,5},{7,6},{4,7},{9,8},{10,9},{11,1... | collective-permute-start | bytes 2359304 | tf_op jit(solution)/shard_map/ppermute | solution.py:230
  93.4 3.5 %copy-start.3 = (bf16[4,768,256]{2,1,0:T(8,128)(2,1)}, bf16[4,768,256]{2,1,0:T(8,128)(2,1)S(1)}, u32[]{:S(2)}) copy-start(bf16[4,768,256]{2,1,0:T(8,128)(2,1)S(1)} %collective-permute-done.5.refs_2_.refs_5_) | copy-start | bytes 4718596
  93.4 19.5 %collective-permute-start.6 = (bf16[2,768,256]{2,1,0:T(8,128)(2,1)S(1)}, bf16[2,768,256]{2,1,0:T(8,128)(2,1)S(1)}, u32[]{:S(2)}, u32[]{:S(2)}) collective-permute-start(bf16[2,768,256]{2,1,0:T(8,128)(2,1)S(1)} %slice.9), channel_id=1, source_target_pairs={{3,0},{0,1},{1,2},{2,3},{7,4},{4,5},{5,6},{6,7},{11,8},{8,9},{9,10... | collective-permute-start | bytes 2359304 | tf_op jit(solution)/shard_map/ppermute | solution.py:230
  107.7 5.3 %copy-start.7 = (bf16[2,768,256]{2,1,0:T(8,128)(2,1)}, bf16[2,768,256]{2,1,0:T(8,128)(2,1)S(1)}, u32[]{:S(2)}) copy-start(bf16[2,768,256]{2,1,0:T(8,128)(2,1)S(1)} %collective-permute-done.4.first.refs_3_) | copy-start | bytes 2359300
  113.0 0.9 copy-start.8
  132.2 19.1 %all-to-all-start.1 = ((f32[32,1,32]{2,1,0:T(1,128)}), f32[32,1,32]{2,1,0:T(1,128)S(1)}, u32[]{:S(2)}, u32[]{:S(2)}) async-start(f32[32,1,32]{2,1,0:T(1,128)} %bitcast.24), calls=%async_computation.1 | async-start | bytes 32768 | tf_op jit(solution)/shard_map/all_to_all | solution.py:278
  143.5 7.8 %copy-start = (f32[32,128]{1,0:T(8,128)S(1)}, f32[32,128]{1,0:T(8,128)}, u32[]{:S(2)}) copy-start(f32[32,128]{1,0:T(8,128)} %get-tuple-element.11.slot_ref) | copy-start | bytes 49156
  143.5 7.8 %copy-start.1 = (s32[128,8]{0,1:T(8,128)S(1)}, s32[128,8]{0,1:T(8,128)}, u32[]{:S(2)}) copy-start(s32[128,8]{0,1:T(8,128)} %param.7) | copy-start | bytes 12292

commit v6 on v5

--- a/solution.py
+++ b/solution.py
@@ -90,26 +90,8 @@
     )(routes.T, route_weight.T, grad_out)
 
 
-def arrived(groups):
-    def kernel(first, *refs):
-        *_, out_ref, sem = refs
-        copy = pltpu.make_async_copy(first.at[0, pl.ds(0, 16), pl.ds(0, 128)], out_ref, sem)
-        copy.start()
-        copy.wait()
-
-    return pl.pallas_call(
-        kernel,
-        out_shape=jax.ShapeDtypeStruct((16, 128), groups[0].dtype),
-        in_specs=[HBM] * len(groups),
-        scratch_shapes=[pltpu.SemaphoreType.DMA],
-        cost_estimate=pl.CostEstimate(flops=int(5e10), bytes_accessed=4096, transcendentals=0),
-        compiler_params=pltpu.CompilerParams(vmem_limit_bytes=VMEM),
-        name="arrived",
-    )(*groups)
-
-
 def project_kernel(cap, counts, received_hbm, *refs):
-    *blocks, hidden_hbm, slot_weight_ref, _, back_hbm, crossing_ref, rows, weight, hidden, back, sems = refs
+    *blocks, hidden_hbm, slot_weight_ref, back_hbm, crossing_ref, rows, weight, hidden, back, sems = refs
     first = blocks[0]
     depth = first.shape[2]
     slots, units = hidden.shape
@@ -157,10 +139,11 @@
     store.wait()
 
 
-def project(received, groups, hidden, slot_weight, tile):
+def project(received, groups, hidden, slot_weight):
     slots, units = hidden.shape
     ranks, cap = slot_weight.shape
-    count, _, depth = groups[0][0].shape
+    depth = groups[0][0].shape[2]
+    count = sum(block.shape[0] for block in groups[0])
     counts = [len(group) for group in groups]
     blocks = [block for group in groups for block in group]
 
@@ -174,7 +157,7 @@
             jax.ShapeDtypeStruct((slots, units), jnp.float32),
             jax.ShapeDtypeStruct((ranks, 2 * cap), jnp.float32),
         ),
-        in_specs=[HBM] * (len(blocks) + 2) + [whole, whole],
+        in_specs=[HBM] * (len(blocks) + 2) + [whole],
         out_specs=(HBM, whole),
         scratch_shapes=[
             pltpu.VMEM((len(groups), slots, count * depth), jnp.bfloat16),
@@ -185,7 +168,7 @@
         ],
         compiler_params=pltpu.CompilerParams(vmem_limit_bytes=VMEM),
         name="project",
-    )(received, *blocks, hidden, slot_weight, tile)
+    )(received, *blocks, hidden, slot_weight)
 
 
 def finish_kernel(routes_ref, slot_ref, crossing_ref, gate_ref, up_ref, grad_gate_ref, grad_up_ref, out_ref):
@@ -242,15 +225,21 @@
 
 def gather_weight(own):
     size = lax.axis_size("context")
-    blocks = [own]
-    for _ in range(lax.axis_size("dp") - 1):
-        blocks.append(fetch_next(blocks[-1]))
-    over_dp = jnp.concatenate(blocks)
-    after = fetch(over_dp, "context", lambda i: (i + 1) % size)
-    before = fetch(over_dp, "context", lambda i: (i - 1) % size)
-    low = fetch(after[:2], "context", lambda i: (i + 1) % size)
-    high = fetch(before[2:], "context", lambda i: (i - 1) % size)
-    return [over_dp, after, (low, high), before]
+
+    def after(block):
+        return fetch(block, "context", lambda i: (i + 1) % size)
+
+    def before(block):
+        return fetch(block, "context", lambda i: (i - 1) % size)
+
+    one = fetch_next(own)
+    two = fetch_next(one)
+    near = jnp.concatenate([own, one])
+    near_after, near_before = after(near), before(near)
+    far = jnp.concatenate([two, fetch_next(two)])
+    far, near_after, near_before = lax.optimization_barrier((far, near_after, near_before))
+    far_after, far_before = after(far), before(far)
+    return [(near, far), (near_after, far_after), (after(near_after), before(far_before)), (near_before, far_before)]
 
 
 def exchange(rows, ranks):
@@ -267,14 +256,12 @@
     sent, slot_weight, slot = head(routes, route_weight, grad_out, ranks, cap, n_dp, n_context)
     received = exchange(sent, ranks)
     groups = gather_weight(down_weight)
-    groups = [group if isinstance(group, tuple) else (group,) for group in groups]
-    tile = arrived([*groups[2], groups[1][0], groups[3][0]])
 
     gate = saved_gate.reshape(slots, units).astype(jnp.float32)
     up = saved_up.reshape(slots, units).astype(jnp.float32)
     sigma = jax.nn.sigmoid(gate)
     hidden = lax.optimization_barrier((gate * sigma * up).astype(jnp.bfloat16))
-    back, crossing = project(received, groups, hidden, slot_weight, tile)
+    back, crossing = project(received, groups, hidden, slot_weight)
     crossing = lax.all_to_all(crossing, "expert", split_axis=0, concat_axis=0, tiled=True)
     by_gate = back * up * sigma * (1.0 + gate * (1.0 - sigma))
     by_up = back * gate * sigma

time: 154 us -> 147 us (0.955)
  waiting for transfers between devices: 78.2 us -> 68.2 us
  starting transfers between devices: 52.2 us -> 56.5 us
    ppermute x4 -> x6, waiting for transfers between devices: 46.2 us -> 30.6 us  [fetch(): lax.ppermute(block, axis, [(partner(i), i) for i in range(lax.axis_size(a...]
    all_to_all x1, waiting for transfers between devices: 8.57 us -> 15.9 us  [exchange(): lax.all_to_all(blocks, 'expert', split_axis=0, concat_axis=0, tiled=True)]
    ppermute x4 -> x6, starting transfers between devices: 13.9 us -> 16.6 us  [fetch(): lax.ppermute(block, axis, [(partner(i), i) for i in range(lax.axis_size(a...]
    all_to_all x1, starting transfers between devices: 11.3 us -> 9.62 us  [body(): lax.all_to_all(crossing, 'expert', split_axis=0, concat_axis=0, tiled=True)]
    ppermute x3, waiting for transfers between devices: 18.1 us -> 16.5 us  [fetch_next(): return lax.ppermute(block, ('dp', 'expert'), pairs)]
    ppermute x3, starting transfers between devices: 15.4 us -> 17.1 us  [fetch_next(): return lax.ppermute(block, ('dp', 'expert'), pairs)]
    all_to_all x1, starting transfers between devices: 11.6 us -> 13.2 us  [exchange(): lax.all_to_all(blocks, 'expert', split_axis=0, concat_axis=0, tiled=True)]
  transfers between devices with their start and end apart: 9 -> 11, of which waited for: 7 -> 9; matrix products, arithmetic and copies ran while one was open for 3% -> 3% of each run, Pallas kernels for 4% -> 0%
where the time goes in v6:
time: 147 us; the launch traced here: 146 us
  waiting for transfers between devices  68.2 us (46%)
  starting transfers between devices  56.5 us (38%)
  Pallas kernels  15.2 us (10%)
  other arithmetic  4.12 us (3%)
    ppermute x6, waiting for transfers between devices, fetch(): lax.ppermute(block, axis, [(partner(i), i) for i in range(lax.axis_size(a...  30.6 us
    ppermute x3, starting transfers between devices, fetch_next(): return lax.ppermute(block, ('dp', 'expert'), pairs)  17.1 us
    ppermute x6, starting transfers between devices, fetch(): lax.ppermute(block, axis, [(partner(i), i) for i in range(lax.axis_size(a...  16.6 us
    ppermute x3, waiting for transfers between devices, fetch_next(): return lax.ppermute(block, ('dp', 'expert'), pairs)  16.5 us
    all_to_all x1, waiting for transfers between devices, exchange(): lax.all_to_all(blocks, 'expert', split_axis=0, concat_axis=0, tiled=True)  15.9 us
    all_to_all x1, starting transfers between devices, exchange(): lax.all_to_all(blocks, 'expert', split_axis=0, concat_axis=0, tiled=True)  13.2 us
    all_to_all x1, starting transfers between devices, body(): lax.all_to_all(crossing, 'expert', split_axis=0, concat_axis=0, tiled=True)  9.62 us
    pallas_call x1, Pallas kernels, project(): pl.pallas_call(kernel, out_shape=(jax.ShapeDtypeStruct((slots, units), jn...  8.51 us
  transfers between devices with their start and end apart: 11, of which 9 were waited for; matrix products, arithmetic and copies ran while one was open for 3% of the time, Pallas kernels for 0%

profile of v6, /device:TPU:1, one launch (start us, length us, event | category | flops | bytes accessed | tf_op | source)
XLA Modules:
  0.0 145.9 jit_solution(2473079663357449776)
XLA Ops:
  0.6 5.1 %head.1 = (bf16[512,4096]{1,0:T(8,128)(2,1)}, f32[32,16]{1,0:T(8,128)}, f32[32,128]{1,0:T(8,128)}) custom-call(s32[8,128]{1,0:T(8,128)} %bitcast.21, bf16[8,128]{1,0:T(8,128)(2,1)} %bitcast.25, bf16[128,4096]{1,0:T(8,128)(2,1)} %refs_2_.1), custom_call_target="tpu_custom_call" | custom-call | tf_op jit(solution)/shard_map/head/pallas_call | solution.py:73
  5.7 0.0 copy-start.11
  5.8 13.2 %all-to-all-start = ((bf16[32,16,4096]{2,1,0:T(8,128)(2,1)}), bf16[32,16,4096]{2,1,0:T(8,128)(2,1)}, u32[]{:S(2)}, u32[]{:S(2)}) async-start(bf16[32,16,4096]{2,1,0:T(8,128)(2,1)} %bitcast.23), calls=%async_computation | async-start | bytes 8388608 | tf_op jit(solution)/shard_map/all_to_all | solution.py:247
  19.0 0.0 copy-done.11
  19.0 0.0 copy-start.2
  19.0 0.0 copy-start.3
  19.0 5.1 %collective-permute-start = (bf16[1,768,256]{2,1,0:T(8,128)(2,1)S(1)}, bf16[1,768,256]{2,1,0:T(8,128)(2,1)S(1)}, u32[]{:S(2)}, u32[]{:S(2)}) collective-permute-start(bf16[1,768,256]{2,1,0:T(8,128)(2,1)S(1)} %copy-done.11), channel_id=1, source_target_pairs={{128,0},{132,4},{392,8},{396,12},{144,16},{148,20},{408,24},{412,2... | collective-permute-start | bytes 1179656 | tf_op jit(solution)/shard_map/ppermute | solution.py:223
  24.1 8.3 %collective-permute-done = bf16[1,768,256]{2,1,0:T(8,128)(2,1)S(1)} collective-permute-done((bf16[1,768,256]{2,1,0:T(8,128)(2,1)S(1)}, bf16[1,768,256]{2,1,0:T(8,128)(2,1)S(1)}, u32[]{:S(2)}, u32[]{:S(2)}) %collective-permute-start) | collective-permute-done | bytes 393248 | tf_op jit(solution)/shard_map/ppermute | solution.py:223
  32.5 6.2 %collective-permute-start.1 = (bf16[1,768,256]{2,1,0:T(8,128)(2,1)S(1)}, bf16[1,768,256]{2,1,0:T(8,128)(2,1)S(1)}, u32[]{:S(2)}, u32[]{:S(2)}) collective-permute-start(bf16[1,768,256]{2,1,0:T(8,128)(2,1)S(1)} %collective-permute-done), channel_id=1, source_target_pairs={{128,0},{132,4},{392,8},{396,12},{144,16},{148,20},{408,24},{412,2... | collective-permute-start | bytes 1179656 | tf_op jit(solution)/shard_map/ppermute | solution.py:223
  38.7 0.0 copy-start.5
  38.7 4.4 %collective-permute-start.3 = (bf16[2,768,256]{2,1,0:T(8,128)(2,1)S(1)}, bf16[2,768,256]{2,1,0:T(8,128)(2,1)S(1)}, u32[]{:S(2)}, u32[]{:S(2)}) collective-permute-start(bf16[2,768,256]{2,1,0:T(8,128)(2,1)S(1)} %constant_dynamic-update-slice_fusion.refs_1_), channel_id=1, source_target_pairs={{1,0},{2,1},{3,2},{0,3},{5,4},{6,5},{7,6},{4,7},{9,8},{10,9},{11,1... | collective-permute-start | bytes 2359304 | tf_op jit(solution)/shard_map/ppermute | solution.py:213
  43.1 1.9 %collective-permute-start.4 = (bf16[2,768,256]{2,1,0:T(8,128)(2,1)S(1)}, bf16[2,768,256]{2,1,0:T(8,128)(2,1)S(1)}, u32[]{:S(2)}, u32[]{:S(2)}) collective-permute-start(bf16[2,768,256]{2,1,0:T(8,128)(2,1)S(1)} %constant_dynamic-update-slice_fusion.refs_1_), channel_id=1, source_target_pairs={{3,0},{0,1},{1,2},{2,3},{7,4},{4,5},{5,6},{6,7},{11,8},{8,9},{9,10... | collective-permute-start | bytes 2359304 | tf_op jit(solution)/shard_map/ppermute | solution.py:213
  45.1 1.4 collective-permute-done.1
  46.4 5.8 %collective-permute-start.2 = (bf16[1,768,256]{2,1,0:T(8,128)(2,1)S(1)}, bf16[1,768,256]{2,1,0:T(8,128)(2,1)S(1)}, u32[]{:S(2)}, u32[]{:S(2)}) collective-permute-start(bf16[1,768,256]{2,1,0:T(8,128)(2,1)S(1)} %collective-permute-done.1), channel_id=1, source_target_pairs={{128,0},{132,4},{392,8},{396,12},{144,16},{148,20},{408,24},{412,2... | collective-permute-start | bytes 1179656 | tf_op jit(solution)/shard_map/ppermute | solution.py:223
  52.2 6.8 %collective-permute-done.2 = bf16[1,768,256]{2,1,0:T(8,128)(2,1)S(1)} collective-permute-done((bf16[1,768,256]{2,1,0:T(8,128)(2,1)S(1)}, bf16[1,768,256]{2,1,0:T(8,128)(2,1)S(1)}, u32[]{:S(2)}, u32[]{:S(2)}) %collective-permute-start.2) | collective-permute-done | bytes 393248 | tf_op jit(solution)/shard_map/ppermute | solution.py:223
  59.0 0.1 pad_maximum_fusion.refs_2_
  59.0 0.0 copy-start.4
  59.1 0.0 collective-permute-done.3.refs_3_
  59.1 0.0 copy-start.6
  59.1 4.6 %collective-permute-done.4.refs_7_ = bf16[2,768,256]{2,1,0:T(8,128)(2,1)S(1)} collective-permute-done((bf16[2,768,256]{2,1,0:T(8,128)(2,1)S(1)}, bf16[2,768,256]{2,1,0:T(8,128)(2,1)S(1)}, u32[]{:S(2)}, u32[]{:S(2)}) %collective-permute-start.4) | collective-permute-done | bytes 786464 | tf_op jit(solution)/shard_map/ppermute | solution.py:213
  63.7 0.0 copy-start.7
  63.7 1.9 %collective-permute-start.7 = (bf16[2,768,256]{2,1,0:T(8,128)(2,1)S(1)}, bf16[2,768,256]{2,1,0:T(8,128)(2,1)S(1)}, u32[]{:S(2)}, u32[]{:S(2)}) collective-permute-start(bf16[2,768,256]{2,1,0:T(8,128)(2,1)S(1)} %pad_maximum_fusion.refs_2_), channel_id=1, source_target_pairs={{3,0},{0,1},{1,2},{2,3},{7,4},{4,5},{5,6},{6,7},{11,8},{8,9},{9,10... | collective-permute-start | bytes 2359304 | tf_op jit(solution)/shard_map/ppermute | solution.py:213
  65.6 4.6 %collective-permute-start.5 = (bf16[2,768,256]{2,1,0:T(8,128)(2,1)S(1)}, bf16[2,768,256]{2,1,0:T(8,128)(2,1)S(1)}, u32[]{:S(2)}, u32[]{:S(2)}) collective-permute-start(bf16[2,768,256]{2,1,0:T(8,128)(2,1)S(1)} %pad_maximum_fusion.refs_2_), channel_id=1, source_target_pairs={{1,0},{2,1},{3,2},{0,3},{5,4},{6,5},{7,6},{4,7},{9,8},{10,9},{11,1... | collective-permute-start | bytes 2359304 | tf_op jit(solution)/shard_map/ppermute | solution.py:213
  70.2 1.9 %collective-permute-start.6 = (bf16[2,768,256]{2,1,0:T(8,128)(2,1)S(1)}, bf16[2,768,256]{2,1,0:T(8,128)(2,1)S(1)}, u32[]{:S(2)}, u32[]{:S(2)}) collective-permute-start(bf16[2,768,256]{2,1,0:T(8,128)(2,1)S(1)} %collective-permute-done.3.refs_3_), channel_id=1, source_target_pairs={{1,0},{2,1},{3,2},{0,3},{5,4},{6,5},{7,6},{4,7},{9,8},{10,9},{11,1... | collective-permute-start | bytes 2359304 | tf_op jit(solution)/shard_map/ppermute | solution.py:213
  72.1 11.3 %collective-permute-done.7.refs_8_ = bf16[2,768,256]{2,1,0:T(8,128)(2,1)S(1)} collective-permute-done((bf16[2,768,256]{2,1,0:T(8,128)(2,1)S(1)}, bf16[2,768,256]{2,1,0:T(8,128)(2,1)S(1)}, u32[]{:S(2)}, u32[]{:S(2)}) %collective-permute-start.7) | collective-permute-done | bytes 786464 | tf_op jit(solution)/shard_map/ppermute | solution.py:213
  83.5 0.0 copy-start.8
  83.5 1.9 %collective-permute-start.8 = (bf16[2,768,256]{2,1,0:T(8,128)(2,1)S(1)}, bf16[2,768,256]{2,1,0:T(8,128)(2,1)}, u32[]{:S(2)}, u32[]{:S(2)}) collective-permute-start(bf16[2,768,256]{2,1,0:T(8,128)(2,1)S(1)} %collective-permute-done.7.refs_8_), channel_id=1, source_target_pairs={{3,0},{0,1},{1,2},{2,3},{7,4},{4,5},{5,6},{6,7},{11,8},{8,9},{9,10... | collective-permute-start | bytes 2359304 | tf_op jit(solution)/shard_map/ppermute | solution.py:213
  85.4 0.0 copy-done.2
  85.4 0.0 copy-done.3
  85.4 1.5 %fusion.refs_9_ = bf16[512,768]{1,0:T(8,128)(2,1)} fusion(bf16[1,1,1,32,16,768]{5,4,3,2,1,0:T(8,128)(2,1)S(1)} %copy-done.2, bf16[1,1,1,32,16,768]{5,4,3,2,1,0:T(8,128)(2,1)S(1)} %copy-done.3), kind=kLoop, calls=%fused_computation.6 | loop fusion | flops 3145728 | bytes 2359296 | tf_op jit(solution)/shard_map/convert_element_type | solution.py:263
  86.9 0.0 copy-done.5
  86.9 0.0 collective-permute-done.5.refs_4_
  86.9 0.0 copy-start.9
  86.9 14.2 %collective-permute-done.6.refs_5_ = bf16[2,768,256]{2,1,0:T(8,128)(2,1)S(1)} collective-permute-done((bf16[2,768,256]{2,1,0:T(8,128)(2,1)S(1)}, bf16[2,768,256]{2,1,0:T(8,128)(2,1)S(1)}, u32[]{:S(2)}, u32[]{:S(2)}) %collective-permute-start.6) | collective-permute-done | bytes 786464 | tf_op jit(solution)/shard_map/ppermute | solution.py:213
  101.1 0.0 copy-done.9
  101.1 0.0 copy-start.10
  101.1 0.9 copy-done.10
  102.0 0.4 collective-permute-done.8.refs_6_
  102.4 15.9 %all-to-all-done = bf16[32,16,4096]{2,1,0:T(8,128)(2,1)} async-done(((bf16[32,16,4096]{2,1,0:T(8,128)(2,1)}), bf16[32,16,4096]{2,1,0:T(8,128)(2,1)}, u32[]{:S(2)}, u32[]{:S(2)}) %all-to-all-start) | async-done | bytes 4194336 | tf_op jit(solution)/shard_map/all_to_all | solution.py:247
  118.4 0.0 copy-done.4
  118.4 0.0 copy-done.6
  118.4 0.0 copy-done.7
  118.4 0.0 copy-done.8
  118.4 8.5 %project.1 = (f32[512,768]{1,0:T(8,128)}, f32[32,32]{1,0:T(8,128)}) custom-call(bf16[512,4096]{1,0:T(8,128)(2,1)} %bitcast.3.refs_0_, bf16[2,768,256]{2,1,0:T(8,128)(2,1)} %copy-done.5, bf16[2,768,256]{2,1,0:T(8,128)(2,1)} %copy-done.4, bf16[2,768,256]{2,1,0:T(8,128)(2,1)} %copy-done.6, bf16[2,768,256]{2,1,0:T(8,128)(2,1)} %copy-done.9, ...), custom_call_target="tpu_custom_call" | custom-call | tf_op jit(solution)/shard_map/project/pallas_call | solution.py:154
  126.9 9.6 %all-to-all-start.1 = ((f32[32,1,32]{2,1,0:T(1,128)}), f32[32,1,32]{2,1,0:T(1,128)S(1)}, u32[]{:S(2)}, u32[]{:S(2)}) async-start(f32[32,1,32]{2,1,0:T(1,128)} %bitcast.24), calls=%async_computation.1 | async-start | bytes 32768 | tf_op jit(solution)/shard_map/all_to_all | solution.py:265
  136.5 0.0 copy-start
  136.5 0.0 copy-start.1
  136.5 2.6 %fusion.7 = (f32[512,768]{1,0:T(8,128)S(1)}, f32[512,768]{1,0:T(8,128)S(1)}) fusion(f32[512,768]{1,0:T(8,128)} %get-tuple-element.21, bf16[1,1,1,32,16,768]{5,4,3,2,1,0:T(8,128)(2,1)} %param.9, bf16[1,1,1,32,16,768]{5,4,3,2,1,0:T(8,128)(2,1)} %param.10), kind=kLoop, calls=%fused_computation.13 | loop fusion | flops 5111808 | bytes 6291456 | tf_op jit(solution)/shard_map/mul | solution.py:267
  139.1 5.2 %all-to-all-done.1 = f32[32,1,32]{2,1,0:T(1,128)S(1)} async-done(((f32[32,1,32]{2,1,0:T(1,128)}), f32[32,1,32]{2,1,0:T(1,128)S(1)}, u32[]{:S(2)}, u32[]{:S(2)}) %all-to-all-start.1) | async-done | bytes 4128 | tf_op jit(solution)/shard_map/all_to_all | solution.py:265
  144.3 0.0 copy-done
  144.3 0.0 copy-done.1
  144.3 1.6 %finish.1 = (bf16[512,768]{1,0:T(8,128)(2,1)}, bf16[512,768]{1,0:T(8,128)(2,1)}, f32[8,128]{1,0:T(8,128)}) custom-call(s32[8,128]{1,0:T(8,128)S(1)} %bitcast.22, f32[32,128]{1,0:T(8,128)S(1)} %copy-done, f32[32,32]{1,0:T(8,128)S(1)} %bitcast.20, f32[512,768]{1,0:T(8,128)S(1)} %get-tuple-element.26.gate_ref, f32[512,768]{1,0:T(8,128)S(1)} %get-tuple-element.25.up_ref), custom_call_target="tpu_custom_call" | custom-call | tf_op jit(solution)/shard_map/finish/pallas_call | solution.py:204
  (2 shorter events, 0.1 us)
Async XLA Ops:
  5.7 13.2 %copy-start.11 = (bf16[1,768,256]{2,1,0:T(8,128)(2,1)S(1)}, bf16[1,768,256]{2,1,0:T(8,128)(2,1)}, u32[]{:S(2)}) copy-start(bf16[1,768,256]{2,1,0:T(8,128)(2,1)} %param.11) | copy-start | bytes 1179652
  5.8 112.6 %all-to-all-start = ((bf16[32,16,4096]{2,1,0:T(8,128)(2,1)}), bf16[32,16,4096]{2,1,0:T(8,128)(2,1)}, u32[]{:S(2)}, u32[]{:S(2)}) async-start(bf16[32,16,4096]{2,1,0:T(8,128)(2,1)} %bitcast.23), calls=%async_computation | async-start | bytes 8388608 | tf_op jit(solution)/shard_map/all_to_all | solution.py:247
  19.0 66.4 %copy-start.2 = (bf16[1,1,1,32,16,768]{5,4,3,2,1,0:T(8,128)(2,1)S(1)}, bf16[1,1,1,32,16,768]{5,4,3,2,1,0:T(8,128)(2,1)}, u32[]{:S(2)}) copy-start(bf16[1,1,1,32,16,768]{5,4,3,2,1,0:T(8,128)(2,1)} %param.10) | copy-start | bytes 2359300
  19.0 66.4 %copy-start.3 = (bf16[1,1,1,32,16,768]{5,4,3,2,1,0:T(8,128)(2,1)S(1)}, bf16[1,1,1,32,16,768]{5,4,3,2,1,0:T(8,128)(2,1)}, u32[]{:S(2)}) copy-start(bf16[1,1,1,32,16,768]{5,4,3,2,1,0:T(8,128)(2,1)} %param.9) | copy-start | bytes 2359300
  19.0 13.5 %collective-permute-start = (bf16[1,768,256]{2,1,0:T(8,128)(2,1)S(1)}, bf16[1,768,256]{2,1,0:T(8,128)(2,1)S(1)}, u32[]{:S(2)}, u32[]{:S(2)}) collective-permute-start(bf16[1,768,256]{2,1,0:T(8,128)(2,1)S(1)} %copy-done.11), channel_id=1, source_target_pairs={{128,0},{132,4},{392,8},{396,12},{144,16},{148,20},{408,24},{412,2... | collective-permute-start | bytes 1179656 | tf_op jit(solution)/shard_map/ppermute | solution.py:223
  32.5 14.0 %collective-permute-start.1 = (bf16[1,768,256]{2,1,0:T(8,128)(2,1)S(1)}, bf16[1,768,256]{2,1,0:T(8,128)(2,1)S(1)}, u32[]{:S(2)}, u32[]{:S(2)}) collective-permute-start(bf16[1,768,256]{2,1,0:T(8,128)(2,1)S(1)} %collective-permute-done), channel_id=1, source_target_pairs={{128,0},{132,4},{392,8},{396,12},{144,16},{148,20},{408,24},{412,2... | collective-permute-start | bytes 1179656 | tf_op jit(solution)/shard_map/ppermute | solution.py:223
  38.7 48.2 %copy-start.5 = (bf16[2,768,256]{2,1,0:T(8,128)(2,1)}, bf16[2,768,256]{2,1,0:T(8,128)(2,1)S(1)}, u32[]{:S(2)}) copy-start(bf16[2,768,256]{2,1,0:T(8,128)(2,1)S(1)} %constant_dynamic-update-slice_fusion.refs_1_) | copy-start | bytes 2359300
  38.7 20.3 %collective-permute-start.3 = (bf16[2,768,256]{2,1,0:T(8,128)(2,1)S(1)}, bf16[2,768,256]{2,1,0:T(8,128)(2,1)S(1)}, u32[]{:S(2)}, u32[]{:S(2)}) collective-permute-start(bf16[2,768,256]{2,1,0:T(8,128)(2,1)S(1)} %constant_dynamic-update-slice_fusion.refs_1_), channel_id=1, source_target_pairs={{1,0},{2,1},{3,2},{0,3},{5,4},{6,5},{7,6},{4,7},{9,8},{10,9},{11,1... | collective-permute-start | bytes 2359304 | tf_op jit(solution)/shard_map/ppermute | solution.py:213
  43.1 20.6 %collective-permute-start.4 = (bf16[2,768,256]{2,1,0:T(8,128)(2,1)S(1)}, bf16[2,768,256]{2,1,0:T(8,128)(2,1)S(1)}, u32[]{:S(2)}, u32[]{:S(2)}) collective-permute-start(bf16[2,768,256]{2,1,0:T(8,128)(2,1)S(1)} %constant_dynamic-update-slice_fusion.refs_1_), channel_id=1, source_target_pairs={{3,0},{0,1},{1,2},{2,3},{7,4},{4,5},{5,6},{6,7},{11,8},{8,9},{9,10... | collective-permute-start | bytes 2359304 | tf_op jit(solution)/shard_map/ppermute | solution.py:213
  46.4 12.5 %collective-permute-start.2 = (bf16[1,768,256]{2,1,0:T(8,128)(2,1)S(1)}, bf16[1,768,256]{2,1,0:T(8,128)(2,1)S(1)}, u32[]{:S(2)}, u32[]{:S(2)}) collective-permute-start(bf16[1,768,256]{2,1,0:T(8,128)(2,1)S(1)} %collective-permute-done.1), channel_id=1, source_target_pairs={{128,0},{132,4},{392,8},{396,12},{144,16},{148,20},{408,24},{412,2... | collective-permute-start | bytes 1179656 | tf_op jit(solution)/shard_map/ppermute | solution.py:223
  59.0 59.3 %copy-start.4 = (bf16[2,768,256]{2,1,0:T(8,128)(2,1)}, bf16[2,768,256]{2,1,0:T(8,128)(2,1)S(1)}, u32[]{:S(2)}) copy-start(bf16[2,768,256]{2,1,0:T(8,128)(2,1)S(1)} %pad_maximum_fusion.refs_2_) | copy-start | bytes 2359300
  59.1 59.3 %copy-start.6 = (bf16[2,768,256]{2,1,0:T(8,128)(2,1)}, bf16[2,768,256]{2,1,0:T(8,128)(2,1)S(1)}, u32[]{:S(2)}) copy-start(bf16[2,768,256]{2,1,0:T(8,128)(2,1)S(1)} %collective-permute-done.3.refs_3_) | copy-start | bytes 2359300
  63.7 54.6 %copy-start.7 = (bf16[2,768,256]{2,1,0:T(8,128)(2,1)}, bf16[2,768,256]{2,1,0:T(8,128)(2,1)S(1)}, u32[]{:S(2)}) copy-start(bf16[2,768,256]{2,1,0:T(8,128)(2,1)S(1)} %collective-permute-done.4.refs_7_) | copy-start | bytes 2359300
  63.7 19.8 %collective-permute-start.7 = (bf16[2,768,256]{2,1,0:T(8,128)(2,1)S(1)}, bf16[2,768,256]{2,1,0:T(8,128)(2,1)S(1)}, u32[]{:S(2)}, u32[]{:S(2)}) collective-permute-start(bf16[2,768,256]{2,1,0:T(8,128)(2,1)S(1)} %pad_maximum_fusion.refs_2_), channel_id=1, source_target_pairs={{3,0},{0,1},{1,2},{2,3},{7,4},{4,5},{5,6},{6,7},{11,8},{8,9},{9,10... | collective-permute-start | bytes 2359304 | tf_op jit(solution)/shard_map/ppermute | solution.py:213
  65.6 21.3 %collective-permute-start.5 = (bf16[2,768,256]{2,1,0:T(8,128)(2,1)S(1)}, bf16[2,768,256]{2,1,0:T(8,128)(2,1)S(1)}, u32[]{:S(2)}, u32[]{:S(2)}) collective-permute-start(bf16[2,768,256]{2,1,0:T(8,128)(2,1)S(1)} %pad_maximum_fusion.refs_2_), channel_id=1, source_target_pairs={{1,0},{2,1},{3,2},{0,3},{5,4},{6,5},{7,6},{4,7},{9,8},{10,9},{11,1... | collective-permute-start | bytes 2359304 | tf_op jit(solution)/shard_map/ppermute | solution.py:213
  70.2 30.9 %collective-permute-start.6 = (bf16[2,768,256]{2,1,0:T(8,128)(2,1)S(1)}, bf16[2,768,256]{2,1,0:T(8,128)(2,1)S(1)}, u32[]{:S(2)}, u32[]{:S(2)}) collective-permute-start(bf16[2,768,256]{2,1,0:T(8,128)(2,1)S(1)} %collective-permute-done.3.refs_3_), channel_id=1, source_target_pairs={{1,0},{2,1},{3,2},{0,3},{5,4},{6,5},{7,6},{4,7},{9,8},{10,9},{11,1... | collective-permute-start | bytes 2359304 | tf_op jit(solution)/shard_map/ppermute | solution.py:213
  83.5 34.9 %copy-start.8 = (bf16[2,768,256]{2,1,0:T(8,128)(2,1)}, bf16[2,768,256]{2,1,0:T(8,128)(2,1)S(1)}, u32[]{:S(2)}) copy-start(bf16[2,768,256]{2,1,0:T(8,128)(2,1)S(1)} %collective-permute-done.7.refs_8_) | copy-start | bytes 2359300
  83.5 18.9 %collective-permute-start.8 = (bf16[2,768,256]{2,1,0:T(8,128)(2,1)S(1)}, bf16[2,768,256]{2,1,0:T(8,128)(2,1)}, u32[]{:S(2)}, u32[]{:S(2)}) collective-permute-start(bf16[2,768,256]{2,1,0:T(8,128)(2,1)S(1)} %collective-permute-done.7.refs_8_), channel_id=1, source_target_pairs={{3,0},{0,1},{1,2},{2,3},{7,4},{4,5},{5,6},{6,7},{11,8},{8,9},{9,10... | collective-permute-start | bytes 2359304 | tf_op jit(solution)/shard_map/ppermute | solution.py:213
  86.9 14.2 %copy-start.9 = (bf16[2,768,256]{2,1,0:T(8,128)(2,1)}, bf16[2,768,256]{2,1,0:T(8,128)(2,1)S(1)}, u32[]{:S(2)}) copy-start(bf16[2,768,256]{2,1,0:T(8,128)(2,1)S(1)} %collective-permute-done.5.refs_4_) | copy-start | bytes 2359300
  101.1 0.9 copy-start.10
  126.9 17.4 %all-to-all-start.1 = ((f32[32,1,32]{2,1,0:T(1,128)}), f32[32,1,32]{2,1,0:T(1,128)S(1)}, u32[]{:S(2)}, u32[]{:S(2)}) async-start(f32[32,1,32]{2,1,0:T(1,128)} %bitcast.24), calls=%async_computation.1 | async-start | bytes 32768 | tf_op jit(solution)/shard_map/all_to_all | solution.py:265
  136.5 7.8 %copy-start = (f32[32,128]{1,0:T(8,128)S(1)}, f32[32,128]{1,0:T(8,128)}, u32[]{:S(2)}) copy-start(f32[32,128]{1,0:T(8,128)} %get-tuple-element.14.slot_ref) | copy-start | bytes 49156
  136.5 7.8 %copy-start.1 = (s32[128,8]{0,1:T(8,128)S(1)}, s32[128,8]{0,1:T(8,128)}, u32[]{:S(2)}) copy-start(s32[128,8]{0,1:T(8,128)} %param.7) | copy-start | bytes 12292

commit v7 on v6

--- a/solution.py
+++ b/solution.py
@@ -49,10 +49,10 @@
             at = j * group + i * cols
             out = jnp.dot(choose, part, preferred_element_type=jnp.float32)
             sent[:, at : at + cols] = out.astype(jnp.bfloat16)
-        where = pl.ds(j * group, group)
-        store = pltpu.make_async_copy(sent.at[:, where], sent_hbm.at[:, where], sent_sem.at[j])
-        store.start()
-        stores.append(store)
+            where = pl.ds(at, cols)
+            store = pltpu.make_async_copy(sent.at[:, where], sent_hbm.at[:, where], sent_sem.at[j * n_dp + i])
+            store.start()
+            stores.append(store)
     lane = lax.broadcasted_iota(jnp.int32, (ranks, cap), 1).astype(jnp.float32)
     found = jnp.zeros((ranks, cap), jnp.float32)
     for j in range(cap):
@@ -83,7 +83,7 @@
             pltpu.VMEM((tokens, width), jnp.bfloat16),
             pltpu.VMEM((ranks * cap, width), jnp.bfloat16),
             pltpu.SemaphoreType.DMA,
-            pltpu.SemaphoreType.DMA((n_context,)),
+            pltpu.SemaphoreType.DMA((n_context * n_dp,)),
         ],
         compiler_params=pltpu.CompilerParams(vmem_limit_bytes=VMEM),
         name="head",

time: 147 us -> 147 us (level)
  no operation moved by 1% of the time
where the time goes in v7:
time: 147 us; the launch traced here: 146 us
  waiting for transfers between devices  68.2 us (46%)
  starting transfers between devices  56.5 us (38%)
  Pallas kernels  15.3 us (10%)
  other arithmetic  4.12 us (3%)
    ppermute x6, waiting for transfers between devices, fetch(): lax.ppermute(block, axis, [(partner(i), i) for i in range(lax.axis_size(a...  30.6 us
    ppermute x3, starting transfers between devices, fetch_next(): return lax.ppermute(block, ('dp', 'expert'), pairs)  17.1 us
    ppermute x6, starting transfers between devices, fetch(): lax.ppermute(block, axis, [(partner(i), i) for i in range(lax.axis_size(a...  16.6 us
    ppermute x3, waiting for transfers between devices, fetch_next(): return lax.ppermute(block, ('dp', 'expert'), pairs)  16.5 us
    all_to_all x1, waiting for transfers between devices, exchange(): lax.all_to_all(blocks, 'expert', split_axis=0, concat_axis=0, tiled=True)  15.9 us
    all_to_all x1, starting transfers between devices, exchange(): lax.all_to_all(blocks, 'expert', split_axis=0, concat_axis=0, tiled=True)  13.2 us
    all_to_all x1, starting transfers between devices, body(): lax.all_to_all(crossing, 'expert', split_axis=0, concat_axis=0, tiled=True)  9.65 us
    pallas_call x1, Pallas kernels, project(): pl.pallas_call(kernel, out_shape=(jax.ShapeDtypeStruct((slots, units), jn...  8.5 us
  transfers between devices with their start and end apart: 11, of which 9 were waited for; matrix products, arithmetic and copies ran while one was open for 3% of the time, Pallas kernels for 0%

profile of v7, /device:TPU:1, one launch (start us, length us, event | category | flops | bytes accessed | tf_op | source)
XLA Modules:
  0.0 146.0 jit_solution(14503325727060603583)
XLA Ops:
  0.6 5.2 %head.1 = (bf16[512,4096]{1,0:T(8,128)(2,1)}, f32[32,16]{1,0:T(8,128)}, f32[32,128]{1,0:T(8,128)}) custom-call(s32[8,128]{1,0:T(8,128)} %bitcast.21, bf16[8,128]{1,0:T(8,128)(2,1)} %bitcast.25, bf16[128,4096]{1,0:T(8,128)(2,1)} %refs_2_.1), custom_call_target="tpu_custom_call" | custom-call | tf_op jit(solution)/shard_map/head/pallas_call | solution.py:73
  5.8 0.0 copy-start.11
  5.8 13.2 %all-to-all-start = ((bf16[32,16,4096]{2,1,0:T(8,128)(2,1)}), bf16[32,16,4096]{2,1,0:T(8,128)(2,1)}, u32[]{:S(2)}, u32[]{:S(2)}) async-start(bf16[32,16,4096]{2,1,0:T(8,128)(2,1)} %bitcast.23), calls=%async_computation | async-start | bytes 8388608 | tf_op jit(solution)/shard_map/all_to_all | solution.py:247
  19.0 0.0 copy-done.11
  19.0 0.0 copy-start.2
  19.1 0.0 copy-start.3
  19.1 5.1 %collective-permute-start = (bf16[1,768,256]{2,1,0:T(8,128)(2,1)S(1)}, bf16[1,768,256]{2,1,0:T(8,128)(2,1)S(1)}, u32[]{:S(2)}, u32[]{:S(2)}) collective-permute-start(bf16[1,768,256]{2,1,0:T(8,128)(2,1)S(1)} %copy-done.11), channel_id=1, source_target_pairs={{128,0},{132,4},{392,8},{396,12},{144,16},{148,20},{408,24},{412,2... | collective-permute-start | bytes 1179656 | tf_op jit(solution)/shard_map/ppermute | solution.py:223
  24.2 8.3 %collective-permute-done = bf16[1,768,256]{2,1,0:T(8,128)(2,1)S(1)} collective-permute-done((bf16[1,768,256]{2,1,0:T(8,128)(2,1)S(1)}, bf16[1,768,256]{2,1,0:T(8,128)(2,1)S(1)}, u32[]{:S(2)}, u32[]{:S(2)}) %collective-permute-start) | collective-permute-done | bytes 393248 | tf_op jit(solution)/shard_map/ppermute | solution.py:223
  32.5 6.2 %collective-permute-start.1 = (bf16[1,768,256]{2,1,0:T(8,128)(2,1)S(1)}, bf16[1,768,256]{2,1,0:T(8,128)(2,1)S(1)}, u32[]{:S(2)}, u32[]{:S(2)}) collective-permute-start(bf16[1,768,256]{2,1,0:T(8,128)(2,1)S(1)} %collective-permute-done), channel_id=1, source_target_pairs={{128,0},{132,4},{392,8},{396,12},{144,16},{148,20},{408,24},{412,2... | collective-permute-start | bytes 1179656 | tf_op jit(solution)/shard_map/ppermute | solution.py:223
  38.8 0.0 copy-start.5
  38.8 4.4 %collective-permute-start.3 = (bf16[2,768,256]{2,1,0:T(8,128)(2,1)S(1)}, bf16[2,768,256]{2,1,0:T(8,128)(2,1)S(1)}, u32[]{:S(2)}, u32[]{:S(2)}) collective-permute-start(bf16[2,768,256]{2,1,0:T(8,128)(2,1)S(1)} %constant_dynamic-update-slice_fusion.refs_1_), channel_id=1, source_target_pairs={{1,0},{2,1},{3,2},{0,3},{5,4},{6,5},{7,6},{4,7},{9,8},{10,9},{11,1... | collective-permute-start | bytes 2359304 | tf_op jit(solution)/shard_map/ppermute | solution.py:213
  43.2 1.9 %collective-permute-start.4 = (bf16[2,768,256]{2,1,0:T(8,128)(2,1)S(1)}, bf16[2,768,256]{2,1,0:T(8,128)(2,1)S(1)}, u32[]{:S(2)}, u32[]{:S(2)}) collective-permute-start(bf16[2,768,256]{2,1,0:T(8,128)(2,1)S(1)} %constant_dynamic-update-slice_fusion.refs_1_), channel_id=1, source_target_pairs={{3,0},{0,1},{1,2},{2,3},{7,4},{4,5},{5,6},{6,7},{11,8},{8,9},{9,10... | collective-permute-start | bytes 2359304 | tf_op jit(solution)/shard_map/ppermute | solution.py:213
  45.1 1.4 collective-permute-done.1
  46.5 5.8 %collective-permute-start.2 = (bf16[1,768,256]{2,1,0:T(8,128)(2,1)S(1)}, bf16[1,768,256]{2,1,0:T(8,128)(2,1)S(1)}, u32[]{:S(2)}, u32[]{:S(2)}) collective-permute-start(bf16[1,768,256]{2,1,0:T(8,128)(2,1)S(1)} %collective-permute-done.1), channel_id=1, source_target_pairs={{128,0},{132,4},{392,8},{396,12},{144,16},{148,20},{408,24},{412,2... | collective-permute-start | bytes 1179656 | tf_op jit(solution)/shard_map/ppermute | solution.py:223
  52.3 6.8 %collective-permute-done.2 = bf16[1,768,256]{2,1,0:T(8,128)(2,1)S(1)} collective-permute-done((bf16[1,768,256]{2,1,0:T(8,128)(2,1)S(1)}, bf16[1,768,256]{2,1,0:T(8,128)(2,1)S(1)}, u32[]{:S(2)}, u32[]{:S(2)}) %collective-permute-start.2) | collective-permute-done | bytes 393248 | tf_op jit(solution)/shard_map/ppermute | solution.py:223
  59.0 0.1 pad_maximum_fusion.refs_2_
  59.1 0.0 copy-start.4
  59.1 0.0 collective-permute-done.3.refs_3_
  59.1 0.0 copy-start.6
  59.2 4.6 %collective-permute-done.4.refs_7_ = bf16[2,768,256]{2,1,0:T(8,128)(2,1)S(1)} collective-permute-done((bf16[2,768,256]{2,1,0:T(8,128)(2,1)S(1)}, bf16[2,768,256]{2,1,0:T(8,128)(2,1)S(1)}, u32[]{:S(2)}, u32[]{:S(2)}) %collective-permute-start.4) | collective-permute-done | bytes 786464 | tf_op jit(solution)/shard_map/ppermute | solution.py:213
  63.8 0.0 copy-start.7
  63.8 1.9 %collective-permute-start.7 = (bf16[2,768,256]{2,1,0:T(8,128)(2,1)S(1)}, bf16[2,768,256]{2,1,0:T(8,128)(2,1)S(1)}, u32[]{:S(2)}, u32[]{:S(2)}) collective-permute-start(bf16[2,768,256]{2,1,0:T(8,128)(2,1)S(1)} %pad_maximum_fusion.refs_2_), channel_id=1, source_target_pairs={{3,0},{0,1},{1,2},{2,3},{7,4},{4,5},{5,6},{6,7},{11,8},{8,9},{9,10... | collective-permute-start | bytes 2359304 | tf_op jit(solution)/shard_map/ppermute | solution.py:213
  65.7 4.6 %collective-permute-start.5 = (bf16[2,768,256]{2,1,0:T(8,128)(2,1)S(1)}, bf16[2,768,256]{2,1,0:T(8,128)(2,1)S(1)}, u32[]{:S(2)}, u32[]{:S(2)}) collective-permute-start(bf16[2,768,256]{2,1,0:T(8,128)(2,1)S(1)} %pad_maximum_fusion.refs_2_), channel_id=1, source_target_pairs={{1,0},{2,1},{3,2},{0,3},{5,4},{6,5},{7,6},{4,7},{9,8},{10,9},{11,1... | collective-permute-start | bytes 2359304 | tf_op jit(solution)/shard_map/ppermute | solution.py:213
  70.3 1.9 %collective-permute-start.6 = (bf16[2,768,256]{2,1,0:T(8,128)(2,1)S(1)}, bf16[2,768,256]{2,1,0:T(8,128)(2,1)S(1)}, u32[]{:S(2)}, u32[]{:S(2)}) collective-permute-start(bf16[2,768,256]{2,1,0:T(8,128)(2,1)S(1)} %collective-permute-done.3.refs_3_), channel_id=1, source_target_pairs={{1,0},{2,1},{3,2},{0,3},{5,4},{6,5},{7,6},{4,7},{9,8},{10,9},{11,1... | collective-permute-start | bytes 2359304 | tf_op jit(solution)/shard_map/ppermute | solution.py:213
  72.2 11.3 %collective-permute-done.7.refs_8_ = bf16[2,768,256]{2,1,0:T(8,128)(2,1)S(1)} collective-permute-done((bf16[2,768,256]{2,1,0:T(8,128)(2,1)S(1)}, bf16[2,768,256]{2,1,0:T(8,128)(2,1)S(1)}, u32[]{:S(2)}, u32[]{:S(2)}) %collective-permute-start.7) | collective-permute-done | bytes 786464 | tf_op jit(solution)/shard_map/ppermute | solution.py:213
  83.6 0.0 copy-start.8
  83.6 1.9 %collective-permute-start.8 = (bf16[2,768,256]{2,1,0:T(8,128)(2,1)S(1)}, bf16[2,768,256]{2,1,0:T(8,128)(2,1)}, u32[]{:S(2)}, u32[]{:S(2)}) collective-permute-start(bf16[2,768,256]{2,1,0:T(8,128)(2,1)S(1)} %collective-permute-done.7.refs_8_), channel_id=1, source_target_pairs={{3,0},{0,1},{1,2},{2,3},{7,4},{4,5},{5,6},{6,7},{11,8},{8,9},{9,10... | collective-permute-start | bytes 2359304 | tf_op jit(solution)/shard_map/ppermute | solution.py:213
  85.5 0.0 copy-done.2
  85.5 0.0 copy-done.3
  85.5 1.5 %fusion.refs_9_ = bf16[512,768]{1,0:T(8,128)(2,1)} fusion(bf16[1,1,1,32,16,768]{5,4,3,2,1,0:T(8,128)(2,1)S(1)} %copy-done.2, bf16[1,1,1,32,16,768]{5,4,3,2,1,0:T(8,128)(2,1)S(1)} %copy-done.3), kind=kLoop, calls=%fused_computation.6 | loop fusion | flops 3145728 | bytes 2359296 | tf_op jit(solution)/shard_map/convert_element_type | solution.py:263
  87.0 0.0 copy-done.5
  87.0 0.0 collective-permute-done.5.refs_4_
  87.0 0.0 copy-start.9
  87.0 14.2 %collective-permute-done.6.refs_5_ = bf16[2,768,256]{2,1,0:T(8,128)(2,1)S(1)} collective-permute-done((bf16[2,768,256]{2,1,0:T(8,128)(2,1)S(1)}, bf16[2,768,256]{2,1,0:T(8,128)(2,1)S(1)}, u32[]{:S(2)}, u32[]{:S(2)}) %collective-permute-start.6) | collective-permute-done | bytes 786464 | tf_op jit(solution)/shard_map/ppermute | solution.py:213
  101.2 0.0 copy-done.9
  101.2 0.0 copy-start.10
  101.2 0.9 copy-done.10
  102.1 0.4 collective-permute-done.8.refs_6_
  102.5 15.9 %all-to-all-done = bf16[32,16,4096]{2,1,0:T(8,128)(2,1)} async-done(((bf16[32,16,4096]{2,1,0:T(8,128)(2,1)}), bf16[32,16,4096]{2,1,0:T(8,128)(2,1)}, u32[]{:S(2)}, u32[]{:S(2)}) %all-to-all-start) | async-done | bytes 4194336 | tf_op jit(solution)/shard_map/all_to_all | solution.py:247
  118.4 0.0 copy-done.4
  118.4 0.0 copy-done.6
  118.4 0.0 copy-done.7
  118.4 0.0 copy-done.8
  118.4 8.5 %project.1 = (f32[512,768]{1,0:T(8,128)}, f32[32,32]{1,0:T(8,128)}) custom-call(bf16[512,4096]{1,0:T(8,128)(2,1)} %bitcast.3.refs_0_, bf16[2,768,256]{2,1,0:T(8,128)(2,1)} %copy-done.5, bf16[2,768,256]{2,1,0:T(8,128)(2,1)} %copy-done.4, bf16[2,768,256]{2,1,0:T(8,128)(2,1)} %copy-done.6, bf16[2,768,256]{2,1,0:T(8,128)(2,1)} %copy-done.9, ...), custom_call_target="tpu_custom_call" | custom-call | tf_op jit(solution)/shard_map/project/pallas_call | solution.py:154
  126.9 9.7 %all-to-all-start.1 = ((f32[32,1,32]{2,1,0:T(1,128)}), f32[32,1,32]{2,1,0:T(1,128)S(1)}, u32[]{:S(2)}, u32[]{:S(2)}) async-start(f32[32,1,32]{2,1,0:T(1,128)} %bitcast.24), calls=%async_computation.1 | async-start | bytes 32768 | tf_op jit(solution)/shard_map/all_to_all | solution.py:265
  136.6 0.0 copy-start
  136.6 0.0 copy-start.1
  136.6 2.6 %fusion.7 = (f32[512,768]{1,0:T(8,128)S(1)}, f32[512,768]{1,0:T(8,128)S(1)}) fusion(f32[512,768]{1,0:T(8,128)} %get-tuple-element.21, bf16[1,1,1,32,16,768]{5,4,3,2,1,0:T(8,128)(2,1)} %param.9, bf16[1,1,1,32,16,768]{5,4,3,2,1,0:T(8,128)(2,1)} %param.10), kind=kLoop, calls=%fused_computation.13 | loop fusion | flops 5111808 | bytes 6291456 | tf_op jit(solution)/shard_map/mul | solution.py:267
  139.2 5.2 %all-to-all-done.1 = f32[32,1,32]{2,1,0:T(1,128)S(1)} async-done(((f32[32,1,32]{2,1,0:T(1,128)}), f32[32,1,32]{2,1,0:T(1,128)S(1)}, u32[]{:S(2)}, u32[]{:S(2)}) %all-to-all-start.1) | async-done | bytes 4128 | tf_op jit(solution)/shard_map/all_to_all | solution.py:265
  144.4 0.0 copy-done
  144.4 0.0 copy-done.1
  144.4 1.6 %finish.1 = (bf16[512,768]{1,0:T(8,128)(2,1)}, bf16[512,768]{1,0:T(8,128)(2,1)}, f32[8,128]{1,0:T(8,128)}) custom-call(s32[8,128]{1,0:T(8,128)S(1)} %bitcast.22, f32[32,128]{1,0:T(8,128)S(1)} %copy-done, f32[32,32]{1,0:T(8,128)S(1)} %bitcast.20, f32[512,768]{1,0:T(8,128)S(1)} %get-tuple-element.26.gate_ref, f32[512,768]{1,0:T(8,128)S(1)} %get-tuple-element.25.up_ref), custom_call_target="tpu_custom_call" | custom-call | tf_op jit(solution)/shard_map/finish/pallas_call | solution.py:204
  (2 shorter events, 0.1 us)
Async XLA Ops:
  5.8 13.2 %copy-start.11 = (bf16[1,768,256]{2,1,0:T(8,128)(2,1)S(1)}, bf16[1,768,256]{2,1,0:T(8,128)(2,1)}, u32[]{:S(2)}) copy-start(bf16[1,768,256]{2,1,0:T(8,128)(2,1)} %param.11) | copy-start | bytes 1179652
  5.8 112.6 %all-to-all-start = ((bf16[32,16,4096]{2,1,0:T(8,128)(2,1)}), bf16[32,16,4096]{2,1,0:T(8,128)(2,1)}, u32[]{:S(2)}, u32[]{:S(2)}) async-start(bf16[32,16,4096]{2,1,0:T(8,128)(2,1)} %bitcast.23), calls=%async_computation | async-start | bytes 8388608 | tf_op jit(solution)/shard_map/all_to_all | solution.py:247
  19.0 66.4 %copy-start.2 = (bf16[1,1,1,32,16,768]{5,4,3,2,1,0:T(8,128)(2,1)S(1)}, bf16[1,1,1,32,16,768]{5,4,3,2,1,0:T(8,128)(2,1)}, u32[]{:S(2)}) copy-start(bf16[1,1,1,32,16,768]{5,4,3,2,1,0:T(8,128)(2,1)} %param.10) | copy-start | bytes 2359300
  19.1 66.4 %copy-start.3 = (bf16[1,1,1,32,16,768]{5,4,3,2,1,0:T(8,128)(2,1)S(1)}, bf16[1,1,1,32,16,768]{5,4,3,2,1,0:T(8,128)(2,1)}, u32[]{:S(2)}) copy-start(bf16[1,1,1,32,16,768]{5,4,3,2,1,0:T(8,128)(2,1)} %param.9) | copy-start | bytes 2359300
  19.1 13.5 %collective-permute-start = (bf16[1,768,256]{2,1,0:T(8,128)(2,1)S(1)}, bf16[1,768,256]{2,1,0:T(8,128)(2,1)S(1)}, u32[]{:S(2)}, u32[]{:S(2)}) collective-permute-start(bf16[1,768,256]{2,1,0:T(8,128)(2,1)S(1)} %copy-done.11), channel_id=1, source_target_pairs={{128,0},{132,4},{392,8},{396,12},{144,16},{148,20},{408,24},{412,2... | collective-permute-start | bytes 1179656 | tf_op jit(solution)/shard_map/ppermute | solution.py:223
  32.5 14.0 %collective-permute-start.1 = (bf16[1,768,256]{2,1,0:T(8,128)(2,1)S(1)}, bf16[1,768,256]{2,1,0:T(8,128)(2,1)S(1)}, u32[]{:S(2)}, u32[]{:S(2)}) collective-permute-start(bf16[1,768,256]{2,1,0:T(8,128)(2,1)S(1)} %collective-permute-done), channel_id=1, source_target_pairs={{128,0},{132,4},{392,8},{396,12},{144,16},{148,20},{408,24},{412,2... | collective-permute-start | bytes 1179656 | tf_op jit(solution)/shard_map/ppermute | solution.py:223
  38.8 48.2 %copy-start.5 = (bf16[2,768,256]{2,1,0:T(8,128)(2,1)}, bf16[2,768,256]{2,1,0:T(8,128)(2,1)S(1)}, u32[]{:S(2)}) copy-start(bf16[2,768,256]{2,1,0:T(8,128)(2,1)S(1)} %constant_dynamic-update-slice_fusion.refs_1_) | copy-start | bytes 2359300
  38.8 20.3 %collective-permute-start.3 = (bf16[2,768,256]{2,1,0:T(8,128)(2,1)S(1)}, bf16[2,768,256]{2,1,0:T(8,128)(2,1)S(1)}, u32[]{:S(2)}, u32[]{:S(2)}) collective-permute-start(bf16[2,768,256]{2,1,0:T(8,128)(2,1)S(1)} %constant_dynamic-update-slice_fusion.refs_1_), channel_id=1, source_target_pairs={{1,0},{2,1},{3,2},{0,3},{5,4},{6,5},{7,6},{4,7},{9,8},{10,9},{11,1... | collective-permute-start | bytes 2359304 | tf_op jit(solution)/shard_map/ppermute | solution.py:213
  43.2 20.6 %collective-permute-start.4 = (bf16[2,768,256]{2,1,0:T(8,128)(2,1)S(1)}, bf16[2,768,256]{2,1,0:T(8,128)(2,1)S(1)}, u32[]{:S(2)}, u32[]{:S(2)}) collective-permute-start(bf16[2,768,256]{2,1,0:T(8,128)(2,1)S(1)} %constant_dynamic-update-slice_fusion.refs_1_), channel_id=1, source_target_pairs={{3,0},{0,1},{1,2},{2,3},{7,4},{4,5},{5,6},{6,7},{11,8},{8,9},{9,10... | collective-permute-start | bytes 2359304 | tf_op jit(solution)/shard_map/ppermute | solution.py:213
  46.5 12.5 %collective-permute-start.2 = (bf16[1,768,256]{2,1,0:T(8,128)(2,1)S(1)}, bf16[1,768,256]{2,1,0:T(8,128)(2,1)S(1)}, u32[]{:S(2)}, u32[]{:S(2)}) collective-permute-start(bf16[1,768,256]{2,1,0:T(8,128)(2,1)S(1)} %collective-permute-done.1), channel_id=1, source_target_pairs={{128,0},{132,4},{392,8},{396,12},{144,16},{148,20},{408,24},{412,2... | collective-permute-start | bytes 1179656 | tf_op jit(solution)/shard_map/ppermute | solution.py:223
  59.1 59.3 %copy-start.4 = (bf16[2,768,256]{2,1,0:T(8,128)(2,1)}, bf16[2,768,256]{2,1,0:T(8,128)(2,1)S(1)}, u32[]{:S(2)}) copy-start(bf16[2,768,256]{2,1,0:T(8,128)(2,1)S(1)} %pad_maximum_fusion.refs_2_) | copy-start | bytes 2359300
  59.1 59.3 %copy-start.6 = (bf16[2,768,256]{2,1,0:T(8,128)(2,1)}, bf16[2,768,256]{2,1,0:T(8,128)(2,1)S(1)}, u32[]{:S(2)}) copy-start(bf16[2,768,256]{2,1,0:T(8,128)(2,1)S(1)} %collective-permute-done.3.refs_3_) | copy-start | bytes 2359300
  63.8 54.6 %copy-start.7 = (bf16[2,768,256]{2,1,0:T(8,128)(2,1)}, bf16[2,768,256]{2,1,0:T(8,128)(2,1)S(1)}, u32[]{:S(2)}) copy-start(bf16[2,768,256]{2,1,0:T(8,128)(2,1)S(1)} %collective-permute-done.4.refs_7_) | copy-start | bytes 2359300
  63.8 19.8 %collective-permute-start.7 = (bf16[2,768,256]{2,1,0:T(8,128)(2,1)S(1)}, bf16[2,768,256]{2,1,0:T(8,128)(2,1)S(1)}, u32[]{:S(2)}, u32[]{:S(2)}) collective-permute-start(bf16[2,768,256]{2,1,0:T(8,128)(2,1)S(1)} %pad_maximum_fusion.refs_2_), channel_id=1, source_target_pairs={{3,0},{0,1},{1,2},{2,3},{7,4},{4,5},{5,6},{6,7},{11,8},{8,9},{9,10... | collective-permute-start | bytes 2359304 | tf_op jit(solution)/shard_map/ppermute | solution.py:213
  65.7 21.3 %collective-permute-start.5 = (bf16[2,768,256]{2,1,0:T(8,128)(2,1)S(1)}, bf16[2,768,256]{2,1,0:T(8,128)(2,1)S(1)}, u32[]{:S(2)}, u32[]{:S(2)}) collective-permute-start(bf16[2,768,256]{2,1,0:T(8,128)(2,1)S(1)} %pad_maximum_fusion.refs_2_), channel_id=1, source_target_pairs={{1,0},{2,1},{3,2},{0,3},{5,4},{6,5},{7,6},{4,7},{9,8},{10,9},{11,1... | collective-permute-start | bytes 2359304 | tf_op jit(solution)/shard_map/ppermute | solution.py:213
  70.3 30.9 %collective-permute-start.6 = (bf16[2,768,256]{2,1,0:T(8,128)(2,1)S(1)}, bf16[2,768,256]{2,1,0:T(8,128)(2,1)S(1)}, u32[]{:S(2)}, u32[]{:S(2)}) collective-permute-start(bf16[2,768,256]{2,1,0:T(8,128)(2,1)S(1)} %collective-permute-done.3.refs_3_), channel_id=1, source_target_pairs={{1,0},{2,1},{3,2},{0,3},{5,4},{6,5},{7,6},{4,7},{9,8},{10,9},{11,1... | collective-permute-start | bytes 2359304 | tf_op jit(solution)/shard_map/ppermute | solution.py:213
  83.6 34.9 %copy-start.8 = (bf16[2,768,256]{2,1,0:T(8,128)(2,1)}, bf16[2,768,256]{2,1,0:T(8,128)(2,1)S(1)}, u32[]{:S(2)}) copy-start(bf16[2,768,256]{2,1,0:T(8,128)(2,1)S(1)} %collective-permute-done.7.refs_8_) | copy-start | bytes 2359300
  83.6 18.9 %collective-permute-start.8 = (bf16[2,768,256]{2,1,0:T(8,128)(2,1)S(1)}, bf16[2,768,256]{2,1,0:T(8,128)(2,1)}, u32[]{:S(2)}, u32[]{:S(2)}) collective-permute-start(bf16[2,768,256]{2,1,0:T(8,128)(2,1)S(1)} %collective-permute-done.7.refs_8_), channel_id=1, source_target_pairs={{3,0},{0,1},{1,2},{2,3},{7,4},{4,5},{5,6},{6,7},{11,8},{8,9},{9,10... | collective-permute-start | bytes 2359304 | tf_op jit(solution)/shard_map/ppermute | solution.py:213
  87.0 14.2 %copy-start.9 = (bf16[2,768,256]{2,1,0:T(8,128)(2,1)}, bf16[2,768,256]{2,1,0:T(8,128)(2,1)S(1)}, u32[]{:S(2)}) copy-start(bf16[2,768,256]{2,1,0:T(8,128)(2,1)S(1)} %collective-permute-done.5.refs_4_) | copy-start | bytes 2359300
  101.2 0.9 copy-start.10
  126.9 17.5 %all-to-all-start.1 = ((f32[32,1,32]{2,1,0:T(1,128)}), f32[32,1,32]{2,1,0:T(1,128)S(1)}, u32[]{:S(2)}, u32[]{:S(2)}) async-start(f32[32,1,32]{2,1,0:T(1,128)} %bitcast.24), calls=%async_computation.1 | async-start | bytes 32768 | tf_op jit(solution)/shard_map/all_to_all | solution.py:265
  136.6 7.8 %copy-start = (f32[32,128]{1,0:T(8,128)S(1)}, f32[32,128]{1,0:T(8,128)}, u32[]{:S(2)}) copy-start(f32[32,128]{1,0:T(8,128)} %get-tuple-element.14.slot_ref) | copy-start | bytes 49156
  136.6 7.8 %copy-start.1 = (s32[128,8]{0,1:T(8,128)S(1)}, s32[128,8]{0,1:T(8,128)}, u32[]{:S(2)}) copy-start(s32[128,8]{0,1:T(8,128)} %param.7) | copy-start | bytes 12292
